TPU v7x, 256 devices: a whole 4x4x8 slice. The times are simulated.
256 devices in a mesh: dp: 16 (over x, z_hi, core), seq: 16 (over y, z_lo).
Axes of the slice: x: 4, y: 4, z: 8 (z_hi: 2, z_lo: 4; z = z_hi * 4 + z_lo), core: 2. Of those that a mesh axis runs over, the one named last changes fastest.
Arguments:
- tokens: bfloat16 [16, 2048, 1536], P('dp', 'seq'), may hold values from -6 to 6
- w_proj: bfloat16 [1536, 2304], replicated, may hold values from -1 to 1
- d_attended: bfloat16 [16, 2048, 768], P('dp', 'seq'), may hold values from -6 to 6
Outputs:
- attended: bfloat16 [16, 2048, 768], P('dp', 'seq')
- d_tokens: bfloat16 [16, 2048, 1536], P('dp', 'seq')
- grad_proj: float32 [1536, 2304], P('seq', 'dp')
All inputs are finite; a program needn't handle non-finite values.
Results may differ from a plain program's by a relative error of at most 0.03.
Values may be sent and summed in bfloat16 or wider, within the bound.
No kernel may reach another device: no remote copies, remote signals or barrier semaphores. Data moves between devices by JAX's collectives and lax.ppermute only.
A program may use at most 128 MiB of HBM per device.

v0:
```python
import math

import jax
import jax.numpy as jnp
from jax import lax
from jax.sharding import PartitionSpec as P

HS = 192
HEADS = 4
HD = 768


EPS = 1e-06


def split_heads(rows):
    return rows.reshape(rows.shape[0], HEADS, -1).transpose(1, 0, 2)


def join_heads(stacked):
    return stacked.transpose(1, 0, 2).reshape(stacked.shape[1], -1)


def per_device(tokens, w_proj, d_attended):
    score_scale = 1.0 / math.sqrt(HS)
    own_rows = tokens.shape[1]
    inputs = tokens[0].astype(jnp.float32)
    inverse = lax.rsqrt(jnp.mean(inputs * inputs, -1, keepdims=True) + EPS)
    normed = (inputs * inverse).astype(jnp.bfloat16)
    projected = jnp.dot(normed, w_proj, preferred_element_type=jnp.float32).astype(jnp.bfloat16)
    own_keys = projected[:, HD : 2 * HD]
    own_values = projected[:, 2 * HD :]
    all_keys, all_values = (
        lax.all_gather(own_keys, "seq", axis=0, tiled=True),
        lax.all_gather(own_values, "seq", axis=0, tiled=True),
    )
    queries = split_heads(projected[:, :HD])
    key_heads = split_heads(all_keys)
    value_heads = split_heads(all_values)
    scores = (
        jnp.einsum("hqd,hkd->hqk", queries, key_heads, preferred_element_type=jnp.float32)
        * score_scale
    )
    softmaxed = jax.nn.softmax(scores, axis=-1)
    weights = softmaxed.astype(jnp.bfloat16)
    attended = join_heads(
        jnp.einsum("hqk,hkd->hqd", weights, value_heads, preferred_element_type=jnp.float32)
    ).astype(jnp.bfloat16)
    grads_out = split_heads(d_attended[0])
    d_probs = jnp.einsum("hqd,hkd->hqk", grads_out, value_heads, preferred_element_type=jnp.float32)
    row_total = jnp.sum(softmaxed * d_probs, -1, keepdims=True)
    d_scores = (softmaxed * (d_probs - row_total) * score_scale).astype(jnp.bfloat16)
    d_queries = jnp.einsum("hqk,hkd->hqd", d_scores, key_heads, preferred_element_type=jnp.float32)
    key_part = jnp.einsum(
        "hqk,hqd->khd", d_scores, queries, preferred_element_type=jnp.float32
    ).reshape(own_rows * lax.axis_size("seq"), -1)
    value_part = jnp.einsum(
        "hqk,hqd->khd", weights, grads_out, preferred_element_type=jnp.float32
    ).reshape(own_rows * lax.axis_size("seq"), -1)
    key_grads = lax.psum_scatter(
        jnp.concatenate([key_part, value_part], 1).astype(jnp.bfloat16),
        "seq",
        scatter_dimension=0,
        tiled=True,
    ).astype(jnp.float32)
    d_proj = jnp.concatenate([join_heads(d_queries), key_grads], 1).astype(jnp.bfloat16)
    d_normed = jnp.einsum("rc,dc->rd", d_proj, w_proj, preferred_element_type=jnp.float32)
    unrounded = inputs * inverse
    d_tokens = (
        inverse * (d_normed - unrounded * jnp.mean(d_normed * unrounded, -1, keepdims=True))
    ).astype(jnp.bfloat16)
    partial_value = lax.psum_scatter(
        jnp.einsum("tr,tc->rc", normed, d_proj, preferred_element_type=jnp.float32).astype(
            jnp.bfloat16
        ),
        "seq",
        scatter_dimension=0,
        tiled=True,
    )
    gradient = lax.psum_scatter(partial_value, "dp", scatter_dimension=1, tiled=True).astype(
        jnp.float32
    )
    return (attended[None], d_tokens[None], gradient)


def solution(mesh):
    placed = (P("dp", "seq", None), P(), P("dp", "seq", None))
    return jax.shard_map(
        per_device,
        mesh=mesh,
        in_specs=placed,
        out_specs=(P("dp", "seq", None), P("dp", "seq", None), P("seq", "dp")),
        check_vma=False,
    )
```

profile of v0, /device:TPU:32, one launch (start us, length us, event | category | flops | bytes accessed | tf_op | source)
XLA Modules:
  0.0 632.9 jit_solution(12931700409445309754)
XLA Ops:
  7.2 0.0 all-gather.5.cloned.1.call-start
  7.2 1.2 fusion.19
  8.4 0.0 copy-start.1
  8.4 4.3 convolution_convert_fusion.1
  12.7 0.8 fusion.33
  13.5 0.0 all-gather.5.cloned.1.call-update
  13.5 0.0 all-gather.3.cloned.1.call-start
  13.6 0.7 all-gather.3.cloned.1.call-update
  14.3 0.0 reduce-scatter.10.cloned.1.call-start
  14.3 0.0 copy-done.1
  14.4 0.2 copy.23
  14.5 0.2 copy.20
  14.7 92.1 %all-gather.5.cloned.1.call-done = bf16[2048,768]{1,0:T(8,128)(2,1)} async-done(((bf16[128,768]{1,0:T(8,128)(2,1)}), bf16[2048,768]{1,0:T(8,128)(2,1)}) %all-gather.5.cloned.1.call-update) | async-done | bytes 3145744 | tf_op jit(solution)/shard_map/all_gather | solution.py:35
  106.7 3.2 copy.22
  109.9 2.7 fusion.35
  112.6 86.4 %all-gather.3.cloned.1.call-done = bf16[2048,768]{1,0:T(8,128)(2,1)} async-done(((bf16[128,768]{1,0:T(8,128)(2,1)}), bf16[2048,768]{1,0:T(8,128)(2,1)}) %all-gather.3.cloned.1.call-update) | async-done | bytes 3145744 | tf_op jit(solution)/shard_map/all_gather | solution.py:34
  199.0 4.7 copy.21
  203.6 5.4 fusion.34
  209.1 4.9 convolution_convert_fusion.2
  214.0 9.5 %convolution_convert_fusion.3 = bf16[4,192,2048]{2,1,0:T(8,128)(2,1)} fusion(bf16[4,128,192]{1,2,0:T(8,128)(2,1)S(1)} %bitcast.83, f32[4,2048,128]{1,2,0:T(8,128)} %fusion.35, f32[4,128,2048]{2,1,0:T(8,128)} %get-tuple-element.16, f32[4,128]{1,0:T(4,128)S(1)} %get-tuple-element.15), kind=kOutput, calls=%fused_computation.14 | convolution fusion | flops 411568640 | bytes 11732992 | tf_op jit(solution)/shard_map/hqk,hqd->khd/dot_general | solution.py:54
  223.5 6.6 %pad_maximum_fusion = bf16[2048,1536]{0,1:T(8,128)(2,1)} fusion(bf16[2048,768]{0,1:T(8,128)(2,1)} %bitcast.75, bf16[2048,768]{0,1:T(8,128)(2,1)} %bitcast.76), kind=kLoop, calls=%fused_computation.3 | loop fusion | flops 12582912 | bytes 12582912 | tf_op jit(solution)/shard_map/concatenate | solution.py:61
  230.1 8.7 %copy.28 = bf16[2048,1536]{1,0:T(8,128)(2,1)} copy(bf16[2048,1536]{0,1:T(8,128)(2,1)} %pad_maximum_fusion) | data formatting | bytes 12582912
  238.8 0.0 reduce-scatter.10.cloned.1.call-update
  238.8 0.0 copy-start
  238.8 0.2 reduce-scatter.8.cloned.1.call-start
  239.1 9.4 %fusion.9 = bf16[4,128,192]{1,2,0:T(8,128)(2,1)} fusion(bf16[4,2048,192]{1,2,0:T(8,128)(2,1)} %bitcast.74, f32[4,2048,128]{1,2,0:T(8,128)} %fusion.35, f32[4,128,2048]{2,1,0:T(8,128)} %get-tuple-element.16, f32[4,128]{1,0:T(4,128)S(1)} %get-tuple-element.15), kind=kOutput, calls=%fused_computation.19 | convolution fusion | flops 410094080 | bytes 11732992 | tf_op jit(solution)/shard_map/hqk,hkd->hqd/dot_general | solution.py:53
  248.5 129.6 %reduce-scatter.10.cloned.1.call-done = bf16[128,1536]{1,0:T(8,128)(2,1)} async-done(((bf16[2048,1536]{1,0:T(8,128)(2,1)}), bf16[128,1536]{1,0:T(8,128)(2,1)}) %reduce-scatter.10.cloned.1.call-update) | async-done | bytes 393232
  378.1 1.9 copy.29
  380.0 0.0 copy-done
  380.0 6.1 convolution_convert_fusion
  386.1 0.0 reduce-scatter.8.cloned.1.call-update
  386.1 0.0 reduce-scatter.12.cloned.1.call-start
  386.2 3.9 convolution_convert_fusion.4
  390.1 1.7 copy.25
  391.8 5.7 fusion.15
  397.6 146.7 %reduce-scatter.8.cloned.1.call-done = bf16[96,2304]{1,0:T(8,128)(2,1)} async-done(((bf16[1536,2304]{1,0:T(8,128)(2,1)}), bf16[96,2304]{1,0:T(8,128)(2,1)}) %reduce-scatter.8.cloned.1.call-update) | async-done | bytes 442384 | tf_op jit(solution)/shard_map/reduce_scatter | solution.py:72
  544.3 2.1 copy.30
  546.4 0.0 reduce-scatter.12.cloned.1.call-update
  546.4 1.0 fusion.20
  547.5 77.4 %reduce-scatter.12.cloned.1.call-done = bf16[144,96]{1,0:T(8,128)(2,1)} async-done(((bf16[2304,96]{1,0:T(8,128)(2,1)}), bf16[144,96]{1,0:T(8,128)(2,1)}) %reduce-scatter.12.cloned.1.call-update) | async-done | bytes 27664
  624.8 0.9 copy.31
  625.7 0.7 copy.26
  (2 shorter events, 0.0 us)
Async XLA Ops:
  7.2 99.6 %all-gather.5.cloned.1.call-start = ((), (), s32[]{:S(2)}) async-start(), calls=%async_computation.4 | async-start | bytes 3342336 | tf_op jit(solution)/shard_map/all_gather | solution.py:35
  8.4 6.0 copy-start.1
  13.5 185.4 %all-gather.3.cloned.1.call-start = ((), (), s32[]{:S(2)}) async-start(), calls=%async_computation.3 | async-start | bytes 3342336 | tf_op jit(solution)/shard_map/all_gather | solution.py:34
  14.3 363.8 %reduce-scatter.10.cloned.1.call-start = ((), (), s32[]{:S(2)}) async-start(), calls=%async_computation.6 | async-start | bytes 6684672
  238.8 141.2 %copy-start = (bf16[1,128,1536]{2,1,0:T(8,128)(2,1)S(1)}, bf16[1,128,1536]{2,1,0:T(8,128)(2,1)}, u32[]{:S(2)}) copy-start(bf16[1,128,1536]{2,1,0:T(8,128)(2,1)} %param.3) | copy-start | bytes 1179652
  238.8 305.5 %reduce-scatter.8.cloned.1.call-start = ((), (), s32[]{:S(2)}) async-start(), calls=%async_computation.5 | async-start | bytes 7520256 | tf_op jit(solution)/shard_map/reduce_scatter | solution.py:72
  386.1 238.7 %reduce-scatter.12.cloned.1.call-start = ((), (), s32[]{:S(2)}) async-start(), calls=%async_computation.7 | async-start | bytes 626688
Sparse Core Ops, SparseCore 0:
  13.7 93.0 all-gather.4
  109.1 89.8 all-gather.2
  238.9 139.0 reduce-scatter.9
  386.2 158.0 reduce-scatter.7
  548.8 76.0 reduce-scatter.11
where the time goes:
time: 635 us; the launch traced here: 633 us
  waiting for transfers between devices  533 us (84%)
  matrix products  52 us (8%)
  local copies, waits for them, and re-layouts  24.9 us (4%)
  between operations  13.8 us (2%)
  other arithmetic  8.83 us (1%)
    unnamed x7, waiting for transfers between devices  208 us
    reduce_scatter x1, waiting for transfers between devices, per_device(): lax.psum_scatter(jnp.einsum('tr,tc->rc', normed, d_proj, preferred_elemen...  147 us
    all_gather x1, waiting for transfers between devices, per_device(): lax.all_gather(own_values, 'seq', axis=0, tiled=True)  92.1 us
    all_gather x1, waiting for transfers between devices, per_device(): lax.all_gather(own_keys, 'seq', axis=0, tiled=True)  86.4 us
    unnamed x11, local copies, waits for them, and re-layouts  16.1 us
  transfers between devices with their start and end apart: 5, of which 5 were waited for; matrix products, arithmetic and copies ran while one was open for 4% of the time, Pallas kernels for 0%

commit v1 on v0

v1 whole, which is shorter than its diff:
```python
import math

import jax
import jax.numpy as jnp
from jax import lax
from jax.experimental import pallas as pl
from jax.experimental.pallas import tpu as pltpu
from jax.sharding import Mesh
from jax.sharding import PartitionSpec as P

HS = 192
HEADS = 4
HD = 768
D = 1536
ROWS = 128
EPS = 1e-06
SCALE = 1.0 / math.sqrt(HS)
SCALE2 = SCALE * math.log2(math.e)
BF = jnp.bfloat16
F32 = jnp.float32
NN = (((1,), (0,)), ((), ()))
NT = (((1,), (1,)), ((), ()))

SMEM = pl.BlockSpec(memory_space=pltpu.SMEM)


def shape(dims, dtype=BF):
    return jax.ShapeDtypeStruct(dims, dtype)


def params():
    return pltpu.CompilerParams(vmem_limit_bytes=48 * 2**20)


def dot(a, b, dims=NN):
    return lax.dot_general(a, b, dims, preferred_element_type=F32)


def flip(block):
    return jnp.transpose(block.astype(F32))


def normalise(tokens):
    rows = tokens.astype(F32)
    inverse = lax.rsqrt(jnp.mean(rows * rows, -1, keepdims=True) + EPS)
    return rows * inverse, inverse


def project_kernel(place, tokens, weights, grads, normed, *rest):
    kv, qd, cut = rest[:4], rest[4:8], rest[8]
    step = pl.program_id(0)

    @pl.when(step == 0)
    def _():
        normed[...] = normalise(tokens[...])[0].astype(BF)
        turned = flip(grads[...]).astype(BF)
        for head in range(HEADS):
            cut[head, 3 * HS :, :] = turned[head * HS : (head + 1) * HS]

    turned = flip(dot(normed[...], weights[...])).astype(BF)
    at = pl.ds(pl.multiple_of(step * HS, HS), HS)
    for head in range(HEADS):
        cut[head, at, :] = turned[head * HS : (head + 1) * HS]

    @pl.when(step == 2)
    def _():
        for k in range(4):
            head = lax.rem(place[0] + k, 4)
            kv[k][...] = cut[head, : 2 * HS, :]
            qd[k][...] = cut[head, 2 * HS :, :]


def project(place, tokens, weights, grads):
    whole = lambda dims: pl.BlockSpec(dims, lambda i: (0, 0))
    half = (2 * HS, ROWS)
    return pl.pallas_call(
        project_kernel,
        grid=(3,),
        in_specs=[
            SMEM,
            whole((ROWS, D)),
            pl.BlockSpec((D, HD), lambda i: (0, lax.rem(i + 1, 3))),
            whole((ROWS, HD)),
        ],
        out_specs=[whole((ROWS, D))] + [whole(half)] * 8,
        out_shape=[shape((ROWS, D))] + [shape(half)] * 8,
        scratch_shapes=[pltpu.VMEM((HEADS, 4 * HS, ROWS), BF)],
        compiler_params=params(),
        name="project",
    )(place, tokens, weights, grads)


def side_by_side(blocks, wide):
    for k, block in enumerate(blocks):
        wide[:, k * ROWS : (k + 1) * ROWS] = block[...]


TILE = 256


def stats_kernel(*refs):
    kv_blocks, qd_blocks, stats, kv, qd = refs[:8], refs[8:16], refs[16], refs[17], refs[18]
    side_by_side(kv_blocks, kv)
    side_by_side(qd_blocks, qd)
    keys = flip(kv[:HS, :]).astype(BF)
    values = flip(kv[HS:, :]).astype(BF)
    for tile in range(8 * ROWS // TILE):
        at = slice(tile * TILE, (tile + 1) * TILE)
        scores = dot(keys, qd[:HS, at]) * SCALE2
        top = jnp.max(scores, 0, keepdims=True)
        powers = jnp.exp2(scores - top)
        d_probs = dot(values, qd[HS:, at])
        stats[0:1, at] = top
        stats[1:2, at] = jnp.sum(powers, 0, keepdims=True)
        stats[2:3, at] = jnp.sum(powers * d_probs, 0, keepdims=True)
        stats[3:8, at] = jnp.zeros((5, TILE), F32)


def stats_of(kv_blocks, qd_blocks):
    wide = pltpu.VMEM((2 * HS, 8 * ROWS), BF)
    return pl.pallas_call(
        stats_kernel,
        out_shape=shape((8, 8 * ROWS), F32),
        scratch_shapes=[wide, wide],
        compiler_params=params(),
        name="stats",
    )(*kv_blocks, *qd_blocks)


def attend_kernel(*refs):
    kv_blocks, qd_blocks, mine, theirs = refs[:8], refs[8:16], refs[16], refs[17]
    qo_own, qo_send, kv_own, kv_send, kv, qd, kv_sum = refs[18:]
    side_by_side(kv_blocks, kv)
    side_by_side(qd_blocks, qd)
    keys = flip(kv[:HS, :]).astype(BF)
    values = flip(kv[HS:, :]).astype(BF)
    half = 4 * ROWS
    for tile in range(8 * ROWS // TILE):
        at = slice(tile * TILE, (tile + 1) * TILE)
        start = (tile * TILE + half) % (2 * half)
        across = slice(start, start + TILE)
        top_a, sum_a, total_a = mine[0:1, at], mine[1:2, at], mine[2:3, at]
        top_b, sum_b, total_b = theirs[0:1, across], theirs[1:2, across], theirs[2:3, across]
        top = jnp.maximum(top_a, top_b)
        by_a, by_b = jnp.exp2(top_a - top), jnp.exp2(top_b - top)
        share = 1.0 / (sum_a * by_a + sum_b * by_b)
        row_total = (total_a * by_a + total_b * by_b) * share
        scores = dot(keys, qd[:HS, at]) * SCALE2
        softmaxed = jnp.exp2(scores - top) * share
        d_probs = dot(values, qd[HS:, at])
        d_scores = (softmaxed * (d_probs - row_total) * SCALE).astype(BF)
        weights = softmaxed.astype(BF)
        d_queries = dot(kv[:HS, :], d_scores)
        attended = dot(kv[HS:, :], weights)
        if tile * TILE < half:
            qo_own[:HS, at] = d_queries
            qo_own[HS:, at] = attended
        else:
            qo_send[:HS, across] = d_queries.astype(BF)
            qo_send[HS:, across] = attended.astype(BF)
        d_keys = dot(qd[:HS, at], d_scores, NT)
        d_values = dot(qd[HS:, at], weights, NT)
        if tile == 0:
            kv_sum[:HS, :] = d_keys
            kv_sum[HS:, :] = d_values
        else:
            kv_sum[:HS, :] += d_keys
            kv_sum[HS:, :] += d_values
    kv_own[...] = kv_sum[:, :half]
    kv_send[...] = kv_sum[:, half:].astype(BF)


def attend(kv_blocks, qd_blocks, mine, theirs):
    wide = (2 * HS, 8 * ROWS)
    out = (2 * HS, 4 * ROWS)
    return pl.pallas_call(
        attend_kernel,
        out_shape=[shape(out, F32), shape(out), shape(out, F32), shape(out)],
        scratch_shapes=[pltpu.VMEM(wide, BF), pltpu.VMEM(wide, BF), pltpu.VMEM(wide, F32)],
        compiler_params=params(),
        name="attend",
    )(*kv_blocks, *qd_blocks, mine, theirs)


def gradient_kernel(place, qo_own, qo_got, kv_own, kv_got, *refs):
    normed_blocks, back, keep, send, normed, d_proj, cut = (
        refs[:4], refs[4:8], refs[8], refs[9], refs[10], refs[11], refs[12],
    )
    for k, block in enumerate(normed_blocks):
        normed[k * ROWS : (k + 1) * ROWS, :] = block[...]
    q_sum = qo_own[...] + qo_got[...].astype(F32)
    kv_sum = kv_own[...] + kv_got[...].astype(F32)
    d_proj[:HS, :] = q_sum[:HS].astype(BF)
    d_proj[HS : 3 * HS, :] = kv_sum.astype(BF)
    attended = q_sum[HS:].astype(BF)
    for k in range(4):
        at = slice(k * ROWS, (k + 1) * ROWS)
        back[k][: 3 * HS, :] = d_proj[:, at]
        back[k][3 * HS :, :] = attended[:, at]
    for j in range(3):
        term = dot(d_proj[j * HS : (j + 1) * HS, :], normed[...]).astype(BF)
        for i in range(4):
            cut[i % 2, 2 * j + i // 2] = term[i * 48 : (i + 1) * 48]
    keep[...] = cut[place[2]]
    send[...] = cut[1 - place[2]]


def gradient(place, qo_own, qo_got, kv_own, kv_got, normed_blocks):
    units = (6, 48, D)
    vmem = pl.BlockSpec(memory_space=pltpu.VMEM)
    return pl.pallas_call(
        gradient_kernel,
        in_specs=[SMEM] + [vmem] * 8,
        out_shape=[shape((4 * HS, ROWS))] * 4 + [shape(units)] * 2,
        scratch_shapes=[
            pltpu.VMEM((4 * ROWS, D), BF),
            pltpu.VMEM((3 * HS, 4 * ROWS), BF),
            pltpu.VMEM((2,) + units, BF),
        ],
        compiler_params=params(),
        name="gradient",
    )(place, qo_own, qo_got, kv_own, kv_got, *normed_blocks)


def tokens_kernel(place, tokens, weights, *refs):
    blocks, attended, d_tokens, columns, d_proj, d_normed = (
        refs[:4], refs[4], refs[5], refs[6], refs[7], refs[8],
    )
    step = pl.program_id(0)

    @pl.when(step == 0)
    def _():
        for k in range(4):
            head = lax.rem(place[0] + k, 4)
            for j in range(4):
                at = pl.ds(pl.multiple_of(j * HD + head * HS, HS), HS)
                columns[at, :] = blocks[k][j * HS : (j + 1) * HS, :]
        d_proj[...] = flip(columns[: 3 * HD, :]).astype(BF)
        attended[...] = flip(columns[3 * HD :, :]).astype(BF)

    d_normed[step] = dot(d_proj[...], weights[...], NT)

    @pl.when(step == pl.num_programs(0) - 1)
    def _():
        unrounded, inverse = normalise(tokens[...])
        parts = range(d_normed.shape[0])
        wide = d_normed.shape[2]
        total = sum(
            jnp.sum(d_normed[i] * unrounded[:, i * wide : (i + 1) * wide], -1, keepdims=True)
            for i in parts
        )
        mean = total * (1.0 / D)
        for i in parts:
            at = slice(i * wide, (i + 1) * wide)
            d_tokens[:, at] = (inverse * (d_normed[i] - unrounded[:, at] * mean)).astype(BF)


def tokens_of(place, tokens, weights, blocks):
    whole = lambda dims: pl.BlockSpec(dims, lambda i: (0, 0))
    tile = 256
    return pl.pallas_call(
        tokens_kernel,
        grid=(D // tile,),
        in_specs=[SMEM, whole((ROWS, D)), pl.BlockSpec((tile, 3 * HD), lambda i: (i, 0))]
        + [whole((4 * HS, ROWS))] * 4,
        out_specs=[whole((ROWS, HD)), whole((ROWS, D))],
        out_shape=[shape((ROWS, HD)), shape((ROWS, D))],
        scratch_shapes=[
            pltpu.VMEM((4 * HD, ROWS), BF),
            pltpu.VMEM((ROWS, 3 * HD), BF),
            pltpu.VMEM((D // tile, ROWS, tile), F32),
        ],
        compiler_params=params(),
        name="d_tokens",
    )(place, tokens, weights, *blocks)


def small(kernel, name, place, blocks, outs, scratch):
    vmem = pl.BlockSpec(memory_space=pltpu.VMEM)
    return pl.pallas_call(
        kernel,
        in_specs=[SMEM] + [vmem] * len(blocks),
        out_shape=outs,
        scratch_shapes=scratch,
        compiler_params=params(),
        name=name,
    )(place, *blocks)


def split_y_kernel(place, mine, got, *refs):
    outs, cut = refs[:4], refs[4]
    cut[...] = (mine[...].astype(F32) + got[...].astype(F32)).astype(BF)
    for k in range(4):
        at = pl.ds(pl.multiple_of(lax.rem(place[1] + k, 4) * 384, 384), 384)
        outs[k][...] = cut[:, :, at]


def split_z_kernel(place, *refs):
    blocks, outs, cut = refs[:4], refs[4:8], refs[8]
    total = sum(block[...].astype(F32) for block in blocks)
    for k in range(4):
        cut[k] = total[:, :, k * 96 : (k + 1) * 96].astype(BF)
    for k in range(4):
        outs[k][...] = cut[lax.rem(place[0] + k, 4)]


def split_x_kernel(place, *refs):
    blocks, outs, cut = refs[:4], refs[4:8], refs[8]
    for k in range(4):
        head = lax.rem(place[0] + 4 - k, 4)
        for j in range(3):
            cut[pl.ds((j * 4 + head) * 2, 2)] = blocks[k][2 * j : 2 * j + 2]
    for k in range(4):
        outs[k][...] = cut[pl.ds(lax.rem(place[3] + k, 4) * 6, 6)]


def split_zh_kernel(place, *refs):
    blocks, keep, send, cut = refs[:4], refs[4], refs[5], refs[6]
    cut[...] = sum(block[...].astype(F32) for block in blocks)
    keep[...] = cut[pl.ds(place[4] * 3, 3)]
    send[...] = cut[pl.ds(3 - place[4] * 3, 3)].astype(BF)


def split_c_kernel(place, mine, got, keep, send):
    keep[...] = mine[...] + got[...].astype(F32)
    send[...] = keep[2 - 2 * place[2]].astype(BF)


def finish_kernel(place, mine, got, out):
    core = place[2]
    rows = jnp.concatenate([mine[core], got[...].astype(F32), mine[1 + core]], 0)
    out[...] = jnp.transpose(rows)


def shift(size, by):
    return [(i, (i + by) % size) for i in range(size)]


def per_device(tokens, w_proj, d_attended):
    tokens = tokens[0]
    place = jnp.stack([lax.axis_index(a) for a in ("zl", "y", "c", "x", "zh")]).astype(jnp.int32)
    near = [(0, 1), (1, 0), (2, 3), (3, 2)]
    far = [(0, 3), (3, 0), (1, 2), (2, 1)]
    swap = [(0, 1), (1, 0)]

    def spread(blocks, axis, way=1):
        return [blocks[0]] + [lax.ppermute(blocks[k], axis, shift(4, way * k)) for k in (1, 2, 3)]

    normed, *cuts = project(place, tokens, w_proj, d_attended[0])
    kv = spread(cuts[:4], "zl")
    qd = spread(cuts[4:], "zl")
    kv_far = [lax.ppermute(b, "y", far) for b in kv]
    qd_near = [lax.ppermute(b, "y", near) for b in qd]
    held = lax.optimization_barrier((normed, *kv, *qd))[0]
    normed_all = [normed] + [lax.ppermute(held, "zl", shift(4, k)) for k in (1, 2, 3)]

    kv, qd = kv + kv_far, qd + qd_near
    mine = stats_of(kv, qd)
    theirs = lax.ppermute(mine, "y", near)
    qo_own, qo_send, kv_own, kv_send = attend(kv, qd, mine, theirs)
    qo_got = lax.ppermute(qo_send, "y", near)
    kv_got = lax.ppermute(kv_send, "y", far)

    *back, keep, send = gradient(place, qo_own, qo_got, kv_own, kv_got, normed_all)
    got = lax.ppermute(send, "c", swap)
    blocks = small(
        split_y_kernel, "split_y", place, [keep, got],
        [shape((6, 48, 384))] * 4, [pltpu.VMEM((6, 48, D), BF)],
    )
    blocks = spread(blocks, "y")
    blocks = small(
        split_z_kernel, "split_z", place, blocks,
        [shape((6, 48, 96))] * 4, [pltpu.VMEM((4, 6, 48, 96), BF)],
    )
    blocks = spread(blocks, "zl")
    blocks = small(
        split_x_kernel, "split_x", place, blocks,
        [shape((6, 48, 96))] * 4, [pltpu.VMEM((24, 48, 96), BF)],
    )
    blocks = spread(blocks, "x")
    keep, send = small(
        split_zh_kernel, "split_zh", place, blocks,
        [shape((3, 48, 96), F32), shape((3, 48, 96))], [pltpu.VMEM((6, 48, 96), F32)],
    )
    got = lax.ppermute(send, "zh", swap)
    keep, send = small(
        split_c_kernel, "split_c", place, [keep, got],
        [shape((3, 48, 96), F32), shape((48, 96))], [],
    )
    got = lax.ppermute(send, "c", swap)
    grad = small(finish_kernel, "finish", place, [keep, got], shape((96, 144), F32), [])

    returned = spread(back, "zl", -1)
    attended, d_tokens = tokens_of(place, tokens, w_proj, returned)
    return (attended[None], d_tokens[None], grad)


def solution(mesh):
    fine = Mesh(mesh.devices.reshape(4, 2, 2, 4, 4), ("x", "zh", "c", "y", "zl"))
    dp, seq = ("x", "zh", "c"), ("y", "zl")
    return jax.shard_map(
        per_device,
        mesh=fine,
        in_specs=(P(dp, seq, None), P(), P(dp, seq, None)),
        out_specs=(P(dp, seq, None), P(dp, seq, None), P(seq, dp)),
        check_vma=False,
    )
```

time: 635 us -> 147 us (0.23)
  waiting for transfers between devices: 533 us -> 54.9 us
  starting transfers between devices: 0.38 us -> 60.4 us
  matrix products: 52 us -> 0 us
  Pallas kernels: 0 us -> 25.6 us
  local copies, waits for them, and re-layouts: 24.9 us -> 2.75 us
  between operations: 13.8 us -> 0.78 us
  other arithmetic: 8.83 us -> 0 us
    unnamed x7 -> x0, waiting for transfers between devices: 208 us -> none
    all_gather x2 -> x0, waiting for transfers between devices: 178 us -> none  [the longest x1 92.1 us: per_device(): lax.all_gather(own_values, 'seq', axis=0, tiled=True)]
    reduce_scatter x1 -> x0, waiting for transfers between devices: 147 us -> none  [per_device(): lax.psum_scatter(jnp.einsum('tr,tc->rc', normed, d_proj, preferred_elemen...]
    ppermute x0 -> x35, starting transfers between devices: none -> 60.4 us  [the longest x18 33.1 us: spread(): lax.ppermute(blocks[k], axis, shift(4, way * k))]
    ppermute x0 -> x35, waiting for transfers between devices: none -> 54.9 us  [the longest x18 22.9 us: spread(): lax.ppermute(blocks[k], axis, shift(4, way * k))]
    dot_general x8 -> x0, matrix products: 46.6 us -> none  [the longest x1 9.5 us: per_device(): jnp.einsum('hqk,hqd->khd', d_scores, queries, preferred_element_type=jnp....]
    pallas_call x0 -> x11, Pallas kernels: none -> 25.6 us  [the longest x1 7.82 us: tokens_of(): pl.pallas_call(tokens_kernel, grid=(D // tile,), in_specs=[SMEM, whole((R...]
    unnamed x11 -> x7, local copies, waits for them, and re-layouts: 16.1 us -> 2.67 us
  transfers between devices with their start and end apart: 5 -> 35, of which waited for: 5 -> 18; matrix products, arithmetic and copies ran while one was open for 4% -> 0% of each run, Pallas kernels for 0% -> 9%
where the time goes in v1:
time: 147 us; the launch traced here: 144 us
  starting transfers between devices  60.4 us (41%)
  waiting for transfers between devices  54.9 us (37%)
  Pallas kernels  25.6 us (17%)
  local copies, waits for them, and re-layouts  2.75 us (2%)
    ppermute x18, starting transfers between devices, spread(): lax.ppermute(blocks[k], axis, shift(4, way * k))  33.1 us
    ppermute x18, waiting for transfers between devices, spread(): lax.ppermute(blocks[k], axis, shift(4, way * k))  22.9 us
    ppermute x3, waiting for transfers between devices, per_device(): lax.ppermute(held, 'zl', shift(4, k))  20.9 us
    ppermute x4, starting transfers between devices, per_device(): kv_far = [lax.ppermute(b, 'y', far) for b in kv]  8.54 us
    pallas_call x1, Pallas kernels, tokens_of(): pl.pallas_call(tokens_kernel, grid=(D // tile,), in_specs=[SMEM, whole((R...  7.82 us
    ppermute x1, starting transfers between devices, per_device(): got = lax.ppermute(send, 'zh', swap)  6.21 us
    pallas_call x1, Pallas kernels, project(): pl.pallas_call(project_kernel, grid=(3,), in_specs=[SMEM, whole((ROWS, D)...  4.76 us
    pallas_call x6, Pallas kernels, small(): pl.pallas_call(kernel, in_specs=[SMEM] + [vmem] * len(blocks), out_shape=...  4.36 us
  transfers between devices with their start and end apart: 35, of which 18 were waited for; matrix products, arithmetic and copies ran while one was open for 0% of the time, Pallas kernels for 9%

profile of v1, /device:TPU:32, one launch (start us, length us, event | category | flops | bytes accessed | tf_op | source)
XLA Modules:
  0.0 144.5 jit_solution(102698082052304333)
XLA Ops:
  0.7 1.0 copy-done
  1.7 0.9 copy-done.2
  2.6 4.8 %project.1 = (bf16[128,1536]{1,0:T(8,128)(2,1)S(1)}, bf16[384,128]{1,0:T(8,128)(2,1)S(1)}, bf16[384,128]{1,0:T(8,128)(2,1)S(1)}, bf16[384,128]{1,0:T(8,128)(2,1)...) custom-call(s32[5]{0:T(128)S(1)} %stack.23.place, ...), custom_call_target="tpu_custom_call" | custom-call | tf_op jit(solution)/shard_map/project/pallas_call | solution.py:76
  7.4 2.0 %collective-permute-start = (bf16[384,128]{1,0:T(8,128)(2,1)S(1)}, bf16[384,128]{1,0:T(8,128)(2,1)S(1)}, u32[]{:S(2)}, u32[]{:S(2)}) collective-permute-start(bf16[384,128]{1,0:T(8,128)(2,1)S(1)} %get-tuple-element.42), channel_id=1, source_target_pairs={{0,1},{1,2},{2,3},{3,0},{4,5},{5,6},{6,7},{7,4},{8,9},{9,10},{10,1... | collective-permute-start | bytes 294920 | tf_op jit(solution)/shard_map/ppermute | solution.py:347
  9.4 2.3 %collective-permute-start.1 = (bf16[384,128]{1,0:T(8,128)(2,1)S(1)}, bf16[384,128]{1,0:T(8,128)(2,1)S(1)}, u32[]{:S(2)}, u32[]{:S(2)}) collective-permute-start(bf16[384,128]{1,0:T(8,128)(2,1)S(1)} %get-tuple-element.43), channel_id=1, source_target_pairs={{0,2},{1,3},{2,0},{3,1},{4,6},{5,7},{6,4},{7,5},{8,10},{9,11},{10,... | collective-permute-start | bytes 294920 | tf_op jit(solution)/shard_map/ppermute | solution.py:347
  11.7 1.1 collective-permute-start.2
  12.8 0.9 collective-permute-start.7
  13.7 2.4 %collective-permute-start.8 = (bf16[384,128]{1,0:T(8,128)(2,1)S(1)}, bf16[384,128]{1,0:T(8,128)(2,1)S(1)}, u32[]{:S(2)}, u32[]{:S(2)}) collective-permute-start(bf16[384,128]{1,0:T(8,128)(2,1)S(1)} %get-tuple-element.47), channel_id=1, source_target_pairs={{0,2},{1,3},{2,0},{3,1},{4,6},{5,7},{6,4},{7,5},{8,10},{9,11},{10,... | collective-permute-start | bytes 294920 | tf_op jit(solution)/shard_map/ppermute | solution.py:347
  16.2 0.8 collective-permute-start.9
  17.0 2.9 %collective-permute-done.1.refs_2_ = bf16[384,128]{1,0:T(8,128)(2,1)S(1)} collective-permute-done((bf16[384,128]{1,0:T(8,128)(2,1)S(1)}, bf16[384,128]{1,0:T(8,128)(2,1)S(1)}, u32[]{:S(2)}, u32[]{:S(2)}) %collective-permute-start.1) | collective-permute-done | bytes 98336 | tf_op jit(solution)/shard_map/ppermute | solution.py:347
  19.9 3.0 %collective-permute-start.3 = (bf16[384,128]{1,0:T(8,128)(2,1)S(1)}, bf16[384,128]{1,0:T(8,128)(2,1)S(1)}, u32[]{:S(2)}, u32[]{:S(2)}) collective-permute-start(bf16[384,128]{1,0:T(8,128)(2,1)S(1)} %get-tuple-element.41.refs_0_), channel_id=1, source_target_pairs={{0,12},{12,0},{4,8},{8,4},{1,13},{13,1},{5,9},{9,5},{2,14},{14,2},... | collective-permute-start | bytes 294920 | tf_op jit(solution)/shard_map/ppermute | solution.py:352
  22.9 1.4 collective-permute-done.2.refs_3_
  24.2 1.6 %collective-permute-start.10 = (bf16[384,128]{1,0:T(8,128)(2,1)S(1)}, bf16[384,128]{1,0:T(8,128)(2,1)S(1)}, u32[]{:S(2)}, u32[]{:S(2)}) collective-permute-start(bf16[384,128]{1,0:T(8,128)(2,1)S(1)} %get-tuple-element.45.refs_8_), channel_id=1, source_target_pairs={{0,4},{4,0},{8,12},{12,8},{1,5},{5,1},{9,13},{13,9},{2,6},{6,2},{1... | collective-permute-start | bytes 294920 | tf_op jit(solution)/shard_map/ppermute | solution.py:353
  25.8 2.2 %collective-permute-start.4 = (bf16[384,128]{1,0:T(8,128)(2,1)S(1)}, bf16[384,128]{1,0:T(8,128)(2,1)S(1)}, u32[]{:S(2)}, u32[]{:S(2)}) collective-permute-start(bf16[384,128]{1,0:T(8,128)(2,1)S(1)} %collective-permute-done.refs_1_), channel_id=1, source_target_pairs={{0,12},{12,0},{4,8},{8,4},{1,13},{13,1},{5,9},{9,5},{2,14},{14,2},... | collective-permute-start | bytes 294920 | tf_op jit(solution)/shard_map/ppermute | solution.py:352
  28.0 1.3 collective-permute-start.5
  29.3 2.1 %collective-permute-start.6 = (bf16[384,128]{1,0:T(8,128)(2,1)S(1)}, bf16[384,128]{1,0:T(8,128)(2,1)S(1)}, u32[]{:S(2)}, u32[]{:S(2)}) collective-permute-start(bf16[384,128]{1,0:T(8,128)(2,1)S(1)} %collective-permute-done.2.refs_3_), channel_id=1, source_target_pairs={{0,12},{12,0},{4,8},{8,4},{1,13},{13,1},{5,9},{9,5},{2,14},{14,2},... | collective-permute-start | bytes 294920 | tf_op jit(solution)/shard_map/ppermute | solution.py:352
  31.4 0.1 collective-permute-start.11
  31.5 1.9 %collective-permute-start.12 = (bf16[384,128]{1,0:T(8,128)(2,1)S(1)}, bf16[384,128]{1,0:T(8,128)(2,1)S(1)}, u32[]{:S(2)}, u32[]{:S(2)}) collective-permute-start(bf16[384,128]{1,0:T(8,128)(2,1)S(1)} %collective-permute-done.8.refs_10_), channel_id=1, source_target_pairs={{0,4},{4,0},{8,12},{12,8},{1,5},{5,1},{9,13},{13,9},{2,6},{6,2},{1... | collective-permute-start | bytes 294920 | tf_op jit(solution)/shard_map/ppermute | solution.py:353
  33.4 0.1 collective-permute-start.13
  33.6 1.3 collective-permute-done.5.refs_6_
  34.8 1.1 collective-permute-done.6.refs_7_
  35.9 1.2 collective-permute-done.11.refs_13_
  37.1 1.9 %collective-permute-done.12.refs_14_ = bf16[384,128]{1,0:T(8,128)(2,1)S(1)} collective-permute-done((bf16[384,128]{1,0:T(8,128)(2,1)S(1)}, bf16[384,128]{1,0:T(8,128)(2,1)S(1)}, u32[]{:S(2)}, u32[]{:S(2)}) %collective-permute-start.12) | collective-permute-done | bytes 98336 | tf_op jit(solution)/shard_map/ppermute | solution.py:353
  39.0 1.1 collective-permute-done.13.refs_15_
  40.0 2.0 %stats.1.refs_16_ = f32[8,1024]{1,0:T(8,128)S(1)} custom-call(bf16[384,128]{1,0:T(8,128)(2,1)S(1)} %get-tuple-element.41.refs_0_, bf16[384,128]{1,0:T(8,128)(2,1)S(1)} %collective-permute-done.refs_1_, bf16[384,128]{1,0:T(8,128)(2,1)S(1)} %collective-permute-done.1.refs_2_, bf16[384,128]{1,0:T(8,128)(2,1)S(1)} %collective-permute-done.2.refs_3_, ...), custom_call_target="tpu_custom_call" | custom-call | tf_op jit(solution)/shard_map/stats/pallas_call | solution.py:121
  42.1 0.4 collective-permute-start.14
  42.5 2.5 %collective-permute-start.18 = (bf16[128,1536]{1,0:T(8,128)(2,1)S(1)}, bf16[128,1536]{1,0:T(8,128)(2,1)S(1)}, u32[]{:S(2)}, u32[]{:S(2)}) collective-permute-start(bf16[128,1536]{1,0:T(8,128)(2,1)S(1)} %get-tuple-element.54.refs_0_), channel_id=1, source_target_pairs={{0,2},{1,3},{2,0},{3,1},{4,6},{5,7},{6,4},{7,5},{8,10},{9,11},{10,... | collective-permute-start | bytes 1179656 | tf_op jit(solution)/shard_map/ppermute | solution.py:355
  45.0 1.6 %collective-permute-start.17 = (bf16[128,1536]{1,0:T(8,128)(2,1)S(1)}, bf16[128,1536]{1,0:T(8,128)(2,1)S(1)}, u32[]{:S(2)}, u32[]{:S(2)}) collective-permute-start(bf16[128,1536]{1,0:T(8,128)(2,1)S(1)} %get-tuple-element.54.refs_0_), channel_id=1, source_target_pairs={{0,1},{1,2},{2,3},{3,0},{4,5},{5,6},{6,7},{7,4},{8,9},{9,10},{10,1... | collective-permute-start | bytes 1179656 | tf_op jit(solution)/shard_map/ppermute | solution.py:355
  46.6 3.8 %attend.1 = (f32[384,512]{1,0:T(8,128)S(1)}, bf16[384,512]{1,0:T(8,128)(2,1)S(1)}, f32[384,512]{1,0:T(8,128)S(1)}, bf16[384,512]{1,0:T(8,128)(2,1)S(1)}) custom-call(bf16[384,128]{1,0:T(8,128)(2,1)S(1)} %get-tuple-element.41.refs_0_, bf16[384,128]{1,0:T(8,128)(2,1)S(1)} %collective-permute-done.refs_1_, bf16[384,128]{1,0:T(8,128)(2,1)S(1)} %collective-permute-done.1.refs_2_, ...), custom_call_target="tpu_custom_call" | custom-call | tf_op jit(solution)/shard_map/attend/pallas_call | solution.py:176
  50.4 1.4 collective-permute-start.15
  51.8 2.9 %collective-permute-start.16 = (bf16[384,512]{1,0:T(8,128)(2,1)S(1)}, bf16[384,512]{1,0:T(8,128)(2,1)S(1)}, u32[]{:S(2)}, u32[]{:S(2)}) collective-permute-start(bf16[384,512]{1,0:T(8,128)(2,1)S(1)} %get-tuple-element.52), channel_id=1, source_target_pairs={{0,12},{12,0},{4,8},{8,4},{1,13},{13,1},{5,9},{9,5},{2,14},{14,2},... | collective-permute-start | bytes 1179656 | tf_op jit(solution)/shard_map/ppermute | solution.py:362
  54.7 16.7 %collective-permute-done.19.refs_3_ = bf16[128,1536]{1,0:T(8,128)(2,1)S(1)} collective-permute-done((bf16[128,1536]{1,0:T(8,128)(2,1)S(1)}, bf16[128,1536]{1,0:T(8,128)(2,1)S(1)}, u32[]{:S(2)}, u32[]{:S(2)}) %collective-permute-start.19) | collective-permute-done | bytes 393248 | tf_op jit(solution)/shard_map/ppermute | solution.py:355
  71.4 4.2 %collective-permute-done.17.refs_1_ = bf16[128,1536]{1,0:T(8,128)(2,1)S(1)} collective-permute-done((bf16[128,1536]{1,0:T(8,128)(2,1)S(1)}, bf16[128,1536]{1,0:T(8,128)(2,1)S(1)}, u32[]{:S(2)}, u32[]{:S(2)}) %collective-permute-start.17) | collective-permute-done | bytes 393248 | tf_op jit(solution)/shard_map/ppermute | solution.py:355
  75.6 2.8 %gradient.1 = (bf16[768,128]{1,0:T(8,128)(2,1)S(1)}, bf16[768,128]{1,0:T(8,128)(2,1)S(1)}, bf16[768,128]{1,0:T(8,128)(2,1)S(1)}, bf16[768,128]{1,0:T(8,128)(2,1)...) custom-call(s32[5]{0:T(128)S(1)} %stack.23.place, f32[384,512]{1,0:T(8,128)S(1)} %get-tuple-element.49.qo_own, ...), custom_call_target="tpu_custom_call" | custom-call | tf_op jit(solution)/shard_map/gradient/pallas_call | solution.py:211
  78.4 2.6 %collective-permute-done.23.got = bf16[6,48,1536]{2,1,0:T(8,128)(2,1)S(1)} collective-permute-done((bf16[6,48,1536]{2,1,0:T(8,128)(2,1)}, bf16[6,48,1536]{2,1,0:T(8,128)(2,1)S(1)}, u32[]{:S(2)}, u32[]{:S(2)}) %collective-permute-start.23) | collective-permute-done | bytes 884768 | tf_op jit(solution)/shard_map/ppermute | solution.py:365
  81.0 1.1 split_y.1
  82.2 1.3 collective-permute-start.24
  83.4 3.5 %collective-permute-start.25 = (bf16[6,48,384]{2,1,0:T(8,128)(2,1)S(1)}, bf16[6,48,384]{2,1,0:T(8,128)(2,1)S(1)}, u32[]{:S(2)}, u32[]{:S(2)}) collective-permute-start(bf16[6,48,384]{2,1,0:T(8,128)(2,1)S(1)} %get-tuple-element.65), channel_id=1, source_target_pairs={{0,8},{4,12},{8,0},{12,4},{1,9},{5,13},{9,1},{13,5},{2,10},{6,14},... | collective-permute-start | bytes 663560 | tf_op jit(solution)/shard_map/ppermute | solution.py:347
  86.9 1.3 collective-permute-start.26
  88.1 3.0 %collective-permute-done.24.refs_1_ = bf16[6,48,384]{2,1,0:T(8,128)(2,1)S(1)} collective-permute-done((bf16[6,48,384]{2,1,0:T(8,128)(2,1)S(1)}, bf16[6,48,384]{2,1,0:T(8,128)(2,1)S(1)}, u32[]{:S(2)}, u32[]{:S(2)}) %collective-permute-start.24) | collective-permute-done | bytes 221216 | tf_op jit(solution)/shard_map/ppermute | solution.py:347
  91.1 5.9 %collective-permute-done.25.refs_2_ = bf16[6,48,384]{2,1,0:T(8,128)(2,1)S(1)} collective-permute-done((bf16[6,48,384]{2,1,0:T(8,128)(2,1)S(1)}, bf16[6,48,384]{2,1,0:T(8,128)(2,1)S(1)}, u32[]{:S(2)}, u32[]{:S(2)}) %collective-permute-start.25) | collective-permute-done | bytes 221216 | tf_op jit(solution)/shard_map/ppermute | solution.py:347
  97.1 0.8 split_z.1
  97.9 2.6 %collective-permute-start.27 = (bf16[6,48,96]{2,1,0:T(8,128)(2,1)S(1)}, bf16[6,48,96]{2,1,0:T(8,128)(2,1)S(1)}, u32[]{:S(2)}, u32[]{:S(2)}) collective-permute-start(bf16[6,48,96]{2,1,0:T(8,128)(2,1)S(1)} %get-tuple-element.68), channel_id=1, source_target_pairs={{0,1},{1,2},{2,3},{3,0},{4,5},{5,6},{6,7},{7,4},{8,9},{9,10},{10,1... | collective-permute-start | bytes 165896 | tf_op jit(solution)/shard_map/ppermute | solution.py:347
  100.4 2.7 %collective-permute-start.28 = (bf16[6,48,96]{2,1,0:T(8,128)(2,1)S(1)}, bf16[6,48,96]{2,1,0:T(8,128)(2,1)S(1)}, u32[]{:S(2)}, u32[]{:S(2)}) collective-permute-start(bf16[6,48,96]{2,1,0:T(8,128)(2,1)S(1)} %get-tuple-element.69), channel_id=1, source_target_pairs={{0,2},{1,3},{2,0},{3,1},{4,6},{5,7},{6,4},{7,5},{8,10},{9,11},{10,... | collective-permute-start | bytes 165896 | tf_op jit(solution)/shard_map/ppermute | solution.py:347
  103.1 1.7 %collective-permute-start.20 = (bf16[768,128]{1,0:T(8,128)(2,1)S(1)}, bf16[768,128]{1,0:T(8,128)(2,1)S(1)}, u32[]{:S(2)}, u32[]{:S(2)}) collective-permute-start(bf16[768,128]{1,0:T(8,128)(2,1)S(1)} %get-tuple-element.56), channel_id=1, source_target_pairs={{0,3},{1,0},{2,1},{3,2},{4,7},{5,4},{6,5},{7,6},{8,11},{9,8},{10,9... | collective-permute-start | bytes 589832 | tf_op jit(solution)/shard_map/ppermute | solution.py:347
  104.8 1.8 %collective-permute-start.21 = (bf16[768,128]{1,0:T(8,128)(2,1)S(1)}, bf16[768,128]{1,0:T(8,128)(2,1)S(1)}, u32[]{:S(2)}, u32[]{:S(2)}) collective-permute-start(bf16[768,128]{1,0:T(8,128)(2,1)S(1)} %get-tuple-element.57), channel_id=1, source_target_pairs={{0,2},{1,3},{2,0},{3,1},{4,6},{5,7},{6,4},{7,5},{8,10},{9,11},{10,... | collective-permute-start | bytes 589832 | tf_op jit(solution)/shard_map/ppermute | solution.py:347
  106.6 5.4 %collective-permute-done.27.refs_1_ = bf16[6,48,96]{2,1,0:T(8,128)(2,1)S(1)} collective-permute-done((bf16[6,48,96]{2,1,0:T(8,128)(2,1)S(1)}, bf16[6,48,96]{2,1,0:T(8,128)(2,1)S(1)}, u32[]{:S(2)}, u32[]{:S(2)}) %collective-permute-start.27) | collective-permute-done | bytes 55328 | tf_op jit(solution)/shard_map/ppermute | solution.py:347
  112.0 3.0 %collective-permute-start.22 = (bf16[768,128]{1,0:T(8,128)(2,1)S(1)}, bf16[768,128]{1,0:T(8,128)(2,1)S(1)}, u32[]{:S(2)}, u32[]{:S(2)}) collective-permute-start(bf16[768,128]{1,0:T(8,128)(2,1)S(1)} %get-tuple-element.58), channel_id=1, source_target_pairs={{0,1},{1,2},{2,3},{3,0},{4,5},{5,6},{6,7},{7,4},{8,9},{9,10},{10,1... | collective-permute-start | bytes 589832 | tf_op jit(solution)/shard_map/ppermute | solution.py:347
  115.0 0.2 collective-permute-done.28.refs_2_
  115.2 0.7 split_x.1
  115.9 1.5 %collective-permute-start.30 = (bf16[6,48,96]{2,1,0:T(8,128)(2,1)S(1)}, bf16[6,48,96]{2,1,0:T(8,128)(2,1)S(1)}, u32[]{:S(2)}, u32[]{:S(2)}) collective-permute-start(bf16[6,48,96]{2,1,0:T(8,128)(2,1)S(1)} %get-tuple-element.72), channel_id=1, source_target_pairs={{0,64},{64,128},{128,192},{192,0},{1,65},{65,129},{129,193},{193,1... | collective-permute-start | bytes 165896 | tf_op jit(solution)/shard_map/ppermute | solution.py:347
  117.4 2.8 %collective-permute-start.31 = (bf16[6,48,96]{2,1,0:T(8,128)(2,1)S(1)}, bf16[6,48,96]{2,1,0:T(8,128)(2,1)S(1)}, u32[]{:S(2)}, u32[]{:S(2)}) collective-permute-start(bf16[6,48,96]{2,1,0:T(8,128)(2,1)S(1)} %get-tuple-element.73), channel_id=1, source_target_pairs={{0,128},{64,192},{128,0},{192,64},{1,129},{65,193},{129,1},{193,65... | collective-permute-start | bytes 165896 | tf_op jit(solution)/shard_map/ppermute | solution.py:347
  120.2 1.3 collective-permute-done.30.refs_1_
  121.5 1.5 %collective-permute-start.32 = (bf16[6,48,96]{2,1,0:T(8,128)(2,1)S(1)}, bf16[6,48,96]{2,1,0:T(8,128)(2,1)S(1)}, u32[]{:S(2)}, u32[]{:S(2)}) collective-permute-start(bf16[6,48,96]{2,1,0:T(8,128)(2,1)S(1)} %get-tuple-element.74), channel_id=1, source_target_pairs={{0,192},{64,0},{128,64},{192,128},{1,193},{65,1},{129,65},{193,129... | collective-permute-start | bytes 165896 | tf_op jit(solution)/shard_map/ppermute | solution.py:347
  123.0 0.2 collective-permute-done.31.refs_2_
  123.3 2.6 %collective-permute-done.32.refs_3_ = bf16[6,48,96]{2,1,0:T(8,128)(2,1)S(1)} collective-permute-done((bf16[6,48,96]{2,1,0:T(8,128)(2,1)S(1)}, bf16[6,48,96]{2,1,0:T(8,128)(2,1)S(1)}, u32[]{:S(2)}, u32[]{:S(2)}) %collective-permute-start.32) | collective-permute-done | bytes 55328 | tf_op jit(solution)/shard_map/ppermute | solution.py:347
  125.8 0.6 split_zh.1
  126.4 6.2 %collective-permute-start.33 = (bf16[3,48,96]{2,1,0:T(8,128)(2,1)S(1)}, bf16[3,48,96]{2,1,0:T(8,128)(2,1)S(1)}, u32[]{:S(2)}, u32[]{:S(2)}) collective-permute-start(bf16[3,48,96]{2,1,0:T(8,128)(2,1)S(1)} %get-tuple-element.76), channel_id=1, source_target_pairs={{0,32},{32,0},{1,33},{33,1},{2,34},{34,2},{3,35},{35,3},{4,36},{36... | collective-permute-start | bytes 82952 | tf_op jit(solution)/shard_map/ppermute | solution.py:385
  132.7 1.9 %collective-permute-done.33.got = bf16[3,48,96]{2,1,0:T(8,128)(2,1)S(1)} collective-permute-done((bf16[3,48,96]{2,1,0:T(8,128)(2,1)S(1)}, bf16[3,48,96]{2,1,0:T(8,128)(2,1)S(1)}, u32[]{:S(2)}, u32[]{:S(2)}) %collective-permute-start.33) | collective-permute-done | bytes 27680 | tf_op jit(solution)/shard_map/ppermute | solution.py:385
  134.6 0.6 split_c.1
  135.2 0.1 collective-permute-start.34
  135.3 7.8 %d_tokens.1 = (bf16[128,768]{1,0:T(8,128)(2,1)}, bf16[128,1536]{1,0:T(8,128)(2,1)}) custom-call(s32[5]{0:T(128)S(1)} %stack.23.place, bf16[128,1536]{1,0:T(8,128)(2,1)S(1)} %bitcast.10, bf16[1536,2304]{1,0:T(8,128)(2,1)} %weights.3, bf16[768,128]{1,0:T(8,128)(2,1)S(1)} %get-tuple-element.55.refs_0_, bf16[768,128]{1,0:T(8,128)(2,1)S(1)} %collective-permute-done.20.refs_1_, ...), custom_call_target="tpu_custom_call" | custom-call | tf_op jit(solution)/shard_map/d_tokens/pallas_call | solution.py:261
  143.1 0.6 finish.1
  143.8 0.7 copy.6
  (25 shorter events, 0.1 us)
Async XLA Ops:
  0.7 1.0 copy-start
  1.7 0.9 copy-start.2
  7.4 127.9 %copy-start.1 = (bf16[1,128,1536]{2,1,0:T(8,128)(2,1)S(1)}, bf16[1,128,1536]{2,1,0:T(8,128)(2,1)}, u32[]{:S(2)}) copy-start(bf16[1,128,1536]{2,1,0:T(8,128)(2,1)} %param.3) | copy-start | bytes 1179652
  7.4 8.7 %collective-permute-start = (bf16[384,128]{1,0:T(8,128)(2,1)S(1)}, bf16[384,128]{1,0:T(8,128)(2,1)S(1)}, u32[]{:S(2)}, u32[]{:S(2)}) collective-permute-start(bf16[384,128]{1,0:T(8,128)(2,1)S(1)} %get-tuple-element.42), channel_id=1, source_target_pairs={{0,1},{1,2},{2,3},{3,0},{4,5},{5,6},{6,7},{7,4},{8,9},{9,10},{10,1... | collective-permute-start | bytes 294920 | tf_op jit(solution)/shard_map/ppermute | solution.py:347
  9.4 10.5 %collective-permute-start.1 = (bf16[384,128]{1,0:T(8,128)(2,1)S(1)}, bf16[384,128]{1,0:T(8,128)(2,1)S(1)}, u32[]{:S(2)}, u32[]{:S(2)}) collective-permute-start(bf16[384,128]{1,0:T(8,128)(2,1)S(1)} %get-tuple-element.43), channel_id=1, source_target_pairs={{0,2},{1,3},{2,0},{3,1},{4,6},{5,7},{6,4},{7,5},{8,10},{9,11},{10,... | collective-permute-start | bytes 294920 | tf_op jit(solution)/shard_map/ppermute | solution.py:347
  11.7 12.5 %collective-permute-start.2 = (bf16[384,128]{1,0:T(8,128)(2,1)S(1)}, bf16[384,128]{1,0:T(8,128)(2,1)S(1)}, u32[]{:S(2)}, u32[]{:S(2)}) collective-permute-start(bf16[384,128]{1,0:T(8,128)(2,1)S(1)} %get-tuple-element.44), channel_id=1, source_target_pairs={{0,3},{1,0},{2,1},{3,2},{4,7},{5,4},{6,5},{7,6},{8,11},{9,8},{10,9... | collective-permute-start | bytes 294920 | tf_op jit(solution)/shard_map/ppermute | solution.py:347
  12.8 13.0 %collective-permute-start.7 = (bf16[384,128]{1,0:T(8,128)(2,1)S(1)}, bf16[384,128]{1,0:T(8,128)(2,1)S(1)}, u32[]{:S(2)}, u32[]{:S(2)}) collective-permute-start(bf16[384,128]{1,0:T(8,128)(2,1)S(1)} %get-tuple-element.46), channel_id=1, source_target_pairs={{0,1},{1,2},{2,3},{3,0},{4,5},{5,6},{6,7},{7,4},{8,9},{9,10},{10,1... | collective-permute-start | bytes 294920 | tf_op jit(solution)/shard_map/ppermute | solution.py:347
  13.7 14.3 %collective-permute-start.8 = (bf16[384,128]{1,0:T(8,128)(2,1)S(1)}, bf16[384,128]{1,0:T(8,128)(2,1)S(1)}, u32[]{:S(2)}, u32[]{:S(2)}) collective-permute-start(bf16[384,128]{1,0:T(8,128)(2,1)S(1)} %get-tuple-element.47), channel_id=1, source_target_pairs={{0,2},{1,3},{2,0},{3,1},{4,6},{5,7},{6,4},{7,5},{8,10},{9,11},{10,... | collective-permute-start | bytes 294920 | tf_op jit(solution)/shard_map/ppermute | solution.py:347
  16.2 13.1 %collective-permute-start.9 = (bf16[384,128]{1,0:T(8,128)(2,1)S(1)}, bf16[384,128]{1,0:T(8,128)(2,1)S(1)}, u32[]{:S(2)}, u32[]{:S(2)}) collective-permute-start(bf16[384,128]{1,0:T(8,128)(2,1)S(1)} %get-tuple-element.48), channel_id=1, source_target_pairs={{0,3},{1,0},{2,1},{3,2},{4,7},{5,4},{6,5},{7,6},{8,11},{9,8},{10,9... | collective-permute-start | bytes 294920 | tf_op jit(solution)/shard_map/ppermute | solution.py:347
  19.9 11.5 %collective-permute-start.3 = (bf16[384,128]{1,0:T(8,128)(2,1)S(1)}, bf16[384,128]{1,0:T(8,128)(2,1)S(1)}, u32[]{:S(2)}, u32[]{:S(2)}) collective-permute-start(bf16[384,128]{1,0:T(8,128)(2,1)S(1)} %get-tuple-element.41.refs_0_), channel_id=1, source_target_pairs={{0,12},{12,0},{4,8},{8,4},{1,13},{13,1},{5,9},{9,5},{2,14},{14,2},... | collective-permute-start | bytes 294920 | tf_op jit(solution)/shard_map/ppermute | solution.py:352
  24.2 7.3 %collective-permute-start.10 = (bf16[384,128]{1,0:T(8,128)(2,1)S(1)}, bf16[384,128]{1,0:T(8,128)(2,1)S(1)}, u32[]{:S(2)}, u32[]{:S(2)}) collective-permute-start(bf16[384,128]{1,0:T(8,128)(2,1)S(1)} %get-tuple-element.45.refs_8_), channel_id=1, source_target_pairs={{0,4},{4,0},{8,12},{12,8},{1,5},{5,1},{9,13},{13,9},{2,6},{6,2},{1... | collective-permute-start | bytes 294920 | tf_op jit(solution)/shard_map/ppermute | solution.py:353
  25.8 7.6 %collective-permute-start.4 = (bf16[384,128]{1,0:T(8,128)(2,1)S(1)}, bf16[384,128]{1,0:T(8,128)(2,1)S(1)}, u32[]{:S(2)}, u32[]{:S(2)}) collective-permute-start(bf16[384,128]{1,0:T(8,128)(2,1)S(1)} %collective-permute-done.refs_1_), channel_id=1, source_target_pairs={{0,12},{12,0},{4,8},{8,4},{1,13},{13,1},{5,9},{9,5},{2,14},{14,2},... | collective-permute-start | bytes 294920 | tf_op jit(solution)/shard_map/ppermute | solution.py:352
  28.0 6.8 %collective-permute-start.5 = (bf16[384,128]{1,0:T(8,128)(2,1)S(1)}, bf16[384,128]{1,0:T(8,128)(2,1)S(1)}, u32[]{:S(2)}, u32[]{:S(2)}) collective-permute-start(bf16[384,128]{1,0:T(8,128)(2,1)S(1)} %collective-permute-done.1.refs_2_), channel_id=1, source_target_pairs={{0,12},{12,0},{4,8},{8,4},{1,13},{13,1},{5,9},{9,5},{2,14},{14,2},... | collective-permute-start | bytes 294920 | tf_op jit(solution)/shard_map/ppermute | solution.py:352
  29.3 6.5 %collective-permute-start.6 = (bf16[384,128]{1,0:T(8,128)(2,1)S(1)}, bf16[384,128]{1,0:T(8,128)(2,1)S(1)}, u32[]{:S(2)}, u32[]{:S(2)}) collective-permute-start(bf16[384,128]{1,0:T(8,128)(2,1)S(1)} %collective-permute-done.2.refs_3_), channel_id=1, source_target_pairs={{0,12},{12,0},{4,8},{8,4},{1,13},{13,1},{5,9},{9,5},{2,14},{14,2},... | collective-permute-start | bytes 294920 | tf_op jit(solution)/shard_map/ppermute | solution.py:352
  31.4 5.7 %collective-permute-start.11 = (bf16[384,128]{1,0:T(8,128)(2,1)S(1)}, bf16[384,128]{1,0:T(8,128)(2,1)S(1)}, u32[]{:S(2)}, u32[]{:S(2)}) collective-permute-start(bf16[384,128]{1,0:T(8,128)(2,1)S(1)} %collective-permute-done.7.refs_9_), channel_id=1, source_target_pairs={{0,4},{4,0},{8,12},{12,8},{1,5},{5,1},{9,13},{13,9},{2,6},{6,2},{1... | collective-permute-start | bytes 294920 | tf_op jit(solution)/shard_map/ppermute | solution.py:353
  31.5 7.5 %collective-permute-start.12 = (bf16[384,128]{1,0:T(8,128)(2,1)S(1)}, bf16[384,128]{1,0:T(8,128)(2,1)S(1)}, u32[]{:S(2)}, u32[]{:S(2)}) collective-permute-start(bf16[384,128]{1,0:T(8,128)(2,1)S(1)} %collective-permute-done.8.refs_10_), channel_id=1, source_target_pairs={{0,4},{4,0},{8,12},{12,8},{1,5},{5,1},{9,13},{13,9},{2,6},{6,2},{1... | collective-permute-start | bytes 294920 | tf_op jit(solution)/shard_map/ppermute | solution.py:353
  33.4 6.6 %collective-permute-start.13 = (bf16[384,128]{1,0:T(8,128)(2,1)S(1)}, bf16[384,128]{1,0:T(8,128)(2,1)S(1)}, u32[]{:S(2)}, u32[]{:S(2)}) collective-permute-start(bf16[384,128]{1,0:T(8,128)(2,1)S(1)} %collective-permute-done.9.refs_11_), channel_id=1, source_target_pairs={{0,4},{4,0},{8,12},{12,8},{1,5},{5,1},{9,13},{13,9},{2,6},{6,2},{1... | collective-permute-start | bytes 294920 | tf_op jit(solution)/shard_map/ppermute | solution.py:353
  42.1 4.5 %collective-permute-start.14 = (f32[8,1024]{1,0:T(8,128)S(1)}, f32[8,1024]{1,0:T(8,128)S(1)}, u32[]{:S(2)}, u32[]{:S(2)}) collective-permute-start(f32[8,1024]{1,0:T(8,128)S(1)} %stats.1.refs_16_), channel_id=1, source_target_pairs={{0,4},{4,0},{8,12},{12,8},{1,5},{5,1},{9,13},{13,9},{2,6},{6,2},{1... | collective-permute-start | bytes 98312 | tf_op jit(solution)/shard_map/ppermute | solution.py:359
  42.5 28.9 %collective-permute-start.19 = (bf16[128,1536]{1,0:T(8,128)(2,1)S(1)}, bf16[128,1536]{1,0:T(8,128)(2,1)S(1)}, u32[]{:S(2)}, u32[]{:S(2)}) collective-permute-start(bf16[128,1536]{1,0:T(8,128)(2,1)S(1)} %get-tuple-element.54.refs_0_), channel_id=1, source_target_pairs={{0,3},{1,0},{2,1},{3,2},{4,7},{5,4},{6,5},{7,6},{8,11},{9,8},{10,9... | collective-permute-start | bytes 1179656 | tf_op jit(solution)/shard_map/ppermute | solution.py:355
  42.5 28.9 %collective-permute-start.18 = (bf16[128,1536]{1,0:T(8,128)(2,1)S(1)}, bf16[128,1536]{1,0:T(8,128)(2,1)S(1)}, u32[]{:S(2)}, u32[]{:S(2)}) collective-permute-start(bf16[128,1536]{1,0:T(8,128)(2,1)S(1)} %get-tuple-element.54.refs_0_), channel_id=1, source_target_pairs={{0,2},{1,3},{2,0},{3,1},{4,6},{5,7},{6,4},{7,5},{8,10},{9,11},{10,... | collective-permute-start | bytes 1179656 | tf_op jit(solution)/shard_map/ppermute | solution.py:355
  45.0 30.6 %collective-permute-start.17 = (bf16[128,1536]{1,0:T(8,128)(2,1)S(1)}, bf16[128,1536]{1,0:T(8,128)(2,1)S(1)}, u32[]{:S(2)}, u32[]{:S(2)}) collective-permute-start(bf16[128,1536]{1,0:T(8,128)(2,1)S(1)} %get-tuple-element.54.refs_0_), channel_id=1, source_target_pairs={{0,1},{1,2},{2,3},{3,0},{4,5},{5,6},{6,7},{7,4},{8,9},{9,10},{10,1... | collective-permute-start | bytes 1179656 | tf_op jit(solution)/shard_map/ppermute | solution.py:355
  50.4 25.2 %collective-permute-start.15 = (bf16[384,512]{1,0:T(8,128)(2,1)S(1)}, bf16[384,512]{1,0:T(8,128)(2,1)S(1)}, u32[]{:S(2)}, u32[]{:S(2)}) collective-permute-start(bf16[384,512]{1,0:T(8,128)(2,1)S(1)} %get-tuple-element.50), channel_id=1, source_target_pairs={{0,4},{4,0},{8,12},{12,8},{1,5},{5,1},{9,13},{13,9},{2,6},{6,2},{1... | collective-permute-start | bytes 1179656 | tf_op jit(solution)/shard_map/ppermute | solution.py:361
  51.8 23.8 %collective-permute-start.16 = (bf16[384,512]{1,0:T(8,128)(2,1)S(1)}, bf16[384,512]{1,0:T(8,128)(2,1)S(1)}, u32[]{:S(2)}, u32[]{:S(2)}) collective-permute-start(bf16[384,512]{1,0:T(8,128)(2,1)S(1)} %get-tuple-element.52), channel_id=1, source_target_pairs={{0,12},{12,0},{4,8},{8,4},{1,13},{13,1},{5,9},{9,5},{2,14},{14,2},... | collective-permute-start | bytes 1179656 | tf_op jit(solution)/shard_map/ppermute | solution.py:362
  78.4 2.6 %collective-permute-start.23 = (bf16[6,48,1536]{2,1,0:T(8,128)(2,1)}, bf16[6,48,1536]{2,1,0:T(8,128)(2,1)S(1)}, u32[]{:S(2)}, u32[]{:S(2)}) collective-permute-start(bf16[6,48,1536]{2,1,0:T(8,128)(2,1)} %get-tuple-element.62), channel_id=1, source_target_pairs={{0,16},{16,0},{1,17},{17,1},{2,18},{18,2},{3,19},{19,3},{4,20},{20... | collective-permute-start | bytes 2654216 | tf_op jit(solution)/shard_map/ppermute | solution.py:365
  82.2 9.0 %collective-permute-start.24 = (bf16[6,48,384]{2,1,0:T(8,128)(2,1)S(1)}, bf16[6,48,384]{2,1,0:T(8,128)(2,1)S(1)}, u32[]{:S(2)}, u32[]{:S(2)}) collective-permute-start(bf16[6,48,384]{2,1,0:T(8,128)(2,1)S(1)} %get-tuple-element.64), channel_id=1, source_target_pairs={{0,4},{4,8},{8,12},{12,0},{1,5},{5,9},{9,13},{13,1},{2,6},{6,10},{... | collective-permute-start | bytes 663560 | tf_op jit(solution)/shard_map/ppermute | solution.py:347
  83.4 13.6 %collective-permute-start.25 = (bf16[6,48,384]{2,1,0:T(8,128)(2,1)S(1)}, bf16[6,48,384]{2,1,0:T(8,128)(2,1)S(1)}, u32[]{:S(2)}, u32[]{:S(2)}) collective-permute-start(bf16[6,48,384]{2,1,0:T(8,128)(2,1)S(1)} %get-tuple-element.65), channel_id=1, source_target_pairs={{0,8},{4,12},{8,0},{12,4},{1,9},{5,13},{9,1},{13,5},{2,10},{6,14},... | collective-permute-start | bytes 663560 | tf_op jit(solution)/shard_map/ppermute | solution.py:347
  86.9 10.2 %collective-permute-start.26 = (bf16[6,48,384]{2,1,0:T(8,128)(2,1)S(1)}, bf16[6,48,384]{2,1,0:T(8,128)(2,1)S(1)}, u32[]{:S(2)}, u32[]{:S(2)}) collective-permute-start(bf16[6,48,384]{2,1,0:T(8,128)(2,1)S(1)} %get-tuple-element.66), channel_id=1, source_target_pairs={{0,12},{4,0},{8,4},{12,8},{1,13},{5,1},{9,5},{13,9},{2,14},{6,2},{... | collective-permute-start | bytes 663560 | tf_op jit(solution)/shard_map/ppermute | solution.py:347
  97.9 14.2 %collective-permute-start.27 = (bf16[6,48,96]{2,1,0:T(8,128)(2,1)S(1)}, bf16[6,48,96]{2,1,0:T(8,128)(2,1)S(1)}, u32[]{:S(2)}, u32[]{:S(2)}) collective-permute-start(bf16[6,48,96]{2,1,0:T(8,128)(2,1)S(1)} %get-tuple-element.68), channel_id=1, source_target_pairs={{0,1},{1,2},{2,3},{3,0},{4,5},{5,6},{6,7},{7,4},{8,9},{9,10},{10,1... | collective-permute-start | bytes 165896 | tf_op jit(solution)/shard_map/ppermute | solution.py:347
  100.4 14.8 %collective-permute-start.28 = (bf16[6,48,96]{2,1,0:T(8,128)(2,1)S(1)}, bf16[6,48,96]{2,1,0:T(8,128)(2,1)S(1)}, u32[]{:S(2)}, u32[]{:S(2)}) collective-permute-start(bf16[6,48,96]{2,1,0:T(8,128)(2,1)S(1)} %get-tuple-element.69), channel_id=1, source_target_pairs={{0,2},{1,3},{2,0},{3,1},{4,6},{5,7},{6,4},{7,5},{8,10},{9,11},{10,... | collective-permute-start | bytes 165896 | tf_op jit(solution)/shard_map/ppermute | solution.py:347
  103.1 12.1 %collective-permute-start.29 = (bf16[6,48,96]{2,1,0:T(8,128)(2,1)S(1)}, bf16[6,48,96]{2,1,0:T(8,128)(2,1)S(1)}, u32[]{:S(2)}, u32[]{:S(2)}) collective-permute-start(bf16[6,48,96]{2,1,0:T(8,128)(2,1)S(1)} %get-tuple-element.70), channel_id=1, source_target_pairs={{0,3},{1,0},{2,1},{3,2},{4,7},{5,4},{6,5},{7,6},{8,11},{9,8},{10,9... | collective-permute-start | bytes 165896 | tf_op jit(solution)/shard_map/ppermute | solution.py:347
  103.1 32.1 %collective-permute-start.20 = (bf16[768,128]{1,0:T(8,128)(2,1)S(1)}, bf16[768,128]{1,0:T(8,128)(2,1)S(1)}, u32[]{:S(2)}, u32[]{:S(2)}) collective-permute-start(bf16[768,128]{1,0:T(8,128)(2,1)S(1)} %get-tuple-element.56), channel_id=1, source_target_pairs={{0,3},{1,0},{2,1},{3,2},{4,7},{5,4},{6,5},{7,6},{8,11},{9,8},{10,9... | collective-permute-start | bytes 589832 | tf_op jit(solution)/shard_map/ppermute | solution.py:347
  104.8 30.4 %collective-permute-start.21 = (bf16[768,128]{1,0:T(8,128)(2,1)S(1)}, bf16[768,128]{1,0:T(8,128)(2,1)S(1)}, u32[]{:S(2)}, u32[]{:S(2)}) collective-permute-start(bf16[768,128]{1,0:T(8,128)(2,1)S(1)} %get-tuple-element.57), channel_id=1, source_target_pairs={{0,2},{1,3},{2,0},{3,1},{4,6},{5,7},{6,4},{7,5},{8,10},{9,11},{10,... | collective-permute-start | bytes 589832 | tf_op jit(solution)/shard_map/ppermute | solution.py:347
  112.0 23.3 %collective-permute-start.22 = (bf16[768,128]{1,0:T(8,128)(2,1)S(1)}, bf16[768,128]{1,0:T(8,128)(2,1)S(1)}, u32[]{:S(2)}, u32[]{:S(2)}) collective-permute-start(bf16[768,128]{1,0:T(8,128)(2,1)S(1)} %get-tuple-element.58), channel_id=1, source_target_pairs={{0,1},{1,2},{2,3},{3,0},{4,5},{5,6},{6,7},{7,4},{8,9},{9,10},{10,1... | collective-permute-start | bytes 589832 | tf_op jit(solution)/shard_map/ppermute | solution.py:347
  115.9 5.6 %collective-permute-start.30 = (bf16[6,48,96]{2,1,0:T(8,128)(2,1)S(1)}, bf16[6,48,96]{2,1,0:T(8,128)(2,1)S(1)}, u32[]{:S(2)}, u32[]{:S(2)}) collective-permute-start(bf16[6,48,96]{2,1,0:T(8,128)(2,1)S(1)} %get-tuple-element.72), channel_id=1, source_target_pairs={{0,64},{64,128},{128,192},{192,0},{1,65},{65,129},{129,193},{193,1... | collective-permute-start | bytes 165896 | tf_op jit(solution)/shard_map/ppermute | solution.py:347
  117.4 5.9 %collective-permute-start.31 = (bf16[6,48,96]{2,1,0:T(8,128)(2,1)S(1)}, bf16[6,48,96]{2,1,0:T(8,128)(2,1)S(1)}, u32[]{:S(2)}, u32[]{:S(2)}) collective-permute-start(bf16[6,48,96]{2,1,0:T(8,128)(2,1)S(1)} %get-tuple-element.73), channel_id=1, source_target_pairs={{0,128},{64,192},{128,0},{192,64},{1,129},{65,193},{129,1},{193,65... | collective-permute-start | bytes 165896 | tf_op jit(solution)/shard_map/ppermute | solution.py:347
  121.5 4.4 %collective-permute-start.32 = (bf16[6,48,96]{2,1,0:T(8,128)(2,1)S(1)}, bf16[6,48,96]{2,1,0:T(8,128)(2,1)S(1)}, u32[]{:S(2)}, u32[]{:S(2)}) collective-permute-start(bf16[6,48,96]{2,1,0:T(8,128)(2,1)S(1)} %get-tuple-element.74), channel_id=1, source_target_pairs={{0,192},{64,0},{128,64},{192,128},{1,193},{65,1},{129,65},{193,129... | collective-permute-start | bytes 165896 | tf_op jit(solution)/shard_map/ppermute | solution.py:347
  126.4 8.1 %collective-permute-start.33 = (bf16[3,48,96]{2,1,0:T(8,128)(2,1)S(1)}, bf16[3,48,96]{2,1,0:T(8,128)(2,1)S(1)}, u32[]{:S(2)}, u32[]{:S(2)}) collective-permute-start(bf16[3,48,96]{2,1,0:T(8,128)(2,1)S(1)} %get-tuple-element.76), channel_id=1, source_target_pairs={{0,32},{32,0},{1,33},{33,1},{2,34},{34,2},{3,35},{35,3},{4,36},{36... | collective-permute-start | bytes 82952 | tf_op jit(solution)/shard_map/ppermute | solution.py:385
  135.2 8.0 %collective-permute-start.34 = (bf16[48,96]{1,0:T(8,128)(2,1)S(1)}, bf16[48,96]{1,0:T(8,128)(2,1)S(1)}, u32[]{:S(2)}, u32[]{:S(2)}) collective-permute-start(bf16[48,96]{1,0:T(8,128)(2,1)S(1)} %get-tuple-element.78), channel_id=1, source_target_pairs={{0,16},{16,0},{1,17},{17,1},{2,18},{18,2},{3,19},{19,3},{4,20},{20... | collective-permute-start | bytes 27656 | tf_op jit(solution)/shard_map/ppermute | solution.py:390

commit v2 on v1

v2 whole, which is shorter than its diff:
```python
import math

import jax
import jax.numpy as jnp
from jax import lax
from jax.experimental import pallas as pl
from jax.experimental.pallas import tpu as pltpu
from jax.sharding import Mesh
from jax.sharding import PartitionSpec as P

HS = 192
HEADS = 4
HD = 768
D = 1536
ROWS = 128
EPS = 1e-06
SCALE = 1.0 / math.sqrt(HS)
SCALE2 = SCALE * math.log2(math.e)
BF = jnp.bfloat16
F32 = jnp.float32
NN = (((1,), (0,)), ((), ()))
NT = (((1,), (1,)), ((), ()))

SMEM = pl.BlockSpec(memory_space=pltpu.SMEM)
VMEM = pl.BlockSpec(memory_space=pltpu.VMEM)
ANY = pl.BlockSpec(memory_space=pl.ANY)
HBM = pl.BlockSpec(memory_space=pltpu.HBM)


def shape(dims, dtype=BF):
    return jax.ShapeDtypeStruct(dims, dtype)


def params(mib=16):
    return pltpu.CompilerParams(vmem_limit_bytes=mib * 2**20)


def dot(a, b, dims=NN):
    return lax.dot_general(a, b, dims, preferred_element_type=F32)


def flip(block):
    return jnp.transpose(block.astype(F32))


def normalise(tokens):
    rows = tokens.astype(F32)
    inverse = lax.rsqrt(jnp.mean(rows * rows, -1, keepdims=True) + EPS)
    return rows * inverse, inverse


CUT = 256
CUTS = 3 * HD // CUT


def project_kernel(place, tokens_in, weights_in, grads_in, *rest):
    blocks, (tokens, weights, grads, turned, sems) = rest[:4], rest[4:]
    fetches = [pltpu.make_async_copy(tokens_in, tokens, sems.at[0])]
    for n in range(CUTS):
        at = slice(n * CUT, (n + 1) * CUT)
        fetches.append(pltpu.make_async_copy(weights_in.at[:, at], weights.at[n], sems.at[n + 1]))
    fetches.append(pltpu.make_async_copy(grads_in, grads, sems.at[CUTS + 1]))
    for fetch in fetches:
        fetch.start()
    fetches[0].wait()
    rows = normalise(tokens[...])[0].astype(BF)
    last = None
    for n in range(CUTS):
        fetches[n + 1].wait()
        part = dot(rows, weights[n])
        if last is not None:
            turned[(n - 1) * CUT : n * CUT, :] = flip(last).astype(BF)
        last = part
    turned[3 * HD - CUT : 3 * HD, :] = flip(last).astype(BF)
    fetches[-1].wait()
    turned[3 * HD :, :] = flip(grads[...]).astype(BF)
    for k in range(4):
        head = place[0] ^ k
        for n, j in enumerate((1, 2, 0, 3)):
            at = pl.ds(pl.multiple_of(j * HD + head * HS, 64), HS)
            blocks[k][n * HS : (n + 1) * HS, :] = turned[at, :]


def project(place, tokens, weights, grads):
    return pl.pallas_call(
        project_kernel,
        in_specs=[SMEM, HBM, HBM, HBM],
        out_shape=[shape((4 * HS, ROWS))] * 4,
        scratch_shapes=[
            pltpu.VMEM((ROWS, D), BF),
            pltpu.VMEM((CUTS, D, CUT), BF),
            pltpu.VMEM((ROWS, HD), BF),
            pltpu.VMEM((4 * HD, ROWS), BF),
            pltpu.SemaphoreType.DMA((CUTS + 2,)),
        ],
        compiler_params=params(60),
        name="project",
    )(place, tokens, weights, grads)


def stack_kernel(*refs):
    kv, qd = refs[-2:]
    for k, block in enumerate(refs[:4]):
        at = slice(k * ROWS, (k + 1) * ROWS)
        kv[:, at] = block[: 2 * HS, :]
        qd[:, at] = block[2 * HS :, :]


def stack(blocks, after):
    return pl.pallas_call(
        stack_kernel,
        in_specs=[VMEM] * 4 + [ANY] * len(after),
        out_shape=[shape((2 * HS, 4 * ROWS))] * 2,
        compiler_params=params(),
        name="stack",
    )(*blocks, *after)


def side_by_side(blocks, wide):
    for k, block in enumerate(blocks):
        wide[:, k * 4 * ROWS : (k + 1) * 4 * ROWS] = block[...]


TILE = 256


def stats_kernel(*refs):
    kv_blocks, qd_blocks, (stats, kv, qd) = refs[:2], refs[2:4], refs[-3:]
    side_by_side(kv_blocks, kv)
    side_by_side(qd_blocks, qd)
    keys = flip(kv[:HS, :]).astype(BF)
    values = flip(kv[HS:, :]).astype(BF)
    for tile in range(8 * ROWS // TILE):
        at = slice(tile * TILE, (tile + 1) * TILE)
        scores = dot(keys, qd[:HS, at]) * SCALE2
        top = jnp.max(scores, 0, keepdims=True)
        powers = jnp.exp2(scores - top)
        d_probs = dot(values, qd[HS:, at])
        stats[0:1, at] = top
        stats[1:2, at] = jnp.sum(powers, 0, keepdims=True)
        stats[2:3, at] = jnp.sum(powers * d_probs, 0, keepdims=True)
        stats[3:8, at] = jnp.zeros((5, TILE), F32)


def stats_of(kv_blocks, qd_blocks):
    wide = pltpu.VMEM((2 * HS, 8 * ROWS), BF)
    return pl.pallas_call(
        stats_kernel,
        out_shape=shape((8, 8 * ROWS), F32),
        scratch_shapes=[wide, wide],
        compiler_params=params(),
        name="stats",
    )(*kv_blocks, *qd_blocks)


def attend_kernel(*refs):
    kv_blocks, qd_blocks, mine, theirs = refs[:2], refs[2:4], refs[4], refs[5]
    qo_own, qo_send, kv_own, kv_send, kv, qd, kv_sum = refs[-7:]
    side_by_side(kv_blocks, kv)
    side_by_side(qd_blocks, qd)
    keys = flip(kv[:HS, :]).astype(BF)
    values = flip(kv[HS:, :]).astype(BF)
    half = 4 * ROWS
    for tile in range(8 * ROWS // TILE):
        at = slice(tile * TILE, (tile + 1) * TILE)
        start = (tile * TILE + half) % (2 * half)
        across = slice(start, start + TILE)
        top_a, sum_a, total_a = mine[0:1, at], mine[1:2, at], mine[2:3, at]
        top_b, sum_b, total_b = theirs[0:1, across], theirs[1:2, across], theirs[2:3, across]
        top = jnp.maximum(top_a, top_b)
        by_a, by_b = jnp.exp2(top_a - top), jnp.exp2(top_b - top)
        share = 1.0 / (sum_a * by_a + sum_b * by_b)
        row_total = (total_a * by_a + total_b * by_b) * share
        scores = dot(keys, qd[:HS, at]) * SCALE2
        softmaxed = jnp.exp2(scores - top) * share
        d_probs = dot(values, qd[HS:, at])
        d_scores = (softmaxed * (d_probs - row_total) * SCALE).astype(BF)
        weights = softmaxed.astype(BF)
        d_queries = dot(kv[:HS, :], d_scores)
        attended = dot(kv[HS:, :], weights)
        if tile * TILE < half:
            qo_own[:HS, at] = d_queries
            qo_own[HS:, at] = attended
        else:
            qo_send[:HS, across] = d_queries.astype(BF)
            qo_send[HS:, across] = attended.astype(BF)
        d_keys = dot(qd[:HS, at], d_scores, NT)
        d_values = dot(qd[HS:, at], weights, NT)
        if tile == 0:
            kv_sum[:HS, :] = d_keys
            kv_sum[HS:, :] = d_values
        else:
            kv_sum[:HS, :] += d_keys
            kv_sum[HS:, :] += d_values
    kv_own[...] = kv_sum[:, :half]
    kv_send[...] = kv_sum[:, half:].astype(BF)


def attend(kv_blocks, qd_blocks, mine, theirs, after):
    wide = (2 * HS, 8 * ROWS)
    out = (2 * HS, 4 * ROWS)
    return pl.pallas_call(
        attend_kernel,
        in_specs=[VMEM] * (6 + len(after)),
        out_shape=[shape(out, F32), shape(out), shape(out, F32), shape(out)],
        scratch_shapes=[pltpu.VMEM(wide, BF), pltpu.VMEM(wide, BF), pltpu.VMEM(wide, F32)],
        compiler_params=params(24),
        name="attend",
    )(*kv_blocks, *qd_blocks, mine, theirs, *after)


def gradient_kernel(place, qo_own, qo_got, kv_own, kv_got, *refs):
    own, pair, second, middle, ends = refs[:5]
    back, (keep, send, normed, d_proj, cut) = refs[5:9], refs[9:]
    at_end = (place[0] == 0) | (place[0] == 3)
    third = jnp.where(at_end, ends[...], middle[...])
    for k, block in enumerate((own[...], pair[...], second[...], third)):
        normed[k * ROWS : (k + 1) * ROWS, :] = normalise(block)[0].astype(BF)
    q_sum = qo_own[...] + qo_got[...].astype(F32)
    kv_sum = kv_own[...] + kv_got[...].astype(F32)
    d_proj[:HS, :] = q_sum[:HS].astype(BF)
    d_proj[HS : 3 * HS, :] = kv_sum.astype(BF)
    attended = q_sum[HS:].astype(BF)
    for k in range(4):
        at = slice(k * ROWS, (k + 1) * ROWS)
        back[k][: 3 * HS, :] = d_proj[:, at]
        back[k][3 * HS :, :] = attended[:, at]
    counts = [jnp.int32(0), jnp.int32(0)]
    for j in range(3):
        at = slice(j * HS, (j + 1) * HS)
        term = dot(d_proj[at, :], normed[...]).astype(BF)
        for i in range(4):
            unit = 16 * j + 4 * place[0] + i
            core = lax.rem(lax.div(unit, 3), 2)
            slot = jnp.where(core == 0, counts[0], counts[1])
            cut[core, slot] = term[i * 48 : (i + 1) * 48]
            counts = [counts[0] + (1 - core), counts[1] + core]
    keep[...] = cut[place[2]]
    send[...] = cut[1 - place[2]]


def gradient(place, qo_own, qo_got, kv_own, kv_got, tokens):
    units = (6, 48, D)
    return pl.pallas_call(
        gradient_kernel,
        in_specs=[SMEM] + [VMEM] * 9,
        out_shape=[shape((4 * HS, ROWS))] * 4 + [shape(units)] * 2,
        scratch_shapes=[
            pltpu.VMEM((4 * ROWS, D), BF),
            pltpu.VMEM((3 * HS, 4 * ROWS), BF),
            pltpu.VMEM((2,) + units, BF),
        ],
        compiler_params=params(),
        name="gradient",
    )(place, qo_own, qo_got, kv_own, kv_got, *tokens)


WIDE = 512


def tokens_kernel(place, tokens, weights, *refs):
    blocks, (attended, d_tokens, done, columns, d_normed) = refs[:4], refs[4:]
    done[...] = jnp.zeros_like(done)
    for k in range(4):
        head = place[0] ^ k
        for j in range(4):
            at = pl.ds(pl.multiple_of(j * HD + head * HS, 64), HS)
            columns[at, :] = blocks[k][j * HS : (j + 1) * HS, :]
    attended[...] = flip(columns[3 * HD :, :]).astype(BF)
    d_proj = columns[: 3 * HD, :]
    unrounded, inverse = normalise(tokens[...])
    total = jnp.zeros((ROWS, 1), F32)
    for n in range(D // WIDE):
        at = slice(n * WIDE, (n + 1) * WIDE)
        part = jnp.transpose(dot(weights[at, :], d_proj))
        d_normed[:, at] = part
        total += jnp.sum(part * unrounded[:, at], -1, keepdims=True)
    d_tokens[...] = (inverse * (d_normed[...] - unrounded * (total * (1.0 / D)))).astype(BF)


def tokens_of(place, tokens, weights, blocks):
    return pl.pallas_call(
        tokens_kernel,
        in_specs=[SMEM] + [VMEM] * 6,
        out_shape=[shape((ROWS, HD)), shape((ROWS, D)), shape((8, 128), F32)],
        scratch_shapes=[
            pltpu.VMEM((4 * HD, ROWS), BF),
            pltpu.VMEM((ROWS, D), F32),
        ],
        compiler_params=params(20),
        name="d_tokens",
    )(place, tokens, weights, *blocks)


def small(kernel, name, scalars, blocks, outs, scratch, after=()):
    return pl.pallas_call(
        kernel,
        in_specs=[SMEM] * len(scalars) + [VMEM] * (len(blocks) + len(after)),
        out_shape=outs,
        scratch_shapes=scratch,
        compiler_params=params(),
        name=name,
    )(*scalars, *blocks, *after)


def split_y_kernel(place, mine, got, *refs):
    outs, cut = refs[:4], refs[4]
    cut[...] = (mine[...].astype(F32) + got[...].astype(F32)).astype(BF)
    for k in range(4):
        at = pl.ds(pl.multiple_of((place[1] ^ k) * 384, 384), 384)
        outs[k][...] = cut[:, :, at]


def split_z_kernel(place, *refs):
    blocks, outs, cut = refs[:4], refs[4:8], refs[8]
    total = sum(block[...].astype(F32) for block in blocks)
    for k in range(4):
        cut[k] = total[:, :, k * 96 : (k + 1) * 96].astype(BF)
    for k in range(4):
        outs[k][...] = cut[place[0] ^ k]


def lists():
    tables = []
    for core in range(2):
        count, table = [0] * HEADS, []
        for slot in range(24):
            head = (6 * (slot // 3) + 3 * core + slot % 3) % 16 // 4
            table.append((head, count[head]))
            count[head] += 1
        tables.append(table)
    return list(zip(*tables))


def split_x_kernel(place, *refs):
    blocks, outs, by_head, cut = refs[:4], refs[4:8], refs[8], refs[9]
    for k in range(4):
        by_head[place[0] ^ k] = blocks[k][...]
    for slot, (first, second) in enumerate(lists()):
        head, at = (jnp.where(place[2] == 0, a, b) for a, b in zip(first, second))
        cut[slot] = by_head[head, at]
    for k in range(4):
        outs[k][...] = cut[pl.ds((place[3] ^ k) * 6, 6)]


def split_zh_kernel(place, *refs):
    blocks, (keep, send, cut) = refs[:4], refs[-3:]
    cut[...] = sum(block[...].astype(F32) for block in blocks)
    keep[...] = cut[pl.ds(place[4] * 3, 3)]
    send[...] = cut[pl.ds(3 - place[4] * 3, 3)].astype(BF)


def finish_kernel(place, mine, got, out):
    out[...] = (mine[...] + got[...].astype(F32)).reshape(144, 96)


def exchange(by):
    return [(i, i ^ by) for i in range(4)]


def per_device(tokens, w_proj, d_attended):
    tokens = tokens[0]
    place = jnp.stack([lax.axis_index(a) for a in ("zl", "y", "c", "x", "zh")]).astype(jnp.int32)
    near, far, swap = exchange(1), exchange(3), [(0, 1), (1, 0)]

    def spread(blocks, axis):
        return [blocks[0]] + [lax.ppermute(blocks[k], axis, exchange(k)) for k in (1, 2, 3)]

    pair = lax.ppermute(tokens, "zl", near)
    middle = lax.ppermute(tokens, "zl", [(1, 2), (2, 1)])
    heads = spread(project(place, tokens, w_proj, d_attended[0]), "zl")
    kv, qd = stack(heads, [pair, middle])
    late = lax.optimization_barrier((tokens, kv))[0]
    second = lax.ppermute(late, "zl", exchange(2))
    ends = lax.ppermute(late, "zl", [(0, 3), (3, 0)])
    kv, qd = [kv, lax.ppermute(kv, "y", far)], [qd, lax.ppermute(qd, "y", near)]

    mine = stats_of(kv, qd)
    theirs = lax.ppermute(mine, "y", near)
    qo_own, qo_send, kv_own, kv_send = attend(kv, qd, mine, theirs, [ends])
    qo_got = lax.ppermute(qo_send, "y", near)
    kv_got = lax.ppermute(kv_send, "y", far)

    rows = [tokens, pair, second, middle, ends]
    *back, keep, send = gradient(place, qo_own, qo_got, kv_own, kv_got, rows)
    returned = [back[0], lax.ppermute(back[1], "zl", near)]
    later = lax.optimization_barrier((back[2], back[3], returned[1]))
    returned += [lax.ppermute(later[k - 2], "zl", exchange(k)) for k in (2, 3)]
    attended, d_tokens, done = tokens_of(place, tokens, w_proj, returned)
    got = lax.ppermute(send, "c", swap)
    blocks = small(
        split_y_kernel, "split_y", [place], [keep, got],
        [shape((6, 48, 384))] * 4, [pltpu.VMEM((6, 48, D), BF)],
    )
    blocks = spread(blocks, "y")
    blocks = small(
        split_z_kernel, "split_z", [place], blocks,
        [shape((6, 48, 96))] * 4, [pltpu.VMEM((4, 6, 48, 96), BF)],
    )
    blocks = spread(blocks, "zl")
    blocks = small(
        split_x_kernel, "split_x", [place], blocks,
        [shape((6, 48, 96))] * 4,
        [pltpu.VMEM((4, 6, 48, 96), BF), pltpu.VMEM((24, 48, 96), BF)],
    )
    blocks = spread(blocks, "x")
    keep, send = small(
        split_zh_kernel, "split_zh", [place], blocks,
        [shape((3, 48, 96), F32), shape((3, 48, 96))], [pltpu.VMEM((6, 48, 96), F32)], [done],
    )
    got = lax.ppermute(send, "zh", swap)
    grad = small(finish_kernel, "finish", [place], [keep, got], shape((144, 96), F32), [])
    return (attended[None], d_tokens[None], grad.T)


def solution(mesh):
    fine = Mesh(mesh.devices.reshape(4, 2, 2, 4, 4), ("x", "zh", "c", "y", "zl"))
    dp, seq = ("x", "zh", "c"), ("y", "zl")
    return jax.shard_map(
        per_device,
        mesh=fine,
        in_specs=(P(dp, seq, None), P(), P(dp, seq, None)),
        out_specs=(P(dp, seq, None), P(dp, seq, None), P(seq, dp)),
        check_vma=False,
    )
```

time: 147 us -> 120 us (0.82); the launches traced: 144 us -> 120 us
  starting transfers between devices: 60.4 us -> 36 us
  waiting for transfers between devices: 54.9 us -> 59.4 us
  Pallas kernels: 25.6 us -> 22.3 us
    ppermute x29 -> x21, starting transfers between devices: 49.5 us -> 27.5 us  [the longest x12 16.8 us: spread(): lax.ppermute(blocks[k], axis, exchange(k))]
    ppermute x1, waiting for transfers between devices: 0.01 us -> 3.79 us  [per_device(): theirs = lax.ppermute(mine, 'y', near)]
    pallas_call x10, Pallas kernels: 23.6 us -> 20.4 us  [the longest x1 6.4 us: project(): pl.pallas_call(project_kernel, in_specs=[SMEM, HBM, HBM, HBM], out_shape=...]
    unnamed x7 -> x10, local copies, waits for them, and re-layouts: 2.67 us -> 0.94 us
    ppermute x29 -> x21, waiting for transfers between devices: 50.3 us -> 49 us  [the longest x12 37 us: spread(): lax.ppermute(blocks[k], axis, exchange(k))]
  transfers between devices with their start and end apart: 35 -> 26, of which waited for: 18 -> 18; matrix products, arithmetic and copies ran while one was open for 0% -> 1% of each run, Pallas kernels for 9% -> 15%
where the time goes in v2:
time: 120 us
  waiting for transfers between devices  59.4 us (50%)
  starting transfers between devices  36 us (30%)
  Pallas kernels  22.3 us (19%)
  local copies, waits for them, and re-layouts  1.57 us (1%)
    ppermute x12, waiting for transfers between devices, spread(): lax.ppermute(blocks[k], axis, exchange(k))  37 us
    ppermute x12, starting transfers between devices, spread(): lax.ppermute(blocks[k], axis, exchange(k))  16.8 us
    pallas_call x1, Pallas kernels, project(): pl.pallas_call(project_kernel, in_specs=[SMEM, HBM, HBM, HBM], out_shape=...  6.4 us
    ppermute x1, starting transfers between devices, per_device(): got = lax.ppermute(send, 'zh', swap)  5.81 us
    ppermute x1, waiting for transfers between devices, per_device(): lax.ppermute(qd, 'y', near)  4.98 us
    ppermute x1, waiting for transfers between devices, per_device(): second = lax.ppermute(late, 'zl', exchange(2))  4.45 us
    pallas_call x5, Pallas kernels, small(): pl.pallas_call(kernel, in_specs=[SMEM] * len(scalars) + [VMEM] * (len(blo...  4.37 us
    ppermute x1, starting transfers between devices, per_device(): middle = lax.ppermute(tokens, 'zl', [(1, 2), (2, 1)])  3.96 us
  transfers between devices with their start and end apart: 26, of which 18 were waited for; matrix products, arithmetic and copies ran while one was open for 1% of the time, Pallas kernels for 15%

profile of v2, /device:TPU:32, one launch (start us, length us, event | category | flops | bytes accessed | tf_op | source)
XLA Modules:
  0.0 120.1 jit_solution(6271623738372441902)
XLA Ops:
  0.6 0.0 copy-start
  0.6 4.0 %collective-permute-start.4 = (bf16[128,1536]{1,0:T(8,128)(2,1)}, bf16[128,1536]{1,0:T(8,128)(2,1)S(1)}, u32[]{:S(2)}, u32[]{:S(2)}) collective-permute-start(bf16[128,1536]{1,0:T(8,128)(2,1)} %bitcast.12), channel_id=1, source_target_pairs={{1,2},{2,1},{5,6},{6,5},{9,10},{10,9},{13,14},{14,13},{17,18},{18,... | collective-permute-start | bytes 1179656 | tf_op jit(solution)/shard_map/ppermute | solution.py:370
  4.6 0.1 collective-permute-start.3
  4.7 0.6 stack.24.place
  5.4 6.4 %project.1 = (bf16[768,128]{1,0:T(8,128)(2,1)}, bf16[768,128]{1,0:T(8,128)(2,1)}, bf16[768,128]{1,0:T(8,128)(2,1)}, bf16[768,128]{1,0:T(8,128)(2,1)}) custom-call(s32[5]{0:T(128)} %stack.24.place, bf16[128,1536]{1,0:T(8,128)(2,1)} %bitcast.14, bf16[1536,2304]{1,0:T(8,128)(2,1)} %weights.1, bf16[128,768]{1,0:T(8,128)(2,1)} %bitcast.19), custom_call_target="tpu_custom_call" | custom-call | tf_op jit(solution)/shard_map/project/pallas_call | solution.py:85
  11.8 2.1 %collective-permute-start = (bf16[768,128]{1,0:T(8,128)(2,1)}, bf16[768,128]{1,0:T(8,128)(2,1)S(1)}, u32[]{:S(2)}, u32[]{:S(2)}) collective-permute-start(bf16[768,128]{1,0:T(8,128)(2,1)} %get-tuple-element.40), channel_id=1, source_target_pairs={{0,1},{1,0},{2,3},{3,2},{4,5},{5,4},{6,7},{7,6},{8,9},{9,8},{10,11... | collective-permute-start | bytes 589832 | tf_op jit(solution)/shard_map/ppermute | solution.py:367
  13.8 0.1 collective-permute-start.1
  14.0 1.4 %collective-permute-start.2 = (bf16[768,128]{1,0:T(8,128)(2,1)}, bf16[768,128]{1,0:T(8,128)(2,1)S(1)}, u32[]{:S(2)}, u32[]{:S(2)}) collective-permute-start(bf16[768,128]{1,0:T(8,128)(2,1)} %get-tuple-element.42), channel_id=1, source_target_pairs={{0,3},{1,2},{2,1},{3,0},{4,7},{5,6},{6,5},{7,4},{8,11},{9,10},{10,... | collective-permute-start | bytes 589832 | tf_op jit(solution)/shard_map/ppermute | solution.py:367
  15.4 5.6 %collective-permute-done.refs_1_ = bf16[768,128]{1,0:T(8,128)(2,1)S(1)} collective-permute-done((bf16[768,128]{1,0:T(8,128)(2,1)}, bf16[768,128]{1,0:T(8,128)(2,1)S(1)}, u32[]{:S(2)}, u32[]{:S(2)}) %collective-permute-start) | collective-permute-done | bytes 196640 | tf_op jit(solution)/shard_map/ppermute | solution.py:367
  21.0 6.9 %collective-permute-done.1.refs_2_ = bf16[768,128]{1,0:T(8,128)(2,1)S(1)} collective-permute-done((bf16[768,128]{1,0:T(8,128)(2,1)}, bf16[768,128]{1,0:T(8,128)(2,1)S(1)}, u32[]{:S(2)}, u32[]{:S(2)}) %collective-permute-start.1) | collective-permute-done | bytes 196640 | tf_op jit(solution)/shard_map/ppermute | solution.py:367
  27.9 4.4 %collective-permute-done.2.refs_3_ = bf16[768,128]{1,0:T(8,128)(2,1)S(1)} collective-permute-done((bf16[768,128]{1,0:T(8,128)(2,1)}, bf16[768,128]{1,0:T(8,128)(2,1)S(1)}, u32[]{:S(2)}, u32[]{:S(2)}) %collective-permute-start.2) | collective-permute-done | bytes 196640 | tf_op jit(solution)/shard_map/ppermute | solution.py:367
  32.4 0.0 collective-permute-done.4.refs_5_.refs_3_
  32.4 0.0 collective-permute-done.3.refs_4_.refs_1_
  32.4 0.9 copy-done.1
  33.3 0.1 stack.25
  33.4 1.7 %collective-permute-start.6 = (bf16[384,512]{1,0:T(8,128)(2,1)S(1)}, bf16[384,512]{1,0:T(8,128)(2,1)S(1)}, u32[]{:S(2)}, u32[]{:S(2)}) collective-permute-start(bf16[384,512]{1,0:T(8,128)(2,1)S(1)} %get-tuple-element.44.refs_2_), channel_id=1, source_target_pairs={{0,4},{4,0},{8,12},{12,8},{1,5},{5,1},{9,13},{13,9},{2,6},{6,2},{1... | collective-permute-start | bytes 1179656 | tf_op jit(solution)/shard_map/ppermute | solution.py:376
  35.1 2.2 %collective-permute-start.5 = (bf16[384,512]{1,0:T(8,128)(2,1)S(1)}, bf16[384,512]{1,0:T(8,128)(2,1)S(1)}, u32[]{:S(2)}, u32[]{:S(2)}) collective-permute-start(bf16[384,512]{1,0:T(8,128)(2,1)S(1)} %get-tuple-element.43.refs_0_), channel_id=1, source_target_pairs={{0,12},{4,8},{8,4},{12,0},{1,13},{5,9},{9,5},{13,1},{2,14},{6,10},... | collective-permute-start | bytes 1179656 | tf_op jit(solution)/shard_map/ppermute | solution.py:376
  37.3 0.7 collective-permute-start.8
  38.0 5.0 %collective-permute-done.6.refs_3_ = bf16[384,512]{1,0:T(8,128)(2,1)S(1)} collective-permute-done((bf16[384,512]{1,0:T(8,128)(2,1)S(1)}, bf16[384,512]{1,0:T(8,128)(2,1)S(1)}, u32[]{:S(2)}, u32[]{:S(2)}) %collective-permute-start.6) | collective-permute-done | bytes 393248 | tf_op jit(solution)/shard_map/ppermute | solution.py:376
  43.0 2.5 %collective-permute-done.5.refs_1_ = bf16[384,512]{1,0:T(8,128)(2,1)S(1)} collective-permute-done((bf16[384,512]{1,0:T(8,128)(2,1)S(1)}, bf16[384,512]{1,0:T(8,128)(2,1)S(1)}, u32[]{:S(2)}, u32[]{:S(2)}) %collective-permute-start.5) | collective-permute-done | bytes 393248 | tf_op jit(solution)/shard_map/ppermute | solution.py:376
  45.5 1.9 %stats.1.refs_4_ = f32[8,1024]{1,0:T(8,128)S(1)} custom-call(bf16[384,512]{1,0:T(8,128)(2,1)S(1)} %get-tuple-element.43.refs_0_, bf16[384,512]{1,0:T(8,128)(2,1)S(1)} %collective-permute-done.5.refs_1_, bf16[384,512]{1,0:T(8,128)(2,1)S(1)} %get-tuple-element.44.refs_2_, bf16[384,512]{1,0:T(8,128)(2,1)S(1)} %collective-permute-done.6.refs_3_), custom_call_target="tpu_custom_call" | custom-call | tf_op jit(solution)/shard_map/stats/pallas_call | solution.py:147
  47.3 0.1 collective-permute-start.7
  47.4 0.1 collective-permute-start.11
  47.5 0.0 collective-permute-done.8.refs_6_.refs_4_
  47.5 3.8 %collective-permute-done.7.refs_5_ = f32[8,1024]{1,0:T(8,128)S(1)} collective-permute-done((f32[8,1024]{1,0:T(8,128)S(1)}, f32[8,1024]{1,0:T(8,128)S(1)}, u32[]{:S(2)}, u32[]{:S(2)}) %collective-permute-start.7) | collective-permute-done | bytes 32800 | tf_op jit(solution)/shard_map/ppermute | solution.py:379
  51.3 3.6 %attend.1 = (f32[384,512]{1,0:T(8,128)S(1)}, bf16[384,512]{1,0:T(8,128)(2,1)S(1)}, f32[384,512]{1,0:T(8,128)S(1)}, bf16[384,512]{1,0:T(8,128)(2,1)S(1)}) custom-call(bf16[384,512]{1,0:T(8,128)(2,1)S(1)} %get-tuple-element.43.refs_0_, bf16[384,512]{1,0:T(8,128)(2,1)S(1)} %collective-permute-done.5.refs_1_, bf16[384,512]{1,0:T(8,128)(2,1)S(1)} %get-tuple-element.44.refs_2_, ...), custom_call_target="tpu_custom_call" | custom-call | tf_op jit(solution)/shard_map/attend/pallas_call | solution.py:202
  55.0 0.3 collective-permute-start.9
  55.3 2.3 %collective-permute-start.10 = (bf16[384,512]{1,0:T(8,128)(2,1)S(1)}, bf16[384,512]{1,0:T(8,128)(2,1)S(1)}, u32[]{:S(2)}, u32[]{:S(2)}) collective-permute-start(bf16[384,512]{1,0:T(8,128)(2,1)S(1)} %get-tuple-element.49), channel_id=1, source_target_pairs={{0,12},{4,8},{8,4},{12,0},{1,13},{5,9},{9,5},{13,1},{2,14},{6,10},... | collective-permute-start | bytes 1179656 | tf_op jit(solution)/shard_map/ppermute | solution.py:382
  57.5 4.4 %collective-permute-done.11.refs_2_ = bf16[128,1536]{1,0:T(8,128)(2,1)S(1)} collective-permute-done((bf16[128,1536]{1,0:T(8,128)(2,1)S(1)}, bf16[128,1536]{1,0:T(8,128)(2,1)S(1)}, u32[]{:S(2)}, u32[]{:S(2)}) %collective-permute-start.11) | collective-permute-done | bytes 393248 | tf_op jit(solution)/shard_map/ppermute | solution.py:374
  62.0 1.1 collective-permute-done.9.qo_got
  63.0 1.3 %collective-permute-done.10.kv_got = bf16[384,512]{1,0:T(8,128)(2,1)S(1)} collective-permute-done((bf16[384,512]{1,0:T(8,128)(2,1)S(1)}, bf16[384,512]{1,0:T(8,128)(2,1)S(1)}, u32[]{:S(2)}, u32[]{:S(2)}) %collective-permute-start.10) | collective-permute-done | bytes 393248 | tf_op jit(solution)/shard_map/ppermute | solution.py:382
  64.3 2.3 %gradient.1 = (bf16[768,128]{1,0:T(8,128)(2,1)S(1)}, bf16[768,128]{1,0:T(8,128)(2,1)S(1)}, bf16[768,128]{1,0:T(8,128)(2,1)S(1)}, bf16[768,128]{1,0:T(8,128)(2,1)...) custom-call(s32[5]{0:T(128)S(1)} %copy-done.2, f32[384,512]{1,0:T(8,128)S(1)} %get-tuple-element.46.qo_own, ...), custom_call_target="tpu_custom_call" | custom-call | tf_op jit(solution)/shard_map/gradient/pallas_call | solution.py:244
  66.6 0.1 collective-permute-start.15
  66.7 0.3 collective-permute-start.12
  67.1 2.1 %collective-permute-done.15.got = bf16[6,48,1536]{2,1,0:T(8,128)(2,1)S(1)} collective-permute-done((bf16[6,48,1536]{2,1,0:T(8,128)(2,1)S(1)}, bf16[6,48,1536]{2,1,0:T(8,128)(2,1)S(1)}, u32[]{:S(2)}, u32[]{:S(2)}) %collective-permute-start.15) | collective-permute-done | bytes 884768 | tf_op jit(solution)/shard_map/ppermute | solution.py:390
  69.1 1.1 split_y.1
  70.2 0.8 collective-permute-start.16
  71.0 2.9 %collective-permute-start.17 = (bf16[6,48,384]{2,1,0:T(8,128)(2,1)S(1)}, bf16[6,48,384]{2,1,0:T(8,128)(2,1)S(1)}, u32[]{:S(2)}, u32[]{:S(2)}) collective-permute-start(bf16[6,48,384]{2,1,0:T(8,128)(2,1)S(1)} %get-tuple-element.62), channel_id=1, source_target_pairs={{0,8},{4,12},{8,0},{12,4},{1,9},{5,13},{9,1},{13,5},{2,10},{6,14},... | collective-permute-start | bytes 663560 | tf_op jit(solution)/shard_map/ppermute | solution.py:367
  73.9 1.1 collective-permute-start.18
  75.0 0.0 collective-permute-done.12.refs_1_
  75.0 1.0 collective-permute-start.13
  76.0 0.7 collective-permute-start.14
  76.7 1.9 %collective-permute-done.16.refs_1_ = bf16[6,48,384]{2,1,0:T(8,128)(2,1)S(1)} collective-permute-done((bf16[6,48,384]{2,1,0:T(8,128)(2,1)S(1)}, bf16[6,48,384]{2,1,0:T(8,128)(2,1)S(1)}, u32[]{:S(2)}, u32[]{:S(2)}) %collective-permute-start.16) | collective-permute-done | bytes 221216 | tf_op jit(solution)/shard_map/ppermute | solution.py:367
  78.6 5.7 %collective-permute-done.17.refs_2_ = bf16[6,48,384]{2,1,0:T(8,128)(2,1)S(1)} collective-permute-done((bf16[6,48,384]{2,1,0:T(8,128)(2,1)S(1)}, bf16[6,48,384]{2,1,0:T(8,128)(2,1)S(1)}, u32[]{:S(2)}, u32[]{:S(2)}) %collective-permute-start.17) | collective-permute-done | bytes 221216 | tf_op jit(solution)/shard_map/ppermute | solution.py:367
  84.2 2.6 %collective-permute-done.18.refs_3_ = bf16[6,48,384]{2,1,0:T(8,128)(2,1)S(1)} collective-permute-done((bf16[6,48,384]{2,1,0:T(8,128)(2,1)S(1)}, bf16[6,48,384]{2,1,0:T(8,128)(2,1)S(1)}, u32[]{:S(2)}, u32[]{:S(2)}) %collective-permute-start.18) | collective-permute-done | bytes 221216 | tf_op jit(solution)/shard_map/ppermute | solution.py:367
  86.8 0.8 split_z.1
  87.6 0.2 collective-permute-start.19
  87.8 1.9 %collective-permute-start.20 = (bf16[6,48,96]{2,1,0:T(8,128)(2,1)S(1)}, bf16[6,48,96]{2,1,0:T(8,128)(2,1)S(1)}, u32[]{:S(2)}, u32[]{:S(2)}) collective-permute-start(bf16[6,48,96]{2,1,0:T(8,128)(2,1)S(1)} %get-tuple-element.66), channel_id=1, source_target_pairs={{0,2},{1,3},{2,0},{3,1},{4,6},{5,7},{6,4},{7,5},{8,10},{9,11},{10,... | collective-permute-start | bytes 165896 | tf_op jit(solution)/shard_map/ppermute | solution.py:367
  89.8 1.4 %collective-permute-start.21 = (bf16[6,48,96]{2,1,0:T(8,128)(2,1)S(1)}, bf16[6,48,96]{2,1,0:T(8,128)(2,1)S(1)}, u32[]{:S(2)}, u32[]{:S(2)}) collective-permute-start(bf16[6,48,96]{2,1,0:T(8,128)(2,1)S(1)} %get-tuple-element.67), channel_id=1, source_target_pairs={{0,3},{1,2},{2,1},{3,0},{4,7},{5,6},{6,5},{7,4},{8,11},{9,10},{10,... | collective-permute-start | bytes 165896 | tf_op jit(solution)/shard_map/ppermute | solution.py:367
  91.2 1.6 %collective-permute-done.19.refs_1_ = bf16[6,48,96]{2,1,0:T(8,128)(2,1)S(1)} collective-permute-done((bf16[6,48,96]{2,1,0:T(8,128)(2,1)S(1)}, bf16[6,48,96]{2,1,0:T(8,128)(2,1)S(1)}, u32[]{:S(2)}, u32[]{:S(2)}) %collective-permute-start.19) | collective-permute-done | bytes 55328 | tf_op jit(solution)/shard_map/ppermute | solution.py:367
  92.8 4.8 %collective-permute-done.20.refs_2_ = bf16[6,48,96]{2,1,0:T(8,128)(2,1)S(1)} collective-permute-done((bf16[6,48,96]{2,1,0:T(8,128)(2,1)S(1)}, bf16[6,48,96]{2,1,0:T(8,128)(2,1)S(1)}, u32[]{:S(2)}, u32[]{:S(2)}) %collective-permute-start.20) | collective-permute-done | bytes 55328 | tf_op jit(solution)/shard_map/ppermute | solution.py:367
  97.6 2.1 %collective-permute-done.21.refs_3_ = bf16[6,48,96]{2,1,0:T(8,128)(2,1)S(1)} collective-permute-done((bf16[6,48,96]{2,1,0:T(8,128)(2,1)S(1)}, bf16[6,48,96]{2,1,0:T(8,128)(2,1)S(1)}, u32[]{:S(2)}, u32[]{:S(2)}) %collective-permute-start.21) | collective-permute-done | bytes 55328 | tf_op jit(solution)/shard_map/ppermute | solution.py:367
  99.7 0.7 split_x.1
  100.5 1.6 %collective-permute-start.22 = (bf16[6,48,96]{2,1,0:T(8,128)(2,1)S(1)}, bf16[6,48,96]{2,1,0:T(8,128)(2,1)S(1)}, u32[]{:S(2)}, u32[]{:S(2)}) collective-permute-start(bf16[6,48,96]{2,1,0:T(8,128)(2,1)S(1)} %get-tuple-element.69), channel_id=1, source_target_pairs={{0,64},{64,0},{128,192},{192,128},{1,65},{65,1},{129,193},{193,129... | collective-permute-start | bytes 165896 | tf_op jit(solution)/shard_map/ppermute | solution.py:367
  102.0 2.7 %collective-permute-start.23 = (bf16[6,48,96]{2,1,0:T(8,128)(2,1)S(1)}, bf16[6,48,96]{2,1,0:T(8,128)(2,1)S(1)}, u32[]{:S(2)}, u32[]{:S(2)}) collective-permute-start(bf16[6,48,96]{2,1,0:T(8,128)(2,1)S(1)} %get-tuple-element.70), channel_id=1, source_target_pairs={{0,128},{64,192},{128,0},{192,64},{1,129},{65,193},{129,1},{193,65... | collective-permute-start | bytes 165896 | tf_op jit(solution)/shard_map/ppermute | solution.py:367
  104.8 0.5 collective-permute-start.24
  105.3 0.0 collective-permute-done.13.refs_2_
  105.3 0.0 collective-permute-done.14.refs_3_
  105.3 3.6 %d_tokens.1 = (bf16[128,768]{1,0:T(8,128)(2,1)}, bf16[128,1536]{1,0:T(8,128)(2,1)}, f32[8,128]{1,0:T(8,128)S(1)}) custom-call(s32[5]{0:T(128)S(1)} %copy-done.2, bf16[128,1536]{1,0:T(8,128)(2,1)S(1)} %bitcast.18, bf16[1536,2304]{1,0:T(8,128)(2,1)S(1)} %bitcast.11, bf16[768,128]{1,0:T(8,128)(2,1)S(1)} %get-tuple-element.50.refs_0_, ...), custom_call_target="tpu_custom_call" | custom-call | tf_op jit(solution)/shard_map/d_tokens/pallas_call | solution.py:282
  108.9 1.4 %collective-permute-done.24.refs_3_ = bf16[6,48,96]{2,1,0:T(8,128)(2,1)S(1)} collective-permute-done((bf16[6,48,96]{2,1,0:T(8,128)(2,1)S(1)}, bf16[6,48,96]{2,1,0:T(8,128)(2,1)S(1)}, u32[]{:S(2)}, u32[]{:S(2)}) %collective-permute-start.24) | collective-permute-done | bytes 55328 | tf_op jit(solution)/shard_map/ppermute | solution.py:367
  110.3 0.6 split_zh.1
  110.9 5.8 %collective-permute-start.25 = (bf16[3,48,96]{2,1,0:T(8,128)(2,1)S(1)}, bf16[3,48,96]{2,1,0:T(8,128)(2,1)S(1)}, u32[]{:S(2)}, u32[]{:S(2)}) collective-permute-start(bf16[3,48,96]{2,1,0:T(8,128)(2,1)S(1)} %get-tuple-element.74), channel_id=1, source_target_pairs={{0,32},{32,0},{1,33},{33,1},{2,34},{34,2},{3,35},{35,3},{4,36},{36... | collective-permute-start | bytes 82952 | tf_op jit(solution)/shard_map/ppermute | solution.py:411
  116.7 2.1 %collective-permute-done.25.got = bf16[3,48,96]{2,1,0:T(8,128)(2,1)S(1)} collective-permute-done((bf16[3,48,96]{2,1,0:T(8,128)(2,1)S(1)}, bf16[3,48,96]{2,1,0:T(8,128)(2,1)S(1)}, u32[]{:S(2)}, u32[]{:S(2)}) %collective-permute-start.25) | collective-permute-done | bytes 27680 | tf_op jit(solution)/shard_map/ppermute | solution.py:411
  118.9 1.2 finish.1
  (11 shorter events, 0.0 us)
Async XLA Ops:
  0.6 36.7 %copy-start = (bf16[1,128,1536]{2,1,0:T(8,128)(2,1)S(1)}, bf16[1,128,1536]{2,1,0:T(8,128)(2,1)}, u32[]{:S(2)}) copy-start(bf16[1,128,1536]{2,1,0:T(8,128)(2,1)} %param.3) | copy-start | bytes 1179652
  0.6 31.7 %collective-permute-start.4 = (bf16[128,1536]{1,0:T(8,128)(2,1)}, bf16[128,1536]{1,0:T(8,128)(2,1)S(1)}, u32[]{:S(2)}, u32[]{:S(2)}) collective-permute-start(bf16[128,1536]{1,0:T(8,128)(2,1)} %bitcast.12), channel_id=1, source_target_pairs={{1,2},{2,1},{5,6},{6,5},{9,10},{10,9},{13,14},{14,13},{17,18},{18,... | collective-permute-start | bytes 1179656 | tf_op jit(solution)/shard_map/ppermute | solution.py:370
  4.6 27.8 %collective-permute-start.3 = (bf16[128,1536]{1,0:T(8,128)(2,1)}, bf16[128,1536]{1,0:T(8,128)(2,1)S(1)}, u32[]{:S(2)}, u32[]{:S(2)}) collective-permute-start(bf16[128,1536]{1,0:T(8,128)(2,1)} %bitcast.13), channel_id=1, source_target_pairs={{0,1},{1,0},{2,3},{3,2},{4,5},{5,4},{6,7},{7,6},{8,9},{9,8},{10,11... | collective-permute-start | bytes 1179656 | tf_op jit(solution)/shard_map/ppermute | solution.py:369
  5.3 59.0 %copy-start.2 = (s32[5]{0:T(128)S(1)}, s32[5]{0:T(128)}, u32[]{:S(2)}) copy-start(s32[5]{0:T(128)} %stack.24.place) | copy-start | bytes 64
  5.3 99.9 %slice-start = ((s8[7077888]{0:T(1024)(128)(4,1)}), s8[2883584]{0:T(1024)(128)(4,1)S(1)}, s32[]{:S(2)}) async-start(s8[7077888]{0:T(1024)(128)(4,1)} %bitcast.10), calls=%async_computation | async-start | bytes 5767168
  11.8 9.3 %collective-permute-start = (bf16[768,128]{1,0:T(8,128)(2,1)}, bf16[768,128]{1,0:T(8,128)(2,1)S(1)}, u32[]{:S(2)}, u32[]{:S(2)}) collective-permute-start(bf16[768,128]{1,0:T(8,128)(2,1)} %get-tuple-element.40), channel_id=1, source_target_pairs={{0,1},{1,0},{2,3},{3,2},{4,5},{5,4},{6,7},{7,6},{8,9},{9,8},{10,11... | collective-permute-start | bytes 589832 | tf_op jit(solution)/shard_map/ppermute | solution.py:367
  13.8 14.1 %collective-permute-start.1 = (bf16[768,128]{1,0:T(8,128)(2,1)}, bf16[768,128]{1,0:T(8,128)(2,1)S(1)}, u32[]{:S(2)}, u32[]{:S(2)}) collective-permute-start(bf16[768,128]{1,0:T(8,128)(2,1)} %get-tuple-element.41), channel_id=1, source_target_pairs={{0,2},{1,3},{2,0},{3,1},{4,6},{5,7},{6,4},{7,5},{8,10},{9,11},{10,... | collective-permute-start | bytes 589832 | tf_op jit(solution)/shard_map/ppermute | solution.py:367
  14.0 18.4 %collective-permute-start.2 = (bf16[768,128]{1,0:T(8,128)(2,1)}, bf16[768,128]{1,0:T(8,128)(2,1)S(1)}, u32[]{:S(2)}, u32[]{:S(2)}) collective-permute-start(bf16[768,128]{1,0:T(8,128)(2,1)} %get-tuple-element.42), channel_id=1, source_target_pairs={{0,3},{1,2},{2,1},{3,0},{4,7},{5,6},{6,5},{7,4},{8,11},{9,10},{10,... | collective-permute-start | bytes 589832 | tf_op jit(solution)/shard_map/ppermute | solution.py:367
  32.4 0.9 copy-start.1
  33.4 9.5 %collective-permute-start.6 = (bf16[384,512]{1,0:T(8,128)(2,1)S(1)}, bf16[384,512]{1,0:T(8,128)(2,1)S(1)}, u32[]{:S(2)}, u32[]{:S(2)}) collective-permute-start(bf16[384,512]{1,0:T(8,128)(2,1)S(1)} %get-tuple-element.44.refs_2_), channel_id=1, source_target_pairs={{0,4},{4,0},{8,12},{12,8},{1,5},{5,1},{9,13},{13,9},{2,6},{6,2},{1... | collective-permute-start | bytes 1179656 | tf_op jit(solution)/shard_map/ppermute | solution.py:376
  35.1 70.2 %slice-start.1 = ((s8[7077888]{0:T(1024)(128)(4,1)}), s8[4194304]{0:T(1024)(128)(4,1)S(1)}, s32[]{:S(2)}) async-start(s8[7077888]{0:T(1024)(128)(4,1)} %bitcast.10), calls=%async_computation.1 | async-start | bytes 8388608
  35.1 10.4 %collective-permute-start.5 = (bf16[384,512]{1,0:T(8,128)(2,1)S(1)}, bf16[384,512]{1,0:T(8,128)(2,1)S(1)}, u32[]{:S(2)}, u32[]{:S(2)}) collective-permute-start(bf16[384,512]{1,0:T(8,128)(2,1)S(1)} %get-tuple-element.43.refs_0_), channel_id=1, source_target_pairs={{0,12},{4,8},{8,4},{12,0},{1,13},{5,9},{9,5},{13,1},{2,14},{6,10},... | collective-permute-start | bytes 1179656 | tf_op jit(solution)/shard_map/ppermute | solution.py:376
  37.3 10.2 %collective-permute-start.8 = (bf16[128,1536]{1,0:T(8,128)(2,1)S(1)}, bf16[128,1536]{1,0:T(8,128)(2,1)S(1)}, u32[]{:S(2)}, u32[]{:S(2)}) collective-permute-start(bf16[128,1536]{1,0:T(8,128)(2,1)S(1)} %bitcast.15), channel_id=1, source_target_pairs={{0,3},{3,0},{4,7},{7,4},{8,11},{11,8},{12,15},{15,12},{16,19},{19,... | collective-permute-start | bytes 1179656 | tf_op jit(solution)/shard_map/ppermute | solution.py:375
  47.3 4.0 %collective-permute-start.7 = (f32[8,1024]{1,0:T(8,128)S(1)}, f32[8,1024]{1,0:T(8,128)S(1)}, u32[]{:S(2)}, u32[]{:S(2)}) collective-permute-start(f32[8,1024]{1,0:T(8,128)S(1)} %stats.1.refs_4_), channel_id=1, source_target_pairs={{0,4},{4,0},{8,12},{12,8},{1,5},{5,1},{9,13},{13,9},{2,6},{6,2},{1... | collective-permute-start | bytes 98312 | tf_op jit(solution)/shard_map/ppermute | solution.py:379
  47.4 14.5 %collective-permute-start.11 = (bf16[128,1536]{1,0:T(8,128)(2,1)S(1)}, bf16[128,1536]{1,0:T(8,128)(2,1)S(1)}, u32[]{:S(2)}, u32[]{:S(2)}) collective-permute-start(bf16[128,1536]{1,0:T(8,128)(2,1)S(1)} %bitcast.16), channel_id=1, source_target_pairs={{0,2},{1,3},{2,0},{3,1},{4,6},{5,7},{6,4},{7,5},{8,10},{9,11},{10,... | collective-permute-start | bytes 1179656 | tf_op jit(solution)/shard_map/ppermute | solution.py:374
  55.0 8.0 %collective-permute-start.9 = (bf16[384,512]{1,0:T(8,128)(2,1)S(1)}, bf16[384,512]{1,0:T(8,128)(2,1)S(1)}, u32[]{:S(2)}, u32[]{:S(2)}) collective-permute-start(bf16[384,512]{1,0:T(8,128)(2,1)S(1)} %get-tuple-element.47), channel_id=1, source_target_pairs={{0,4},{4,0},{8,12},{12,8},{1,5},{5,1},{9,13},{13,9},{2,6},{6,2},{1... | collective-permute-start | bytes 1179656 | tf_op jit(solution)/shard_map/ppermute | solution.py:381
  55.3 9.1 %collective-permute-start.10 = (bf16[384,512]{1,0:T(8,128)(2,1)S(1)}, bf16[384,512]{1,0:T(8,128)(2,1)S(1)}, u32[]{:S(2)}, u32[]{:S(2)}) collective-permute-start(bf16[384,512]{1,0:T(8,128)(2,1)S(1)} %get-tuple-element.49), channel_id=1, source_target_pairs={{0,12},{4,8},{8,4},{12,0},{1,13},{5,9},{9,5},{13,1},{2,14},{6,10},... | collective-permute-start | bytes 1179656 | tf_op jit(solution)/shard_map/ppermute | solution.py:382
  66.6 2.5 %collective-permute-start.15 = (bf16[6,48,1536]{2,1,0:T(8,128)(2,1)S(1)}, bf16[6,48,1536]{2,1,0:T(8,128)(2,1)S(1)}, u32[]{:S(2)}, u32[]{:S(2)}) collective-permute-start(bf16[6,48,1536]{2,1,0:T(8,128)(2,1)S(1)} %get-tuple-element.59), channel_id=1, source_target_pairs={{0,16},{16,0},{1,17},{17,1},{2,18},{18,2},{3,19},{19,3},{4,20},{20... | collective-permute-start | bytes 2654216 | tf_op jit(solution)/shard_map/ppermute | solution.py:390
  66.7 8.3 %collective-permute-start.12 = (bf16[768,128]{1,0:T(8,128)(2,1)S(1)}, bf16[768,128]{1,0:T(8,128)(2,1)S(1)}, u32[]{:S(2)}, u32[]{:S(2)}) collective-permute-start(bf16[768,128]{1,0:T(8,128)(2,1)S(1)} %get-tuple-element.51), channel_id=1, source_target_pairs={{0,1},{1,0},{2,3},{3,2},{4,5},{5,4},{6,7},{7,6},{8,9},{9,8},{10,11... | collective-permute-start | bytes 589832 | tf_op jit(solution)/shard_map/ppermute | solution.py:386
  70.2 8.4 %collective-permute-start.16 = (bf16[6,48,384]{2,1,0:T(8,128)(2,1)S(1)}, bf16[6,48,384]{2,1,0:T(8,128)(2,1)S(1)}, u32[]{:S(2)}, u32[]{:S(2)}) collective-permute-start(bf16[6,48,384]{2,1,0:T(8,128)(2,1)S(1)} %get-tuple-element.61), channel_id=1, source_target_pairs={{0,4},{4,0},{8,12},{12,8},{1,5},{5,1},{9,13},{13,9},{2,6},{6,2},{1... | collective-permute-start | bytes 663560 | tf_op jit(solution)/shard_map/ppermute | solution.py:367
  71.0 13.2 %collective-permute-start.17 = (bf16[6,48,384]{2,1,0:T(8,128)(2,1)S(1)}, bf16[6,48,384]{2,1,0:T(8,128)(2,1)S(1)}, u32[]{:S(2)}, u32[]{:S(2)}) collective-permute-start(bf16[6,48,384]{2,1,0:T(8,128)(2,1)S(1)} %get-tuple-element.62), channel_id=1, source_target_pairs={{0,8},{4,12},{8,0},{12,4},{1,9},{5,13},{9,1},{13,5},{2,10},{6,14},... | collective-permute-start | bytes 663560 | tf_op jit(solution)/shard_map/ppermute | solution.py:367
  73.9 12.9 %collective-permute-start.18 = (bf16[6,48,384]{2,1,0:T(8,128)(2,1)S(1)}, bf16[6,48,384]{2,1,0:T(8,128)(2,1)S(1)}, u32[]{:S(2)}, u32[]{:S(2)}) collective-permute-start(bf16[6,48,384]{2,1,0:T(8,128)(2,1)S(1)} %get-tuple-element.63), channel_id=1, source_target_pairs={{0,12},{4,8},{8,4},{12,0},{1,13},{5,9},{9,5},{13,1},{2,14},{6,10},... | collective-permute-start | bytes 663560 | tf_op jit(solution)/shard_map/ppermute | solution.py:367
  75.0 30.3 %collective-permute-start.13 = (bf16[768,128]{1,0:T(8,128)(2,1)S(1)}, bf16[768,128]{1,0:T(8,128)(2,1)S(1)}, u32[]{:S(2)}, u32[]{:S(2)}) collective-permute-start(bf16[768,128]{1,0:T(8,128)(2,1)S(1)} %get-tuple-element.54), channel_id=1, source_target_pairs={{0,2},{1,3},{2,0},{3,1},{4,6},{5,7},{6,4},{7,5},{8,10},{9,11},{10,... | collective-permute-start | bytes 589832 | tf_op jit(solution)/shard_map/ppermute | solution.py:388
  76.0 29.2 %collective-permute-start.14 = (bf16[768,128]{1,0:T(8,128)(2,1)S(1)}, bf16[768,128]{1,0:T(8,128)(2,1)S(1)}, u32[]{:S(2)}, u32[]{:S(2)}) collective-permute-start(bf16[768,128]{1,0:T(8,128)(2,1)S(1)} %get-tuple-element.55), channel_id=1, source_target_pairs={{0,3},{1,2},{2,1},{3,0},{4,7},{5,6},{6,5},{7,4},{8,11},{9,10},{10,... | collective-permute-start | bytes 589832 | tf_op jit(solution)/shard_map/ppermute | solution.py:388
  87.6 5.2 %collective-permute-start.19 = (bf16[6,48,96]{2,1,0:T(8,128)(2,1)S(1)}, bf16[6,48,96]{2,1,0:T(8,128)(2,1)S(1)}, u32[]{:S(2)}, u32[]{:S(2)}) collective-permute-start(bf16[6,48,96]{2,1,0:T(8,128)(2,1)S(1)} %get-tuple-element.65), channel_id=1, source_target_pairs={{0,1},{1,0},{2,3},{3,2},{4,5},{5,4},{6,7},{7,6},{8,9},{9,8},{10,11... | collective-permute-start | bytes 165896 | tf_op jit(solution)/shard_map/ppermute | solution.py:367
  87.8 9.8 %collective-permute-start.20 = (bf16[6,48,96]{2,1,0:T(8,128)(2,1)S(1)}, bf16[6,48,96]{2,1,0:T(8,128)(2,1)S(1)}, u32[]{:S(2)}, u32[]{:S(2)}) collective-permute-start(bf16[6,48,96]{2,1,0:T(8,128)(2,1)S(1)} %get-tuple-element.66), channel_id=1, source_target_pairs={{0,2},{1,3},{2,0},{3,1},{4,6},{5,7},{6,4},{7,5},{8,10},{9,11},{10,... | collective-permute-start | bytes 165896 | tf_op jit(solution)/shard_map/ppermute | solution.py:367
  89.8 10.0 %collective-permute-start.21 = (bf16[6,48,96]{2,1,0:T(8,128)(2,1)S(1)}, bf16[6,48,96]{2,1,0:T(8,128)(2,1)S(1)}, u32[]{:S(2)}, u32[]{:S(2)}) collective-permute-start(bf16[6,48,96]{2,1,0:T(8,128)(2,1)S(1)} %get-tuple-element.67), channel_id=1, source_target_pairs={{0,3},{1,2},{2,1},{3,0},{4,7},{5,6},{6,5},{7,4},{8,11},{9,10},{10,... | collective-permute-start | bytes 165896 | tf_op jit(solution)/shard_map/ppermute | solution.py:367
  100.5 8.4 %collective-permute-start.22 = (bf16[6,48,96]{2,1,0:T(8,128)(2,1)S(1)}, bf16[6,48,96]{2,1,0:T(8,128)(2,1)S(1)}, u32[]{:S(2)}, u32[]{:S(2)}) collective-permute-start(bf16[6,48,96]{2,1,0:T(8,128)(2,1)S(1)} %get-tuple-element.69), channel_id=1, source_target_pairs={{0,64},{64,0},{128,192},{192,128},{1,65},{65,1},{129,193},{193,129... | collective-permute-start | bytes 165896 | tf_op jit(solution)/shard_map/ppermute | solution.py:367
  102.0 6.8 %collective-permute-start.23 = (bf16[6,48,96]{2,1,0:T(8,128)(2,1)S(1)}, bf16[6,48,96]{2,1,0:T(8,128)(2,1)S(1)}, u32[]{:S(2)}, u32[]{:S(2)}) collective-permute-start(bf16[6,48,96]{2,1,0:T(8,128)(2,1)S(1)} %get-tuple-element.70), channel_id=1, source_target_pairs={{0,128},{64,192},{128,0},{192,64},{1,129},{65,193},{129,1},{193,65... | collective-permute-start | bytes 165896 | tf_op jit(solution)/shard_map/ppermute | solution.py:367
  104.8 5.6 %collective-permute-start.24 = (bf16[6,48,96]{2,1,0:T(8,128)(2,1)S(1)}, bf16[6,48,96]{2,1,0:T(8,128)(2,1)S(1)}, u32[]{:S(2)}, u32[]{:S(2)}) collective-permute-start(bf16[6,48,96]{2,1,0:T(8,128)(2,1)S(1)} %get-tuple-element.71), channel_id=1, source_target_pairs={{0,192},{64,128},{128,64},{192,0},{1,193},{65,129},{129,65},{193,1... | collective-permute-start | bytes 165896 | tf_op jit(solution)/shard_map/ppermute | solution.py:367
  110.9 8.0 %collective-permute-start.25 = (bf16[3,48,96]{2,1,0:T(8,128)(2,1)S(1)}, bf16[3,48,96]{2,1,0:T(8,128)(2,1)S(1)}, u32[]{:S(2)}, u32[]{:S(2)}) collective-permute-start(bf16[3,48,96]{2,1,0:T(8,128)(2,1)S(1)} %get-tuple-element.74), channel_id=1, source_target_pairs={{0,32},{32,0},{1,33},{33,1},{2,34},{34,2},{3,35},{35,3},{4,36},{36... | collective-permute-start | bytes 82952 | tf_op jit(solution)/shard_map/ppermute | solution.py:411

commit v3 on v2

--- a/solution.py
+++ b/solution.py
@@ -21,7 +21,6 @@
 NN = (((1,), (0,)), ((), ()))
 NT = (((1,), (1,)), ((), ()))
 
-SMEM = pl.BlockSpec(memory_space=pltpu.SMEM)
 VMEM = pl.BlockSpec(memory_space=pltpu.VMEM)
 ANY = pl.BlockSpec(memory_space=pl.ANY)
 HBM = pl.BlockSpec(memory_space=pltpu.HBM)
@@ -29,6 +28,14 @@
 
 def shape(dims, dtype=BF):
     return jax.ShapeDtypeStruct(dims, dtype)
+
+
+class Place:
+    def __getitem__(self, n):
+        return lax.axis_index(("zl", "y", "c", "x", "zh")[n])
+
+
+place = Place()
 
 
 def params(mib=16):
@@ -49,30 +56,21 @@
     return rows * inverse, inverse
 
 
-CUT = 256
-CUTS = 3 * HD // CUT
-
-
-def project_kernel(place, tokens_in, weights_in, grads_in, *rest):
+def project_kernel(tokens_in, weights_in, grads_in, *rest):
     blocks, (tokens, weights, grads, turned, sems) = rest[:4], rest[4:]
     fetches = [pltpu.make_async_copy(tokens_in, tokens, sems.at[0])]
-    for n in range(CUTS):
-        at = slice(n * CUT, (n + 1) * CUT)
-        fetches.append(pltpu.make_async_copy(weights_in.at[:, at], weights.at[n], sems.at[n + 1]))
-    fetches.append(pltpu.make_async_copy(grads_in, grads, sems.at[CUTS + 1]))
+    for j in range(3):
+        at = slice(j * HD, (j + 1) * HD)
+        fetches.append(pltpu.make_async_copy(weights_in.at[:, at], weights.at[j], sems.at[j + 1]))
+    fetches.append(pltpu.make_async_copy(grads_in, grads, sems.at[4]))
     for fetch in fetches:
         fetch.start()
     fetches[0].wait()
     rows = normalise(tokens[...])[0].astype(BF)
-    last = None
-    for n in range(CUTS):
-        fetches[n + 1].wait()
-        part = dot(rows, weights[n])
-        if last is not None:
-            turned[(n - 1) * CUT : n * CUT, :] = flip(last).astype(BF)
-        last = part
-    turned[3 * HD - CUT : 3 * HD, :] = flip(last).astype(BF)
-    fetches[-1].wait()
+    for j in range(3):
+        fetches[j + 1].wait()
+        turned[j * HD : (j + 1) * HD, :] = flip(dot(rows, weights[j])).astype(BF)
+    fetches[4].wait()
     turned[3 * HD :, :] = flip(grads[...]).astype(BF)
     for k in range(4):
         head = place[0] ^ k
@@ -81,21 +79,21 @@
             blocks[k][n * HS : (n + 1) * HS, :] = turned[at, :]
 
 
-def project(place, tokens, weights, grads):
+def project(tokens, weights, grads):
     return pl.pallas_call(
         project_kernel,
-        in_specs=[SMEM, HBM, HBM, HBM],
+        in_specs=[HBM, HBM, HBM],
         out_shape=[shape((4 * HS, ROWS))] * 4,
         scratch_shapes=[
             pltpu.VMEM((ROWS, D), BF),
-            pltpu.VMEM((CUTS, D, CUT), BF),
+            pltpu.VMEM((3, D, HD), BF),
             pltpu.VMEM((ROWS, HD), BF),
             pltpu.VMEM((4 * HD, ROWS), BF),
-            pltpu.SemaphoreType.DMA((CUTS + 2,)),
+            pltpu.SemaphoreType.DMA((5,)),
         ],
-        compiler_params=params(60),
+        compiler_params=pltpu.CompilerParams(vmem_limit_bytes=62_520_000),
         name="project",
-    )(place, tokens, weights, grads)
+    )(tokens, weights, grads)
 
 
 def stack_kernel(*refs):
@@ -209,7 +207,7 @@
     )(*kv_blocks, *qd_blocks, mine, theirs, *after)
 
 
-def gradient_kernel(place, qo_own, qo_got, kv_own, kv_got, *refs):
+def gradient_kernel(qo_own, qo_got, kv_own, kv_got, *refs):
     own, pair, second, middle, ends = refs[:5]
     back, (keep, send, normed, d_proj, cut) = refs[5:9], refs[9:]
     at_end = (place[0] == 0) | (place[0] == 3)
@@ -239,11 +237,11 @@
     send[...] = cut[1 - place[2]]
 
 
-def gradient(place, qo_own, qo_got, kv_own, kv_got, tokens):
+def gradient(qo_own, qo_got, kv_own, kv_got, tokens):
     units = (6, 48, D)
     return pl.pallas_call(
         gradient_kernel,
-        in_specs=[SMEM] + [VMEM] * 9,
+        in_specs=[VMEM] * 9,
         out_shape=[shape((4 * HS, ROWS))] * 4 + [shape(units)] * 2,
         scratch_shapes=[
             pltpu.VMEM((4 * ROWS, D), BF),
@@ -252,13 +250,13 @@
         ],
         compiler_params=params(),
         name="gradient",
-    )(place, qo_own, qo_got, kv_own, kv_got, *tokens)
+    )(qo_own, qo_got, kv_own, kv_got, *tokens)
 
 
 WIDE = 512
 
 
-def tokens_kernel(place, tokens, weights, *refs):
+def tokens_kernel(tokens, weights, *refs):
     blocks, (attended, d_tokens, done, columns, d_normed) = refs[:4], refs[4:]
     done[...] = jnp.zeros_like(done)
     for k in range(4):
@@ -278,10 +276,10 @@
     d_tokens[...] = (inverse * (d_normed[...] - unrounded * (total * (1.0 / D)))).astype(BF)
 
 
-def tokens_of(place, tokens, weights, blocks):
+def tokens_of(tokens, weights, blocks):
     return pl.pallas_call(
         tokens_kernel,
-        in_specs=[SMEM] + [VMEM] * 6,
+        in_specs=[VMEM] * 6,
         out_shape=[shape((ROWS, HD)), shape((ROWS, D)), shape((8, 128), F32)],
         scratch_shapes=[
             pltpu.VMEM((4 * HD, ROWS), BF),
@@ -289,21 +287,21 @@
         ],
         compiler_params=params(20),
         name="d_tokens",
-    )(place, tokens, weights, *blocks)
-
-
-def small(kernel, name, scalars, blocks, outs, scratch, after=()):
+    )(tokens, weights, *blocks)
+
+
+def small(kernel, name, blocks, outs, scratch, after=()):
     return pl.pallas_call(
         kernel,
-        in_specs=[SMEM] * len(scalars) + [VMEM] * (len(blocks) + len(after)),
+        in_specs=[VMEM] * (len(blocks) + len(after)),
         out_shape=outs,
         scratch_shapes=scratch,
         compiler_params=params(),
         name=name,
-    )(*scalars, *blocks, *after)
-
-
-def split_y_kernel(place, mine, got, *refs):
+    )(*blocks, *after)
+
+
+def split_y_kernel(mine, got, *refs):
     outs, cut = refs[:4], refs[4]
     cut[...] = (mine[...].astype(F32) + got[...].astype(F32)).astype(BF)
     for k in range(4):
@@ -311,13 +309,26 @@
         outs[k][...] = cut[:, :, at]
 
 
-def split_z_kernel(place, *refs):
+def ends_high(place):
+    bits = jnp.int32(0)
+    for head in range(HEADS):
+        for core in range(2):
+            units = [u for u in range(48) if u % 16 // 4 == head and u // 3 % 2 == core]
+            value = sum((u // 6 % 2) << n for n, u in enumerate(units))
+            bits = jnp.where((place[0] == head) & (place[2] == core), value, bits)
+    return bits
+
+
+def split_z_kernel(*refs):
     blocks, outs, cut = refs[:4], refs[4:8], refs[8]
     total = sum(block[...].astype(F32) for block in blocks)
     for k in range(4):
         cut[k] = total[:, :, k * 96 : (k + 1) * 96].astype(BF)
-    for k in range(4):
-        outs[k][...] = cut[place[0] ^ k]
+    bits = ends_high(place)
+    for n in range(6):
+        mirror = 3 * (((bits >> n) & 1) ^ place[4])
+        for k in range(4):
+            outs[k][n] = cut[place[0] ^ k ^ mirror, n]
 
 
 def lists():
@@ -332,7 +343,7 @@
     return list(zip(*tables))
 
 
-def split_x_kernel(place, *refs):
+def split_x_kernel(*refs):
     blocks, outs, by_head, cut = refs[:4], refs[4:8], refs[8], refs[9]
     for k in range(4):
         by_head[place[0] ^ k] = blocks[k][...]
@@ -343,14 +354,14 @@
         outs[k][...] = cut[pl.ds((place[3] ^ k) * 6, 6)]
 
 
-def split_zh_kernel(place, *refs):
+def split_zh_kernel(*refs):
     blocks, (keep, send, cut) = refs[:4], refs[-3:]
     cut[...] = sum(block[...].astype(F32) for block in blocks)
     keep[...] = cut[pl.ds(place[4] * 3, 3)]
     send[...] = cut[pl.ds(3 - place[4] * 3, 3)].astype(BF)
 
 
-def finish_kernel(place, mine, got, out):
+def finish_kernel(mine, got, out):
     out[...] = (mine[...] + got[...].astype(F32)).reshape(144, 96)
 
 
@@ -360,7 +371,6 @@
 
 def per_device(tokens, w_proj, d_attended):
     tokens = tokens[0]
-    place = jnp.stack([lax.axis_index(a) for a in ("zl", "y", "c", "x", "zh")]).astype(jnp.int32)
     near, far, swap = exchange(1), exchange(3), [(0, 1), (1, 0)]
 
     def spread(blocks, axis):
@@ -368,7 +378,7 @@
 
     pair = lax.ppermute(tokens, "zl", near)
     middle = lax.ppermute(tokens, "zl", [(1, 2), (2, 1)])
-    heads = spread(project(place, tokens, w_proj, d_attended[0]), "zl")
+    heads = spread(project(tokens, w_proj, d_attended[0]), "zl")
     kv, qd = stack(heads, [pair, middle])
     late = lax.optimization_barrier((tokens, kv))[0]
     second = lax.ppermute(late, "zl", exchange(2))
@@ -382,34 +392,34 @@
     kv_got = lax.ppermute(kv_send, "y", far)
 
     rows = [tokens, pair, second, middle, ends]
-    *back, keep, send = gradient(place, qo_own, qo_got, kv_own, kv_got, rows)
-    returned = [back[0], lax.ppermute(back[1], "zl", near)]
-    later = lax.optimization_barrier((back[2], back[3], returned[1]))
-    returned += [lax.ppermute(later[k - 2], "zl", exchange(k)) for k in (2, 3)]
-    attended, d_tokens, done = tokens_of(place, tokens, w_proj, returned)
+    *back, keep, send = gradient(qo_own, qo_got, kv_own, kv_got, rows)
+    last = lax.ppermute(back[3], "zl", exchange(3))
+    later = lax.optimization_barrier((back[1], back[2], last))
+    returned = [back[0]] + [lax.ppermute(later[k - 1], "zl", exchange(k)) for k in (1, 2)] + [last]
+    attended, d_tokens, done = tokens_of(tokens, w_proj, returned)
     got = lax.ppermute(send, "c", swap)
     blocks = small(
-        split_y_kernel, "split_y", [place], [keep, got],
+        split_y_kernel, "split_y", [keep, got],
         [shape((6, 48, 384))] * 4, [pltpu.VMEM((6, 48, D), BF)],
     )
     blocks = spread(blocks, "y")
     blocks = small(
-        split_z_kernel, "split_z", [place], blocks,
+        split_z_kernel, "split_z", blocks,
         [shape((6, 48, 96))] * 4, [pltpu.VMEM((4, 6, 48, 96), BF)],
     )
     blocks = spread(blocks, "zl")
     blocks = small(
-        split_x_kernel, "split_x", [place], blocks,
+        split_x_kernel, "split_x", blocks,
         [shape((6, 48, 96))] * 4,
         [pltpu.VMEM((4, 6, 48, 96), BF), pltpu.VMEM((24, 48, 96), BF)],
     )
     blocks = spread(blocks, "x")
     keep, send = small(
-        split_zh_kernel, "split_zh", [place], blocks,
+        split_zh_kernel, "split_zh", blocks,
         [shape((3, 48, 96), F32), shape((3, 48, 96))], [pltpu.VMEM((6, 48, 96), F32)], [done],
     )
-    got = lax.ppermute(send, "zh", swap)
-    grad = small(finish_kernel, "finish", [place], [keep, got], shape((144, 96), F32), [])
+    got = lax.ppermute(send, ("zh", "zl"), [(z, 7 - z) for z in range(8)])
+    grad = small(finish_kernel, "finish", [keep, got], shape((144, 96), F32), [])
     return (attended[None], d_tokens[None], grad.T)
 
 

time: 120 us -> 114 us (0.950)
  Pallas kernels: 22.3 us -> 17.2 us
  waiting for transfers between devices: 59.4 us -> 55.3 us
  starting transfers between devices: 36 us -> 39.2 us
    ppermute x12, waiting for transfers between devices: 37 us -> 30.5 us  [spread(): lax.ppermute(blocks[k], axis, exchange(k))]
    pallas_call x8, Pallas kernels: 16.6 us -> 11.6 us  [the longest x1 5.09 us: project(): pl.pallas_call(project_kernel, in_specs=[HBM, HBM, HBM], out_shape=[shape...]
    ppermute x4, waiting for transfers between devices: 2.15 us -> 5.91 us  [the longest x1 3.96 us: per_device(): last = lax.ppermute(back[3], 'zl', exchange(3))]
    ppermute x4, starting transfers between devices: 7.86 us -> 10.9 us  [the longest x1 5.67 us: per_device(): got = lax.ppermute(send, ('zh', 'zl'), [(z, 7 - z) for z in range(8)])]
    ppermute x1, waiting for transfers between devices: 2.08 us -> 0.39 us  [per_device(): got = lax.ppermute(send, 'c', swap)]
  transfers between devices with their start and end apart: 26 -> 26, of which waited for: 18 -> 17; matrix products, arithmetic and copies ran while one was open for 1% -> 0% of each run, Pallas kernels for 15% -> 13%
where the time goes in v3:
time: 114 us; the launch traced here: 113 us
  waiting for transfers between devices  55.3 us (49%)
  starting transfers between devices  39.2 us (34%)
  Pallas kernels  17.2 us (15%)
    ppermute x12, waiting for transfers between devices, spread(): lax.ppermute(blocks[k], axis, exchange(k))  30.5 us
    ppermute x12, starting transfers between devices, spread(): lax.ppermute(blocks[k], axis, exchange(k))  16.9 us
    ppermute x1, starting transfers between devices, per_device(): got = lax.ppermute(send, ('zh', 'zl'), [(z, 7 - z) for z in range(8)])  5.67 us
    ppermute x1, waiting for transfers between devices, per_device(): second = lax.ppermute(late, 'zl', exchange(2))  5.38 us
    ppermute x1, waiting for transfers between devices, per_device(): lax.ppermute(qd, 'y', near)  5.33 us
    pallas_call x1, Pallas kernels, project(): pl.pallas_call(project_kernel, in_specs=[HBM, HBM, HBM], out_shape=[shape...  5.09 us
    ppermute x1, waiting for transfers between devices, per_device(): last = lax.ppermute(back[3], 'zl', exchange(3))  3.96 us
    ppermute x1, starting transfers between devices, per_device(): middle = lax.ppermute(tokens, 'zl', [(1, 2), (2, 1)])  3.96 us
  transfers between devices with their start and end apart: 26, of which 17 were waited for; matrix products, arithmetic and copies ran while one was open for 0% of the time, Pallas kernels for 13%

profile of v3, /device:TPU:32, one launch (start us, length us, event | category | flops | bytes accessed | tf_op | source)
XLA Modules:
  0.0 113.5 jit_solution(17795429798085043286)
XLA Ops:
  0.6 4.0 %collective-permute-start.4 = (bf16[128,1536]{1,0:T(8,128)(2,1)}, bf16[128,1536]{1,0:T(8,128)(2,1)S(1)}, u32[]{:S(2)}, u32[]{:S(2)}) collective-permute-start(bf16[128,1536]{1,0:T(8,128)(2,1)} %bitcast.7), channel_id=1, source_target_pairs={{1,2},{2,1},{5,6},{6,5},{9,10},{10,9},{13,14},{14,13},{17,18},{18,... | collective-permute-start | bytes 1179656 | tf_op jit(solution)/shard_map/ppermute | solution.py:380
  4.6 0.1 collective-permute-start.3
  4.7 0.0 slice-start
  4.7 5.1 %project.1 = (bf16[768,128]{1,0:T(8,128)(2,1)}, bf16[768,128]{1,0:T(8,128)(2,1)}, bf16[768,128]{1,0:T(8,128)(2,1)}, bf16[768,128]{1,0:T(8,128)(2,1)}) custom-call(bf16[128,1536]{1,0:T(8,128)(2,1)} %bitcast.9, bf16[1536,2304]{1,0:T(8,128)(2,1)} %weights.1, bf16[128,768]{1,0:T(8,128)(2,1)} %bitcast.14), custom_call_target="tpu_custom_call" | custom-call | tf_op jit(solution)/shard_map/project/pallas_call | solution.py:83
  9.8 2.1 %collective-permute-start = (bf16[768,128]{1,0:T(8,128)(2,1)}, bf16[768,128]{1,0:T(8,128)(2,1)S(1)}, u32[]{:S(2)}, u32[]{:S(2)}) collective-permute-start(bf16[768,128]{1,0:T(8,128)(2,1)} %get-tuple-element.40), channel_id=1, source_target_pairs={{0,1},{1,0},{2,3},{3,2},{4,5},{5,4},{6,7},{7,6},{8,9},{9,8},{10,11... | collective-permute-start | bytes 589832 | tf_op jit(solution)/shard_map/ppermute | solution.py:377
  11.9 0.1 collective-permute-start.1
  12.0 1.4 %collective-permute-start.2 = (bf16[768,128]{1,0:T(8,128)(2,1)}, bf16[768,128]{1,0:T(8,128)(2,1)S(1)}, u32[]{:S(2)}, u32[]{:S(2)}) collective-permute-start(bf16[768,128]{1,0:T(8,128)(2,1)} %get-tuple-element.42), channel_id=1, source_target_pairs={{0,3},{1,2},{2,1},{3,0},{4,7},{5,6},{6,5},{7,4},{8,11},{9,10},{10,... | collective-permute-start | bytes 589832 | tf_op jit(solution)/shard_map/ppermute | solution.py:377
  13.5 8.4 %collective-permute-done.refs_1_ = bf16[768,128]{1,0:T(8,128)(2,1)S(1)} collective-permute-done((bf16[768,128]{1,0:T(8,128)(2,1)}, bf16[768,128]{1,0:T(8,128)(2,1)S(1)}, u32[]{:S(2)}, u32[]{:S(2)}) %collective-permute-start) | collective-permute-done | bytes 196640 | tf_op jit(solution)/shard_map/ppermute | solution.py:377
  21.9 3.1 %collective-permute-done.1.refs_2_ = bf16[768,128]{1,0:T(8,128)(2,1)S(1)} collective-permute-done((bf16[768,128]{1,0:T(8,128)(2,1)}, bf16[768,128]{1,0:T(8,128)(2,1)S(1)}, u32[]{:S(2)}, u32[]{:S(2)}) %collective-permute-start.1) | collective-permute-done | bytes 196640 | tf_op jit(solution)/shard_map/ppermute | solution.py:377
  25.0 5.8 %collective-permute-done.2.refs_3_ = bf16[768,128]{1,0:T(8,128)(2,1)S(1)} collective-permute-done((bf16[768,128]{1,0:T(8,128)(2,1)}, bf16[768,128]{1,0:T(8,128)(2,1)S(1)}, u32[]{:S(2)}, u32[]{:S(2)}) %collective-permute-start.2) | collective-permute-done | bytes 196640 | tf_op jit(solution)/shard_map/ppermute | solution.py:377
  30.8 0.0 collective-permute-done.4.refs_5_.refs_3_
  30.8 0.0 collective-permute-done.3.refs_4_.refs_1_
  30.8 0.9 copy-done.1
  31.7 0.1 stack.1
  31.9 1.7 %collective-permute-start.6 = (bf16[384,512]{1,0:T(8,128)(2,1)S(1)}, bf16[384,512]{1,0:T(8,128)(2,1)S(1)}, u32[]{:S(2)}, u32[]{:S(2)}) collective-permute-start(bf16[384,512]{1,0:T(8,128)(2,1)S(1)} %get-tuple-element.44.refs_2_), channel_id=1, source_target_pairs={{0,4},{4,0},{8,12},{12,8},{1,5},{5,1},{9,13},{13,9},{2,6},{6,2},{1... | collective-permute-start | bytes 1179656 | tf_op jit(solution)/shard_map/ppermute | solution.py:386
  33.6 2.2 %collective-permute-start.5 = (bf16[384,512]{1,0:T(8,128)(2,1)S(1)}, bf16[384,512]{1,0:T(8,128)(2,1)S(1)}, u32[]{:S(2)}, u32[]{:S(2)}) collective-permute-start(bf16[384,512]{1,0:T(8,128)(2,1)S(1)} %get-tuple-element.43.refs_0_), channel_id=1, source_target_pairs={{0,12},{4,8},{8,4},{12,0},{1,13},{5,9},{9,5},{13,1},{2,14},{6,10},... | collective-permute-start | bytes 1179656 | tf_op jit(solution)/shard_map/ppermute | solution.py:386
  35.7 0.7 collective-permute-start.8
  36.4 5.3 %collective-permute-done.6.refs_3_ = bf16[384,512]{1,0:T(8,128)(2,1)S(1)} collective-permute-done((bf16[384,512]{1,0:T(8,128)(2,1)S(1)}, bf16[384,512]{1,0:T(8,128)(2,1)S(1)}, u32[]{:S(2)}, u32[]{:S(2)}) %collective-permute-start.6) | collective-permute-done | bytes 393248 | tf_op jit(solution)/shard_map/ppermute | solution.py:386
  41.7 2.5 %collective-permute-done.5.refs_1_ = bf16[384,512]{1,0:T(8,128)(2,1)S(1)} collective-permute-done((bf16[384,512]{1,0:T(8,128)(2,1)S(1)}, bf16[384,512]{1,0:T(8,128)(2,1)S(1)}, u32[]{:S(2)}, u32[]{:S(2)}) %collective-permute-start.5) | collective-permute-done | bytes 393248 | tf_op jit(solution)/shard_map/ppermute | solution.py:386
  44.3 1.9 %stats.1.refs_4_ = f32[8,1024]{1,0:T(8,128)S(1)} custom-call(bf16[384,512]{1,0:T(8,128)(2,1)S(1)} %get-tuple-element.43.refs_0_, bf16[384,512]{1,0:T(8,128)(2,1)S(1)} %collective-permute-done.5.refs_1_, bf16[384,512]{1,0:T(8,128)(2,1)S(1)} %get-tuple-element.44.refs_2_, bf16[384,512]{1,0:T(8,128)(2,1)S(1)} %collective-permute-done.6.refs_3_), custom_call_target="tpu_custom_call" | custom-call | tf_op jit(solution)/shard_map/stats/pallas_call | solution.py:145
  46.1 0.1 collective-permute-start.7
  46.2 0.1 collective-permute-start.11
  46.3 0.0 collective-permute-done.8.refs_6_.refs_4_
  46.3 3.8 %collective-permute-done.7.refs_5_ = f32[8,1024]{1,0:T(8,128)S(1)} collective-permute-done((f32[8,1024]{1,0:T(8,128)S(1)}, f32[8,1024]{1,0:T(8,128)S(1)}, u32[]{:S(2)}, u32[]{:S(2)}) %collective-permute-start.7) | collective-permute-done | bytes 32800 | tf_op jit(solution)/shard_map/ppermute | solution.py:389
  50.1 3.6 %attend.1 = (f32[384,512]{1,0:T(8,128)S(1)}, bf16[384,512]{1,0:T(8,128)(2,1)S(1)}, f32[384,512]{1,0:T(8,128)S(1)}, bf16[384,512]{1,0:T(8,128)(2,1)S(1)}) custom-call(bf16[384,512]{1,0:T(8,128)(2,1)S(1)} %get-tuple-element.43.refs_0_, bf16[384,512]{1,0:T(8,128)(2,1)S(1)} %collective-permute-done.5.refs_1_, bf16[384,512]{1,0:T(8,128)(2,1)S(1)} %get-tuple-element.44.refs_2_, ...), custom_call_target="tpu_custom_call" | custom-call | tf_op jit(solution)/shard_map/attend/pallas_call | solution.py:200
  53.8 0.1 collective-permute-start.9
  53.9 2.4 %collective-permute-start.10 = (bf16[384,512]{1,0:T(8,128)(2,1)S(1)}, bf16[384,512]{1,0:T(8,128)(2,1)S(1)}, u32[]{:S(2)}, u32[]{:S(2)}) collective-permute-start(bf16[384,512]{1,0:T(8,128)(2,1)S(1)} %get-tuple-element.49), channel_id=1, source_target_pairs={{0,12},{4,8},{8,4},{12,0},{1,13},{5,9},{9,5},{13,1},{2,14},{6,10},... | collective-permute-start | bytes 1179656 | tf_op jit(solution)/shard_map/ppermute | solution.py:392
  56.3 5.4 %collective-permute-done.11.refs_2_ = bf16[128,1536]{1,0:T(8,128)(2,1)S(1)} collective-permute-done((bf16[128,1536]{1,0:T(8,128)(2,1)S(1)}, bf16[128,1536]{1,0:T(8,128)(2,1)S(1)}, u32[]{:S(2)}, u32[]{:S(2)}) %collective-permute-start.11) | collective-permute-done | bytes 393248 | tf_op jit(solution)/shard_map/ppermute | solution.py:384
  61.7 1.4 %collective-permute-done.10.kv_got = bf16[384,512]{1,0:T(8,128)(2,1)S(1)} collective-permute-done((bf16[384,512]{1,0:T(8,128)(2,1)S(1)}, bf16[384,512]{1,0:T(8,128)(2,1)S(1)}, u32[]{:S(2)}, u32[]{:S(2)}) %collective-permute-start.10) | collective-permute-done | bytes 393248 | tf_op jit(solution)/shard_map/ppermute | solution.py:392
  63.1 1.7 %gradient.1 = (bf16[768,128]{1,0:T(8,128)(2,1)S(1)}, bf16[768,128]{1,0:T(8,128)(2,1)S(1)}, bf16[768,128]{1,0:T(8,128)(2,1)S(1)}, bf16[768,128]{1,0:T(8,128)(2,1)...) custom-call(f32[384,512]{1,0:T(8,128)S(1)} %get-tuple-element.46.qo_own, ...), custom_call_target="tpu_custom_call" | custom-call | tf_op jit(solution)/shard_map/gradient/pallas_call | solution.py:242
  64.9 0.1 collective-permute-start.15
  65.0 2.0 %collective-permute-start.12 = (bf16[768,128]{1,0:T(8,128)(2,1)S(1)}, bf16[768,128]{1,0:T(8,128)(2,1)S(1)}, u32[]{:S(2)}, u32[]{:S(2)}) collective-permute-start(bf16[768,128]{1,0:T(8,128)(2,1)S(1)} %get-tuple-element.53), channel_id=1, source_target_pairs={{0,3},{1,2},{2,1},{3,0},{4,7},{5,6},{6,5},{7,4},{8,11},{9,10},{10,... | collective-permute-start | bytes 589832 | tf_op jit(solution)/shard_map/ppermute | solution.py:396
  67.0 0.4 collective-permute-done.15.got
  67.4 0.5 split_y.1
  68.0 0.6 collective-permute-start.16
  68.6 3.1 %collective-permute-start.17 = (bf16[6,48,384]{2,1,0:T(8,128)(2,1)S(1)}, bf16[6,48,384]{2,1,0:T(8,128)(2,1)S(1)}, u32[]{:S(2)}, u32[]{:S(2)}) collective-permute-start(bf16[6,48,384]{2,1,0:T(8,128)(2,1)S(1)} %get-tuple-element.62), channel_id=1, source_target_pairs={{0,8},{4,12},{8,0},{12,4},{1,9},{5,13},{9,1},{13,5},{2,10},{6,14},... | collective-permute-start | bytes 663560 | tf_op jit(solution)/shard_map/ppermute | solution.py:377
  71.7 1.1 collective-permute-start.18
  72.7 4.0 %collective-permute-done.12.refs_3_ = bf16[768,128]{1,0:T(8,128)(2,1)S(1)} collective-permute-done((bf16[768,128]{1,0:T(8,128)(2,1)S(1)}, bf16[768,128]{1,0:T(8,128)(2,1)S(1)}, u32[]{:S(2)}, u32[]{:S(2)}) %collective-permute-start.12) | collective-permute-done | bytes 196640 | tf_op jit(solution)/shard_map/ppermute | solution.py:396
  76.7 0.0 collective-permute-start.13
  76.7 3.2 %collective-permute-start.14 = (bf16[768,128]{1,0:T(8,128)(2,1)S(1)}, bf16[768,128]{1,0:T(8,128)(2,1)S(1)}, u32[]{:S(2)}, u32[]{:S(2)}) collective-permute-start(bf16[768,128]{1,0:T(8,128)(2,1)S(1)} %get-tuple-element.55), channel_id=1, source_target_pairs={{0,2},{1,3},{2,0},{3,1},{4,6},{5,7},{6,4},{7,5},{8,10},{9,11},{10,... | collective-permute-start | bytes 589832 | tf_op jit(solution)/shard_map/ppermute | solution.py:398
  79.9 0.0 collective-permute-done.16.refs_1_
  79.9 2.0 %collective-permute-done.17.refs_2_ = bf16[6,48,384]{2,1,0:T(8,128)(2,1)S(1)} collective-permute-done((bf16[6,48,384]{2,1,0:T(8,128)(2,1)S(1)}, bf16[6,48,384]{2,1,0:T(8,128)(2,1)S(1)}, u32[]{:S(2)}, u32[]{:S(2)}) %collective-permute-start.17) | collective-permute-done | bytes 221216 | tf_op jit(solution)/shard_map/ppermute | solution.py:377
  82.0 2.6 %collective-permute-done.18.refs_3_ = bf16[6,48,384]{2,1,0:T(8,128)(2,1)S(1)} collective-permute-done((bf16[6,48,384]{2,1,0:T(8,128)(2,1)S(1)}, bf16[6,48,384]{2,1,0:T(8,128)(2,1)S(1)}, u32[]{:S(2)}, u32[]{:S(2)}) %collective-permute-start.18) | collective-permute-done | bytes 221216 | tf_op jit(solution)/shard_map/ppermute | solution.py:377
  84.5 0.3 split_z.1
  84.8 2.1 %collective-permute-start.19 = (bf16[6,48,96]{2,1,0:T(8,128)(2,1)S(1)}, bf16[6,48,96]{2,1,0:T(8,128)(2,1)S(1)}, u32[]{:S(2)}, u32[]{:S(2)}) collective-permute-start(bf16[6,48,96]{2,1,0:T(8,128)(2,1)S(1)} %get-tuple-element.65), channel_id=1, source_target_pairs={{0,1},{1,0},{2,3},{3,2},{4,5},{5,4},{6,7},{7,6},{8,9},{9,8},{10,11... | collective-permute-start | bytes 165896 | tf_op jit(solution)/shard_map/ppermute | solution.py:377
  87.0 1.3 %collective-permute-start.20 = (bf16[6,48,96]{2,1,0:T(8,128)(2,1)S(1)}, bf16[6,48,96]{2,1,0:T(8,128)(2,1)S(1)}, u32[]{:S(2)}, u32[]{:S(2)}) collective-permute-start(bf16[6,48,96]{2,1,0:T(8,128)(2,1)S(1)} %get-tuple-element.66), channel_id=1, source_target_pairs={{0,2},{1,3},{2,0},{3,1},{4,6},{5,7},{6,4},{7,5},{8,10},{9,11},{10,... | collective-permute-start | bytes 165896 | tf_op jit(solution)/shard_map/ppermute | solution.py:377
  88.3 0.2 collective-permute-start.21
  88.5 1.4 %collective-permute-done.19.refs_1_ = bf16[6,48,96]{2,1,0:T(8,128)(2,1)S(1)} collective-permute-done((bf16[6,48,96]{2,1,0:T(8,128)(2,1)S(1)}, bf16[6,48,96]{2,1,0:T(8,128)(2,1)S(1)}, u32[]{:S(2)}, u32[]{:S(2)}) %collective-permute-start.19) | collective-permute-done | bytes 55328 | tf_op jit(solution)/shard_map/ppermute | solution.py:377
  90.0 3.1 %collective-permute-done.20.refs_2_ = bf16[6,48,96]{2,1,0:T(8,128)(2,1)S(1)} collective-permute-done((bf16[6,48,96]{2,1,0:T(8,128)(2,1)S(1)}, bf16[6,48,96]{2,1,0:T(8,128)(2,1)S(1)}, u32[]{:S(2)}, u32[]{:S(2)}) %collective-permute-start.20) | collective-permute-done | bytes 55328 | tf_op jit(solution)/shard_map/ppermute | solution.py:377
  93.0 2.1 %collective-permute-done.21.refs_3_ = bf16[6,48,96]{2,1,0:T(8,128)(2,1)S(1)} collective-permute-done((bf16[6,48,96]{2,1,0:T(8,128)(2,1)S(1)}, bf16[6,48,96]{2,1,0:T(8,128)(2,1)S(1)}, u32[]{:S(2)}, u32[]{:S(2)}) %collective-permute-start.21) | collective-permute-done | bytes 55328 | tf_op jit(solution)/shard_map/ppermute | solution.py:377
  95.1 0.2 split_x.1
  95.3 1.6 %collective-permute-start.22 = (bf16[6,48,96]{2,1,0:T(8,128)(2,1)S(1)}, bf16[6,48,96]{2,1,0:T(8,128)(2,1)S(1)}, u32[]{:S(2)}, u32[]{:S(2)}) collective-permute-start(bf16[6,48,96]{2,1,0:T(8,128)(2,1)S(1)} %get-tuple-element.69), channel_id=1, source_target_pairs={{0,64},{64,0},{128,192},{192,128},{1,65},{65,1},{129,193},{193,129... | collective-permute-start | bytes 165896 | tf_op jit(solution)/shard_map/ppermute | solution.py:377
  96.9 2.7 %collective-permute-start.23 = (bf16[6,48,96]{2,1,0:T(8,128)(2,1)S(1)}, bf16[6,48,96]{2,1,0:T(8,128)(2,1)S(1)}, u32[]{:S(2)}, u32[]{:S(2)}) collective-permute-start(bf16[6,48,96]{2,1,0:T(8,128)(2,1)S(1)} %get-tuple-element.70), channel_id=1, source_target_pairs={{0,128},{64,192},{128,0},{192,64},{1,129},{65,193},{129,1},{193,65... | collective-permute-start | bytes 165896 | tf_op jit(solution)/shard_map/ppermute | solution.py:377
  99.6 0.5 collective-permute-start.24
  100.1 0.0 collective-permute-done.13.refs_1_
  100.1 0.0 collective-permute-done.14.refs_2_
  100.1 3.1 %d_tokens.1 = (bf16[128,768]{1,0:T(8,128)(2,1)}, bf16[128,1536]{1,0:T(8,128)(2,1)}, f32[8,128]{1,0:T(8,128)S(1)}) custom-call(bf16[128,1536]{1,0:T(8,128)(2,1)S(1)} %bitcast.13, bf16[1536,2304]{1,0:T(8,128)(2,1)S(1)} %bitcast.6, bf16[768,128]{1,0:T(8,128)(2,1)S(1)} %get-tuple-element.50.refs_0_, bf16[768,128]{1,0:T(8,128)(2,1)S(1)} %collective-permute-done.13.refs_1_, ...), custom_call_target="tpu_custom_call" | custom-call | tf_op jit(solution)/shard_map/d_tokens/pallas_call | solution.py:280
  103.2 0.0 collective-permute-done.22.refs_1_
  103.2 0.0 collective-permute-done.23.refs_2_
  103.2 2.0 %collective-permute-done.24.refs_3_ = bf16[6,48,96]{2,1,0:T(8,128)(2,1)S(1)} collective-permute-done((bf16[6,48,96]{2,1,0:T(8,128)(2,1)S(1)}, bf16[6,48,96]{2,1,0:T(8,128)(2,1)S(1)}, u32[]{:S(2)}, u32[]{:S(2)}) %collective-permute-start.24) | collective-permute-done | bytes 55328 | tf_op jit(solution)/shard_map/ppermute | solution.py:377
  105.2 0.1 split_zh.1
  105.2 5.7 %collective-permute-start.25 = (bf16[3,48,96]{2,1,0:T(8,128)(2,1)S(1)}, bf16[3,48,96]{2,1,0:T(8,128)(2,1)S(1)}, u32[]{:S(2)}, u32[]{:S(2)}) collective-permute-start(bf16[3,48,96]{2,1,0:T(8,128)(2,1)S(1)} %get-tuple-element.74), channel_id=1, source_target_pairs={{0,35},{1,34},{2,33},{3,32},{32,3},{33,2},{34,1},{35,0},{4,39},{5,... | collective-permute-start | bytes 82952 | tf_op jit(solution)/shard_map/ppermute | solution.py:421
  110.9 1.9 %collective-permute-done.25.got = bf16[3,48,96]{2,1,0:T(8,128)(2,1)S(1)} collective-permute-done((bf16[3,48,96]{2,1,0:T(8,128)(2,1)S(1)}, bf16[3,48,96]{2,1,0:T(8,128)(2,1)S(1)}, u32[]{:S(2)}, u32[]{:S(2)}) %collective-permute-start.25) | collective-permute-done | bytes 27680 | tf_op jit(solution)/shard_map/ppermute | solution.py:421
  112.8 0.6 finish.1
  (8 shorter events, 0.0 us)
Async XLA Ops:
  0.6 35.1 %copy-start = (bf16[1,128,1536]{2,1,0:T(8,128)(2,1)S(1)}, bf16[1,128,1536]{2,1,0:T(8,128)(2,1)}, u32[]{:S(2)}) copy-start(bf16[1,128,1536]{2,1,0:T(8,128)(2,1)} %param.3) | copy-start | bytes 1179652
  0.6 30.2 %collective-permute-start.4 = (bf16[128,1536]{1,0:T(8,128)(2,1)}, bf16[128,1536]{1,0:T(8,128)(2,1)S(1)}, u32[]{:S(2)}, u32[]{:S(2)}) collective-permute-start(bf16[128,1536]{1,0:T(8,128)(2,1)} %bitcast.7), channel_id=1, source_target_pairs={{1,2},{2,1},{5,6},{6,5},{9,10},{10,9},{13,14},{14,13},{17,18},{18,... | collective-permute-start | bytes 1179656 | tf_op jit(solution)/shard_map/ppermute | solution.py:380
  4.6 26.2 %collective-permute-start.3 = (bf16[128,1536]{1,0:T(8,128)(2,1)}, bf16[128,1536]{1,0:T(8,128)(2,1)S(1)}, u32[]{:S(2)}, u32[]{:S(2)}) collective-permute-start(bf16[128,1536]{1,0:T(8,128)(2,1)} %bitcast.8), channel_id=1, source_target_pairs={{0,1},{1,0},{2,3},{3,2},{4,5},{5,4},{6,7},{7,6},{8,9},{9,8},{10,11... | collective-permute-start | bytes 1179656 | tf_op jit(solution)/shard_map/ppermute | solution.py:379
  4.7 95.4 %slice-start = ((s8[7077888]{0:T(1024)(128)(4,1)}), s8[2883584]{0:T(1024)(128)(4,1)S(1)}, s32[]{:S(2)}) async-start(s8[7077888]{0:T(1024)(128)(4,1)} %bitcast.5), calls=%async_computation | async-start | bytes 5767168
  9.8 12.1 %collective-permute-start = (bf16[768,128]{1,0:T(8,128)(2,1)}, bf16[768,128]{1,0:T(8,128)(2,1)S(1)}, u32[]{:S(2)}, u32[]{:S(2)}) collective-permute-start(bf16[768,128]{1,0:T(8,128)(2,1)} %get-tuple-element.40), channel_id=1, source_target_pairs={{0,1},{1,0},{2,3},{3,2},{4,5},{5,4},{6,7},{7,6},{8,9},{9,8},{10,11... | collective-permute-start | bytes 589832 | tf_op jit(solution)/shard_map/ppermute | solution.py:377
  11.9 13.1 %collective-permute-start.1 = (bf16[768,128]{1,0:T(8,128)(2,1)}, bf16[768,128]{1,0:T(8,128)(2,1)S(1)}, u32[]{:S(2)}, u32[]{:S(2)}) collective-permute-start(bf16[768,128]{1,0:T(8,128)(2,1)} %get-tuple-element.41), channel_id=1, source_target_pairs={{0,2},{1,3},{2,0},{3,1},{4,6},{5,7},{6,4},{7,5},{8,10},{9,11},{10,... | collective-permute-start | bytes 589832 | tf_op jit(solution)/shard_map/ppermute | solution.py:377
  12.0 18.8 %collective-permute-start.2 = (bf16[768,128]{1,0:T(8,128)(2,1)}, bf16[768,128]{1,0:T(8,128)(2,1)S(1)}, u32[]{:S(2)}, u32[]{:S(2)}) collective-permute-start(bf16[768,128]{1,0:T(8,128)(2,1)} %get-tuple-element.42), channel_id=1, source_target_pairs={{0,3},{1,2},{2,1},{3,0},{4,7},{5,6},{6,5},{7,4},{8,11},{9,10},{10,... | collective-permute-start | bytes 589832 | tf_op jit(solution)/shard_map/ppermute | solution.py:377
  30.8 0.9 copy-start.1
  31.9 9.9 %collective-permute-start.6 = (bf16[384,512]{1,0:T(8,128)(2,1)S(1)}, bf16[384,512]{1,0:T(8,128)(2,1)S(1)}, u32[]{:S(2)}, u32[]{:S(2)}) collective-permute-start(bf16[384,512]{1,0:T(8,128)(2,1)S(1)} %get-tuple-element.44.refs_2_), channel_id=1, source_target_pairs={{0,4},{4,0},{8,12},{12,8},{1,5},{5,1},{9,13},{13,9},{2,6},{6,2},{1... | collective-permute-start | bytes 1179656 | tf_op jit(solution)/shard_map/ppermute | solution.py:386
  33.6 66.5 %slice-start.1 = ((s8[7077888]{0:T(1024)(128)(4,1)}), s8[4194304]{0:T(1024)(128)(4,1)S(1)}, s32[]{:S(2)}) async-start(s8[7077888]{0:T(1024)(128)(4,1)} %bitcast.5), calls=%async_computation.1 | async-start | bytes 8388608
  33.6 10.7 %collective-permute-start.5 = (bf16[384,512]{1,0:T(8,128)(2,1)S(1)}, bf16[384,512]{1,0:T(8,128)(2,1)S(1)}, u32[]{:S(2)}, u32[]{:S(2)}) collective-permute-start(bf16[384,512]{1,0:T(8,128)(2,1)S(1)} %get-tuple-element.43.refs_0_), channel_id=1, source_target_pairs={{0,12},{4,8},{8,4},{12,0},{1,13},{5,9},{9,5},{13,1},{2,14},{6,10},... | collective-permute-start | bytes 1179656 | tf_op jit(solution)/shard_map/ppermute | solution.py:386
  35.7 10.6 %collective-permute-start.8 = (bf16[128,1536]{1,0:T(8,128)(2,1)S(1)}, bf16[128,1536]{1,0:T(8,128)(2,1)S(1)}, u32[]{:S(2)}, u32[]{:S(2)}) collective-permute-start(bf16[128,1536]{1,0:T(8,128)(2,1)S(1)} %bitcast.10), channel_id=1, source_target_pairs={{0,3},{3,0},{4,7},{7,4},{8,11},{11,8},{12,15},{15,12},{16,19},{19,... | collective-permute-start | bytes 1179656 | tf_op jit(solution)/shard_map/ppermute | solution.py:385
  46.1 4.0 %collective-permute-start.7 = (f32[8,1024]{1,0:T(8,128)S(1)}, f32[8,1024]{1,0:T(8,128)S(1)}, u32[]{:S(2)}, u32[]{:S(2)}) collective-permute-start(f32[8,1024]{1,0:T(8,128)S(1)} %stats.1.refs_4_), channel_id=1, source_target_pairs={{0,4},{4,0},{8,12},{12,8},{1,5},{5,1},{9,13},{13,9},{2,6},{6,2},{1... | collective-permute-start | bytes 98312 | tf_op jit(solution)/shard_map/ppermute | solution.py:389
  46.2 15.5 %collective-permute-start.11 = (bf16[128,1536]{1,0:T(8,128)(2,1)S(1)}, bf16[128,1536]{1,0:T(8,128)(2,1)S(1)}, u32[]{:S(2)}, u32[]{:S(2)}) collective-permute-start(bf16[128,1536]{1,0:T(8,128)(2,1)S(1)} %bitcast.11), channel_id=1, source_target_pairs={{0,2},{1,3},{2,0},{3,1},{4,6},{5,7},{6,4},{7,5},{8,10},{9,11},{10,... | collective-permute-start | bytes 1179656 | tf_op jit(solution)/shard_map/ppermute | solution.py:384
  53.8 7.9 %collective-permute-start.9 = (bf16[384,512]{1,0:T(8,128)(2,1)S(1)}, bf16[384,512]{1,0:T(8,128)(2,1)S(1)}, u32[]{:S(2)}, u32[]{:S(2)}) collective-permute-start(bf16[384,512]{1,0:T(8,128)(2,1)S(1)} %get-tuple-element.47), channel_id=1, source_target_pairs={{0,4},{4,0},{8,12},{12,8},{1,5},{5,1},{9,13},{13,9},{2,6},{6,2},{1... | collective-permute-start | bytes 1179656 | tf_op jit(solution)/shard_map/ppermute | solution.py:391
  53.9 9.3 %collective-permute-start.10 = (bf16[384,512]{1,0:T(8,128)(2,1)S(1)}, bf16[384,512]{1,0:T(8,128)(2,1)S(1)}, u32[]{:S(2)}, u32[]{:S(2)}) collective-permute-start(bf16[384,512]{1,0:T(8,128)(2,1)S(1)} %get-tuple-element.49), channel_id=1, source_target_pairs={{0,12},{4,8},{8,4},{12,0},{1,13},{5,9},{9,5},{13,1},{2,14},{6,10},... | collective-permute-start | bytes 1179656 | tf_op jit(solution)/shard_map/ppermute | solution.py:392
  64.9 2.5 %collective-permute-start.15 = (bf16[6,48,1536]{2,1,0:T(8,128)(2,1)S(1)}, bf16[6,48,1536]{2,1,0:T(8,128)(2,1)S(1)}, u32[]{:S(2)}, u32[]{:S(2)}) collective-permute-start(bf16[6,48,1536]{2,1,0:T(8,128)(2,1)S(1)} %get-tuple-element.59), channel_id=1, source_target_pairs={{0,16},{16,0},{1,17},{17,1},{2,18},{18,2},{3,19},{19,3},{4,20},{20... | collective-permute-start | bytes 2654216 | tf_op jit(solution)/shard_map/ppermute | solution.py:400
  65.0 11.7 %collective-permute-start.12 = (bf16[768,128]{1,0:T(8,128)(2,1)S(1)}, bf16[768,128]{1,0:T(8,128)(2,1)S(1)}, u32[]{:S(2)}, u32[]{:S(2)}) collective-permute-start(bf16[768,128]{1,0:T(8,128)(2,1)S(1)} %get-tuple-element.53), channel_id=1, source_target_pairs={{0,3},{1,2},{2,1},{3,0},{4,7},{5,6},{6,5},{7,4},{8,11},{9,10},{10,... | collective-permute-start | bytes 589832 | tf_op jit(solution)/shard_map/ppermute | solution.py:396
  68.0 12.0 %collective-permute-start.16 = (bf16[6,48,384]{2,1,0:T(8,128)(2,1)S(1)}, bf16[6,48,384]{2,1,0:T(8,128)(2,1)S(1)}, u32[]{:S(2)}, u32[]{:S(2)}) collective-permute-start(bf16[6,48,384]{2,1,0:T(8,128)(2,1)S(1)} %get-tuple-element.61), channel_id=1, source_target_pairs={{0,4},{4,0},{8,12},{12,8},{1,5},{5,1},{9,13},{13,9},{2,6},{6,2},{1... | collective-permute-start | bytes 663560 | tf_op jit(solution)/shard_map/ppermute | solution.py:377
  68.6 13.4 %collective-permute-start.17 = (bf16[6,48,384]{2,1,0:T(8,128)(2,1)S(1)}, bf16[6,48,384]{2,1,0:T(8,128)(2,1)S(1)}, u32[]{:S(2)}, u32[]{:S(2)}) collective-permute-start(bf16[6,48,384]{2,1,0:T(8,128)(2,1)S(1)} %get-tuple-element.62), channel_id=1, source_target_pairs={{0,8},{4,12},{8,0},{12,4},{1,9},{5,13},{9,1},{13,5},{2,10},{6,14},... | collective-permute-start | bytes 663560 | tf_op jit(solution)/shard_map/ppermute | solution.py:377
  71.7 12.9 %collective-permute-start.18 = (bf16[6,48,384]{2,1,0:T(8,128)(2,1)S(1)}, bf16[6,48,384]{2,1,0:T(8,128)(2,1)S(1)}, u32[]{:S(2)}, u32[]{:S(2)}) collective-permute-start(bf16[6,48,384]{2,1,0:T(8,128)(2,1)S(1)} %get-tuple-element.63), channel_id=1, source_target_pairs={{0,12},{4,8},{8,4},{12,0},{1,13},{5,9},{9,5},{13,1},{2,14},{6,10},... | collective-permute-start | bytes 663560 | tf_op jit(solution)/shard_map/ppermute | solution.py:377
  76.7 23.4 %collective-permute-start.13 = (bf16[768,128]{1,0:T(8,128)(2,1)S(1)}, bf16[768,128]{1,0:T(8,128)(2,1)S(1)}, u32[]{:S(2)}, u32[]{:S(2)}) collective-permute-start(bf16[768,128]{1,0:T(8,128)(2,1)S(1)} %get-tuple-element.54), channel_id=1, source_target_pairs={{0,1},{1,0},{2,3},{3,2},{4,5},{5,4},{6,7},{7,6},{8,9},{9,8},{10,11... | collective-permute-start | bytes 589832 | tf_op jit(solution)/shard_map/ppermute | solution.py:398
  76.7 23.4 %collective-permute-start.14 = (bf16[768,128]{1,0:T(8,128)(2,1)S(1)}, bf16[768,128]{1,0:T(8,128)(2,1)S(1)}, u32[]{:S(2)}, u32[]{:S(2)}) collective-permute-start(bf16[768,128]{1,0:T(8,128)(2,1)S(1)} %get-tuple-element.55), channel_id=1, source_target_pairs={{0,2},{1,3},{2,0},{3,1},{4,6},{5,7},{6,4},{7,5},{8,10},{9,11},{10,... | collective-permute-start | bytes 589832 | tf_op jit(solution)/shard_map/ppermute | solution.py:398
  84.8 5.2 %collective-permute-start.19 = (bf16[6,48,96]{2,1,0:T(8,128)(2,1)S(1)}, bf16[6,48,96]{2,1,0:T(8,128)(2,1)S(1)}, u32[]{:S(2)}, u32[]{:S(2)}) collective-permute-start(bf16[6,48,96]{2,1,0:T(8,128)(2,1)S(1)} %get-tuple-element.65), channel_id=1, source_target_pairs={{0,1},{1,0},{2,3},{3,2},{4,5},{5,4},{6,7},{7,6},{8,9},{9,8},{10,11... | collective-permute-start | bytes 165896 | tf_op jit(solution)/shard_map/ppermute | solution.py:377
  87.0 6.1 %collective-permute-start.20 = (bf16[6,48,96]{2,1,0:T(8,128)(2,1)S(1)}, bf16[6,48,96]{2,1,0:T(8,128)(2,1)S(1)}, u32[]{:S(2)}, u32[]{:S(2)}) collective-permute-start(bf16[6,48,96]{2,1,0:T(8,128)(2,1)S(1)} %get-tuple-element.66), channel_id=1, source_target_pairs={{0,2},{1,3},{2,0},{3,1},{4,6},{5,7},{6,4},{7,5},{8,10},{9,11},{10,... | collective-permute-start | bytes 165896 | tf_op jit(solution)/shard_map/ppermute | solution.py:377
  88.3 6.8 %collective-permute-start.21 = (bf16[6,48,96]{2,1,0:T(8,128)(2,1)S(1)}, bf16[6,48,96]{2,1,0:T(8,128)(2,1)S(1)}, u32[]{:S(2)}, u32[]{:S(2)}) collective-permute-start(bf16[6,48,96]{2,1,0:T(8,128)(2,1)S(1)} %get-tuple-element.67), channel_id=1, source_target_pairs={{0,3},{1,2},{2,1},{3,0},{4,7},{5,6},{6,5},{7,4},{8,11},{9,10},{10,... | collective-permute-start | bytes 165896 | tf_op jit(solution)/shard_map/ppermute | solution.py:377
  95.3 7.9 %collective-permute-start.22 = (bf16[6,48,96]{2,1,0:T(8,128)(2,1)S(1)}, bf16[6,48,96]{2,1,0:T(8,128)(2,1)S(1)}, u32[]{:S(2)}, u32[]{:S(2)}) collective-permute-start(bf16[6,48,96]{2,1,0:T(8,128)(2,1)S(1)} %get-tuple-element.69), channel_id=1, source_target_pairs={{0,64},{64,0},{128,192},{192,128},{1,65},{65,1},{129,193},{193,129... | collective-permute-start | bytes 165896 | tf_op jit(solution)/shard_map/ppermute | solution.py:377
  96.9 6.3 %collective-permute-start.23 = (bf16[6,48,96]{2,1,0:T(8,128)(2,1)S(1)}, bf16[6,48,96]{2,1,0:T(8,128)(2,1)S(1)}, u32[]{:S(2)}, u32[]{:S(2)}) collective-permute-start(bf16[6,48,96]{2,1,0:T(8,128)(2,1)S(1)} %get-tuple-element.70), channel_id=1, source_target_pairs={{0,128},{64,192},{128,0},{192,64},{1,129},{65,193},{129,1},{193,65... | collective-permute-start | bytes 165896 | tf_op jit(solution)/shard_map/ppermute | solution.py:377
  99.6 5.6 %collective-permute-start.24 = (bf16[6,48,96]{2,1,0:T(8,128)(2,1)S(1)}, bf16[6,48,96]{2,1,0:T(8,128)(2,1)S(1)}, u32[]{:S(2)}, u32[]{:S(2)}) collective-permute-start(bf16[6,48,96]{2,1,0:T(8,128)(2,1)S(1)} %get-tuple-element.71), channel_id=1, source_target_pairs={{0,192},{64,128},{128,64},{192,0},{1,193},{65,129},{129,65},{193,1... | collective-permute-start | bytes 165896 | tf_op jit(solution)/shard_map/ppermute | solution.py:377
  105.2 7.6 %collective-permute-start.25 = (bf16[3,48,96]{2,1,0:T(8,128)(2,1)S(1)}, bf16[3,48,96]{2,1,0:T(8,128)(2,1)S(1)}, u32[]{:S(2)}, u32[]{:S(2)}) collective-permute-start(bf16[3,48,96]{2,1,0:T(8,128)(2,1)S(1)} %get-tuple-element.74), channel_id=1, source_target_pairs={{0,35},{1,34},{2,33},{3,32},{32,3},{33,2},{34,1},{35,0},{4,39},{5,... | collective-permute-start | bytes 82952 | tf_op jit(solution)/shard_map/ppermute | solution.py:421

commit v4 on v3

--- a/solution.py
+++ b/solution.py
@@ -83,6 +83,7 @@
     return pl.pallas_call(
         project_kernel,
         in_specs=[HBM, HBM, HBM],
+        out_specs=[VMEM] * 4,
         out_shape=[shape((4 * HS, ROWS))] * 4,
         scratch_shapes=[
             pltpu.VMEM((ROWS, D), BF),
@@ -98,17 +99,17 @@
 
 def stack_kernel(*refs):
     kv, qd = refs[-2:]
-    for k, block in enumerate(refs[:4]):
+    for k, block in enumerate(refs[:2]):
         at = slice(k * ROWS, (k + 1) * ROWS)
         kv[:, at] = block[: 2 * HS, :]
         qd[:, at] = block[2 * HS :, :]
 
 
-def stack(blocks, after):
+def stack(blocks, after=()):
     return pl.pallas_call(
         stack_kernel,
-        in_specs=[VMEM] * 4 + [ANY] * len(after),
-        out_shape=[shape((2 * HS, 4 * ROWS))] * 2,
+        in_specs=[VMEM] * 2 + [ANY] * len(after),
+        out_shape=[shape((2 * HS, 2 * ROWS))] * 2,
         compiler_params=params(),
         name="stack",
     )(*blocks, *after)
@@ -116,14 +117,14 @@
 
 def side_by_side(blocks, wide):
     for k, block in enumerate(blocks):
-        wide[:, k * 4 * ROWS : (k + 1) * 4 * ROWS] = block[...]
+        wide[:, k * 2 * ROWS : (k + 1) * 2 * ROWS] = block[...]
 
 
 TILE = 256
 
 
 def stats_kernel(*refs):
-    kv_blocks, qd_blocks, (stats, kv, qd) = refs[:2], refs[2:4], refs[-3:]
+    kv_blocks, qd_blocks, (stats, kv, qd) = refs[:4], refs[4:8], refs[-3:]
     side_by_side(kv_blocks, kv)
     side_by_side(qd_blocks, qd)
     keys = flip(kv[:HS, :]).astype(BF)
@@ -152,7 +153,7 @@
 
 
 def attend_kernel(*refs):
-    kv_blocks, qd_blocks, mine, theirs = refs[:2], refs[2:4], refs[4], refs[5]
+    kv_blocks, qd_blocks, mine, theirs = refs[:4], refs[4:8], refs[8], refs[9]
     qo_own, qo_send, kv_own, kv_send, kv, qd, kv_sum = refs[-7:]
     side_by_side(kv_blocks, kv)
     side_by_side(qd_blocks, qd)
@@ -199,7 +200,7 @@
     out = (2 * HS, 4 * ROWS)
     return pl.pallas_call(
         attend_kernel,
-        in_specs=[VMEM] * (6 + len(after)),
+        in_specs=[VMEM] * (10 + len(after)),
         out_shape=[shape(out, F32), shape(out), shape(out, F32), shape(out)],
         scratch_shapes=[pltpu.VMEM(wide, BF), pltpu.VMEM(wide, BF), pltpu.VMEM(wide, F32)],
         compiler_params=params(24),
@@ -379,11 +380,14 @@
     pair = lax.ppermute(tokens, "zl", near)
     middle = lax.ppermute(tokens, "zl", [(1, 2), (2, 1)])
     heads = spread(project(tokens, w_proj, d_attended[0]), "zl")
-    kv, qd = stack(heads, [pair, middle])
-    late = lax.optimization_barrier((tokens, kv))[0]
+    kv_a, qd_a = stack(heads[:2], [middle, pair])
+    far_a, near_a = lax.ppermute(kv_a, "y", far), lax.ppermute(qd_a, "y", near)
+    kv_b, qd_b = stack(heads[2:], [far_a, near_a])
+    late = lax.optimization_barrier((tokens, kv_b))[0]
     second = lax.ppermute(late, "zl", exchange(2))
     ends = lax.ppermute(late, "zl", [(0, 3), (3, 0)])
-    kv, qd = [kv, lax.ppermute(kv, "y", far)], [qd, lax.ppermute(qd, "y", near)]
+    kv = [kv_a, kv_b, far_a, lax.ppermute(kv_b, "y", far)]
+    qd = [qd_a, qd_b, near_a, lax.ppermute(qd_b, "y", near)]
 
     mine = stats_of(kv, qd)
     theirs = lax.ppermute(mine, "y", near)
@@ -394,8 +398,9 @@
     rows = [tokens, pair, second, middle, ends]
     *back, keep, send = gradient(qo_own, qo_got, kv_own, kv_got, rows)
     last = lax.ppermute(back[3], "zl", exchange(3))
-    later = lax.optimization_barrier((back[1], back[2], last))
-    returned = [back[0]] + [lax.ppermute(later[k - 1], "zl", exchange(k)) for k in (1, 2)] + [last]
+    later = lax.optimization_barrier((back[2], last))[0]
+    first, second = (lax.ppermute(b, "zl", exchange(k)) for k, b in ((1, back[1]), (2, later)))
+    returned = [back[0], first, second, last]
     attended, d_tokens, done = tokens_of(tokens, w_proj, returned)
     got = lax.ppermute(send, "c", swap)
     blocks = small(
@@ -403,6 +408,7 @@
         [shape((6, 48, 384))] * 4, [pltpu.VMEM((6, 48, D), BF)],
     )
     blocks = spread(blocks, "y")
+    blocks = [blocks[k] for k in (0, 1, 3, 2)]
     blocks = small(
         split_z_kernel, "split_z", blocks,
         [shape((6, 48, 96))] * 4, [pltpu.VMEM((4, 6, 48, 96), BF)],
@@ -414,6 +420,7 @@
         [pltpu.VMEM((4, 6, 48, 96), BF), pltpu.VMEM((24, 48, 96), BF)],
     )
     blocks = spread(blocks, "x")
+    blocks = [blocks[k] for k in (0, 1, 3, 2)]
     keep, send = small(
         split_zh_kernel, "split_zh", blocks,
         [shape((3, 48, 96), F32), shape((3, 48, 96))], [pltpu.VMEM((6, 48, 96), F32)], [done],

time: 114 us -> 109 us (0.956)
  waiting for transfers between devices: 55.3 us -> 46 us
  starting transfers between devices: 39.2 us -> 43.9 us
    ppermute x12, waiting for transfers between devices: 30.5 us -> 27.2 us  [spread(): lax.ppermute(blocks[k], axis, exchange(k))]
    ppermute x4 -> x6, waiting for transfers between devices: 7.85 us -> 4.71 us  [the longest x1 2.65 us: per_device(): kv = [kv_a, kv_b, far_a, lax.ppermute(kv_b, 'y', far)]]
    ppermute x4 -> x6, starting transfers between devices: 7.07 us -> 9.66 us  [the longest x1 3.1 us: per_device(): lax.ppermute(kv_a, 'y', far)]
    ppermute x1, starting transfers between devices: 0.09 us -> 2.23 us  [per_device(): second = lax.ppermute(late, 'zl', exchange(2))]
    ppermute x1, waiting for transfers between devices: 3.79 us -> 1.67 us  [per_device(): theirs = lax.ppermute(mine, 'y', near)]
    ppermute x1, waiting for transfers between devices: 3.96 us -> 2.1 us  [per_device(): last = lax.ppermute(back[3], 'zl', exchange(3))]
    ppermute x1, starting transfers between devices: 0.09 us -> 1.93 us  [per_device(): pair = lax.ppermute(tokens, 'zl', near)]
    ppermute x1, starting transfers between devices: 5.67 us -> 3.85 us  [per_device(): got = lax.ppermute(send, ('zh', 'zl'), [(z, 7 - z) for z in range(8)])]
  transfers between devices with their start and end apart: 26 -> 28, of which waited for: 17 -> 18; matrix products, arithmetic and copies ran while one was open for 0% -> 0% of each run, Pallas kernels for 13% -> 14%
where the time goes in v4:
time: 109 us
  waiting for transfers between devices  46 us (42%)
  starting transfers between devices  43.9 us (40%)
  Pallas kernels  17.2 us (16%)
    ppermute x12, waiting for transfers between devices, spread(): lax.ppermute(blocks[k], axis, exchange(k))  27.2 us
    ppermute x12, starting transfers between devices, spread(): lax.ppermute(blocks[k], axis, exchange(k))  16.9 us
    ppermute x1, waiting for transfers between devices, per_device(): second = lax.ppermute(late, 'zl', exchange(2))  5.72 us
    pallas_call x1, Pallas kernels, project(): pl.pallas_call(project_kernel, in_specs=[HBM, HBM, HBM], out_specs=[VMEM]...  5.09 us
    ppermute x1, starting transfers between devices, per_device(): middle = lax.ppermute(tokens, 'zl', [(1, 2), (2, 1)])  3.89 us
    ppermute x1, starting transfers between devices, per_device(): got = lax.ppermute(send, ('zh', 'zl'), [(z, 7 - z) for z in range(8)])  3.85 us
    pallas_call x1, Pallas kernels, attend(): pl.pallas_call(attend_kernel, in_specs=[VMEM] * (10 + len(after)), out_sh...  3.65 us
    ppermute x1, waiting for transfers between devices, per_device(): got = lax.ppermute(send, ('zh', 'zl'), [(z, 7 - z) for z in range(8)])  3.2 us
  transfers between devices with their start and end apart: 28, of which 18 were waited for; matrix products, arithmetic and copies ran while one was open for 0% of the time, Pallas kernels for 14%

profile of v4, /device:TPU:32, one launch (start us, length us, event | category | flops | bytes accessed | tf_op | source)
XLA Modules:
  0.0 108.8 jit_solution(2440808374325177894)
XLA Ops:
  0.6 1.9 %collective-permute-start.2 = (bf16[128,1536]{1,0:T(8,128)(2,1)}, bf16[128,1536]{1,0:T(8,128)(2,1)S(1)}, u32[]{:S(2)}, u32[]{:S(2)}) collective-permute-start(bf16[128,1536]{1,0:T(8,128)(2,1)} %bitcast.7), channel_id=1, source_target_pairs={{0,1},{1,0},{2,3},{3,2},{4,5},{5,4},{6,7},{7,6},{8,9},{9,8},{10,11... | collective-permute-start | bytes 1179656 | tf_op jit(solution)/shard_map/ppermute | solution.py:380
  2.6 3.9 %collective-permute-start.1 = (bf16[128,1536]{1,0:T(8,128)(2,1)}, bf16[128,1536]{1,0:T(8,128)(2,1)S(1)}, u32[]{:S(2)}, u32[]{:S(2)}) collective-permute-start(bf16[128,1536]{1,0:T(8,128)(2,1)} %bitcast.8), channel_id=1, source_target_pairs={{1,2},{2,1},{5,6},{6,5},{9,10},{10,9},{13,14},{14,13},{17,18},{18,... | collective-permute-start | bytes 1179656 | tf_op jit(solution)/shard_map/ppermute | solution.py:381
  6.5 0.0 slice-start
  6.5 5.1 %project.1 = (bf16[768,128]{1,0:T(8,128)(2,1)}, bf16[768,128]{1,0:T(8,128)(2,1)}, bf16[768,128]{1,0:T(8,128)(2,1)}, bf16[768,128]{1,0:T(8,128)(2,1)}) custom-call(bf16[128,1536]{1,0:T(8,128)(2,1)} %bitcast.9, bf16[1536,2304]{1,0:T(8,128)(2,1)} %weights.1, bf16[128,768]{1,0:T(8,128)(2,1)} %bitcast.14), custom_call_target="tpu_custom_call" | custom-call | tf_op jit(solution)/shard_map/project/pallas_call | solution.py:83
  11.6 0.1 collective-permute-start
  11.7 1.5 %collective-permute-start.3 = (bf16[768,128]{1,0:T(8,128)(2,1)}, bf16[768,128]{1,0:T(8,128)(2,1)S(1)}, u32[]{:S(2)}, u32[]{:S(2)}) collective-permute-start(bf16[768,128]{1,0:T(8,128)(2,1)} %get-tuple-element.43), channel_id=1, source_target_pairs={{0,2},{1,3},{2,0},{3,1},{4,6},{5,7},{6,4},{7,5},{8,10},{9,11},{10,... | collective-permute-start | bytes 589832 | tf_op jit(solution)/shard_map/ppermute | solution.py:378
  13.2 2.0 %collective-permute-start.4 = (bf16[768,128]{1,0:T(8,128)(2,1)}, bf16[768,128]{1,0:T(8,128)(2,1)S(1)}, u32[]{:S(2)}, u32[]{:S(2)}) collective-permute-start(bf16[768,128]{1,0:T(8,128)(2,1)} %get-tuple-element.44), channel_id=1, source_target_pairs={{0,3},{1,2},{2,1},{3,0},{4,7},{5,6},{6,5},{7,4},{8,11},{9,10},{10,... | collective-permute-start | bytes 589832 | tf_op jit(solution)/shard_map/ppermute | solution.py:378
  15.1 4.6 %collective-permute-done.refs_1_ = bf16[768,128]{1,0:T(8,128)(2,1)S(1)} collective-permute-done((bf16[768,128]{1,0:T(8,128)(2,1)}, bf16[768,128]{1,0:T(8,128)(2,1)S(1)}, u32[]{:S(2)}, u32[]{:S(2)}) %collective-permute-start) | collective-permute-done | bytes 196640 | tf_op jit(solution)/shard_map/ppermute | solution.py:378
  19.7 0.0 collective-permute-done.2.refs_3_.refs_1_
  19.7 0.9 copy-done.1
  20.6 0.1 stack.2
  20.7 3.1 %collective-permute-start.5 = (bf16[384,256]{1,0:T(8,128)(2,1)S(1)}, bf16[384,256]{1,0:T(8,128)(2,1)S(1)}, u32[]{:S(2)}, u32[]{:S(2)}) collective-permute-start(bf16[384,256]{1,0:T(8,128)(2,1)S(1)} %get-tuple-element.42.refs_0_), channel_id=1, source_target_pairs={{0,12},{4,8},{8,4},{12,0},{1,13},{5,9},{9,5},{13,1},{2,14},{6,10},... | collective-permute-start | bytes 589832 | tf_op jit(solution)/shard_map/ppermute | solution.py:384
  23.8 0.1 collective-permute-start.6
  24.0 5.0 %collective-permute-done.3.refs_0_ = bf16[768,128]{1,0:T(8,128)(2,1)S(1)} collective-permute-done((bf16[768,128]{1,0:T(8,128)(2,1)}, bf16[768,128]{1,0:T(8,128)(2,1)S(1)}, u32[]{:S(2)}, u32[]{:S(2)}) %collective-permute-start.3) | collective-permute-done | bytes 196640 | tf_op jit(solution)/shard_map/ppermute | solution.py:378
  29.0 3.4 %collective-permute-done.4.refs_1_ = bf16[768,128]{1,0:T(8,128)(2,1)S(1)} collective-permute-done((bf16[768,128]{1,0:T(8,128)(2,1)}, bf16[768,128]{1,0:T(8,128)(2,1)S(1)}, u32[]{:S(2)}, u32[]{:S(2)}) %collective-permute-start.4) | collective-permute-done | bytes 196640 | tf_op jit(solution)/shard_map/ppermute | solution.py:378
  32.4 0.1 stack.3
  32.4 0.7 collective-permute-start.10
  33.1 0.0 slice-start.1
  33.1 1.7 %collective-permute-start.8 = (bf16[384,256]{1,0:T(8,128)(2,1)S(1)}, bf16[384,256]{1,0:T(8,128)(2,1)S(1)}, u32[]{:S(2)}, u32[]{:S(2)}) collective-permute-start(bf16[384,256]{1,0:T(8,128)(2,1)S(1)} %get-tuple-element.47.refs_5_), channel_id=1, source_target_pairs={{0,4},{4,0},{8,12},{12,8},{1,5},{5,1},{9,13},{13,9},{2,6},{6,2},{1... | collective-permute-start | bytes 589832 | tf_op jit(solution)/shard_map/ppermute | solution.py:390
  34.8 2.2 %collective-permute-start.7 = (bf16[384,256]{1,0:T(8,128)(2,1)S(1)}, bf16[384,256]{1,0:T(8,128)(2,1)S(1)}, u32[]{:S(2)}, u32[]{:S(2)}) collective-permute-start(bf16[384,256]{1,0:T(8,128)(2,1)S(1)} %get-tuple-element.46.refs_1_), channel_id=1, source_target_pairs={{0,12},{4,8},{8,4},{12,0},{1,13},{5,9},{9,5},{13,1},{2,14},{6,10},... | collective-permute-start | bytes 589832 | tf_op jit(solution)/shard_map/ppermute | solution.py:389
  37.0 2.0 %collective-permute-done.8.refs_7_ = bf16[384,256]{1,0:T(8,128)(2,1)S(1)} collective-permute-done((bf16[384,256]{1,0:T(8,128)(2,1)S(1)}, bf16[384,256]{1,0:T(8,128)(2,1)S(1)}, u32[]{:S(2)}, u32[]{:S(2)}) %collective-permute-start.8) | collective-permute-done | bytes 196640 | tf_op jit(solution)/shard_map/ppermute | solution.py:390
  39.0 2.6 %collective-permute-done.7.refs_3_ = bf16[384,256]{1,0:T(8,128)(2,1)S(1)} collective-permute-done((bf16[384,256]{1,0:T(8,128)(2,1)S(1)}, bf16[384,256]{1,0:T(8,128)(2,1)S(1)}, u32[]{:S(2)}, u32[]{:S(2)}) %collective-permute-start.7) | collective-permute-done | bytes 196640 | tf_op jit(solution)/shard_map/ppermute | solution.py:389
  41.7 1.9 %stats.1.refs_8_ = f32[8,1024]{1,0:T(8,128)S(1)} custom-call(bf16[384,256]{1,0:T(8,128)(2,1)S(1)} %get-tuple-element.42.refs_0_, bf16[384,256]{1,0:T(8,128)(2,1)S(1)} %get-tuple-element.46.refs_1_, bf16[384,256]{1,0:T(8,128)(2,1)S(1)} %collective-permute-done.5.refs_2_, bf16[384,256]{1,0:T(8,128)(2,1)S(1)} %collective-permute-done.7.refs_3_, ...), custom_call_target="tpu_custom_call" | custom-call | tf_op jit(solution)/shard_map/stats/pallas_call | solution.py:146
  43.6 0.1 collective-permute-start.9
  43.7 2.2 %collective-permute-start.13 = (bf16[128,1536]{1,0:T(8,128)(2,1)S(1)}, bf16[128,1536]{1,0:T(8,128)(2,1)S(1)}, u32[]{:S(2)}, u32[]{:S(2)}) collective-permute-start(bf16[128,1536]{1,0:T(8,128)(2,1)S(1)} %bitcast.11), channel_id=1, source_target_pairs={{0,2},{1,3},{2,0},{3,1},{4,6},{5,7},{6,4},{7,5},{8,10},{9,11},{10,... | collective-permute-start | bytes 1179656 | tf_op jit(solution)/shard_map/ppermute | solution.py:387
  45.9 1.7 %collective-permute-done.9.refs_9_ = f32[8,1024]{1,0:T(8,128)S(1)} collective-permute-done((f32[8,1024]{1,0:T(8,128)S(1)}, f32[8,1024]{1,0:T(8,128)S(1)}, u32[]{:S(2)}, u32[]{:S(2)}) %collective-permute-start.9) | collective-permute-done | bytes 32800 | tf_op jit(solution)/shard_map/ppermute | solution.py:393
  47.6 0.0 collective-permute-done.10.refs_10_.refs_4_
  47.6 3.6 %attend.1 = (f32[384,512]{1,0:T(8,128)S(1)}, bf16[384,512]{1,0:T(8,128)(2,1)S(1)}, f32[384,512]{1,0:T(8,128)S(1)}, bf16[384,512]{1,0:T(8,128)(2,1)S(1)}) custom-call(bf16[384,256]{1,0:T(8,128)(2,1)S(1)} %get-tuple-element.42.refs_0_, bf16[384,256]{1,0:T(8,128)(2,1)S(1)} %get-tuple-element.46.refs_1_, bf16[384,256]{1,0:T(8,128)(2,1)S(1)} %collective-permute-done.5.refs_2_, ...), custom_call_target="tpu_custom_call" | custom-call | tf_op jit(solution)/shard_map/attend/pallas_call | solution.py:201
  51.2 0.2 collective-permute-start.11
  51.4 2.2 %collective-permute-start.12 = (bf16[384,512]{1,0:T(8,128)(2,1)S(1)}, bf16[384,512]{1,0:T(8,128)(2,1)S(1)}, u32[]{:S(2)}, u32[]{:S(2)}) collective-permute-start(bf16[384,512]{1,0:T(8,128)(2,1)S(1)} %get-tuple-element.52), channel_id=1, source_target_pairs={{0,12},{4,8},{8,4},{12,0},{1,13},{5,9},{9,5},{13,1},{2,14},{6,10},... | collective-permute-start | bytes 1179656 | tf_op jit(solution)/shard_map/ppermute | solution.py:396
  53.6 5.7 %collective-permute-done.13.refs_2_ = bf16[128,1536]{1,0:T(8,128)(2,1)S(1)} collective-permute-done((bf16[128,1536]{1,0:T(8,128)(2,1)S(1)}, bf16[128,1536]{1,0:T(8,128)(2,1)S(1)}, u32[]{:S(2)}, u32[]{:S(2)}) %collective-permute-start.13) | collective-permute-done | bytes 393248 | tf_op jit(solution)/shard_map/ppermute | solution.py:387
  59.3 1.1 collective-permute-done.12.kv_got
  60.4 1.7 %gradient.1 = (bf16[768,128]{1,0:T(8,128)(2,1)S(1)}, bf16[768,128]{1,0:T(8,128)(2,1)S(1)}, bf16[768,128]{1,0:T(8,128)(2,1)S(1)}, bf16[768,128]{1,0:T(8,128)(2,1)...) custom-call(f32[384,512]{1,0:T(8,128)S(1)} %get-tuple-element.49.qo_own, ...), custom_call_target="tpu_custom_call" | custom-call | tf_op jit(solution)/shard_map/gradient/pallas_call | solution.py:243
  62.1 0.1 collective-permute-start.17
  62.2 2.1 %collective-permute-start.15 = (bf16[768,128]{1,0:T(8,128)(2,1)S(1)}, bf16[768,128]{1,0:T(8,128)(2,1)S(1)}, u32[]{:S(2)}, u32[]{:S(2)}) collective-permute-start(bf16[768,128]{1,0:T(8,128)(2,1)S(1)} %get-tuple-element.56), channel_id=1, source_target_pairs={{0,3},{1,2},{2,1},{3,0},{4,7},{5,6},{6,5},{7,4},{8,11},{9,10},{10,... | collective-permute-start | bytes 589832 | tf_op jit(solution)/shard_map/ppermute | solution.py:400
  64.4 0.3 collective-permute-done.17.got
  64.7 0.5 split_y.1
  65.2 0.8 collective-permute-start.18
  66.0 2.2 %collective-permute-start.19 = (bf16[6,48,384]{2,1,0:T(8,128)(2,1)S(1)}, bf16[6,48,384]{2,1,0:T(8,128)(2,1)S(1)}, u32[]{:S(2)}, u32[]{:S(2)}) collective-permute-start(bf16[6,48,384]{2,1,0:T(8,128)(2,1)S(1)} %get-tuple-element.64), channel_id=1, source_target_pairs={{0,12},{4,8},{8,4},{12,0},{1,13},{5,9},{9,5},{13,1},{2,14},{6,10},... | collective-permute-start | bytes 663560 | tf_op jit(solution)/shard_map/ppermute | solution.py:378
  68.2 1.2 %collective-permute-start.20 = (bf16[6,48,384]{2,1,0:T(8,128)(2,1)S(1)}, bf16[6,48,384]{2,1,0:T(8,128)(2,1)S(1)}, u32[]{:S(2)}, u32[]{:S(2)}) collective-permute-start(bf16[6,48,384]{2,1,0:T(8,128)(2,1)S(1)} %get-tuple-element.65), channel_id=1, source_target_pairs={{0,8},{4,12},{8,0},{12,4},{1,9},{5,13},{9,1},{13,5},{2,10},{6,14},... | collective-permute-start | bytes 663560 | tf_op jit(solution)/shard_map/ppermute | solution.py:378
  69.4 2.6 %collective-permute-start.14 = (bf16[768,128]{1,0:T(8,128)(2,1)S(1)}, bf16[768,128]{1,0:T(8,128)(2,1)S(1)}, u32[]{:S(2)}, u32[]{:S(2)}) collective-permute-start(bf16[768,128]{1,0:T(8,128)(2,1)S(1)} %get-tuple-element.54), channel_id=1, source_target_pairs={{0,1},{1,0},{2,3},{3,2},{4,5},{5,4},{6,7},{7,6},{8,9},{9,8},{10,11... | collective-permute-start | bytes 589832 | tf_op jit(solution)/shard_map/ppermute | solution.py:402
  72.0 2.1 %collective-permute-done.15.refs_3_ = bf16[768,128]{1,0:T(8,128)(2,1)S(1)} collective-permute-done((bf16[768,128]{1,0:T(8,128)(2,1)S(1)}, bf16[768,128]{1,0:T(8,128)(2,1)S(1)}, u32[]{:S(2)}, u32[]{:S(2)}) %collective-permute-start.15) | collective-permute-done | bytes 196640 | tf_op jit(solution)/shard_map/ppermute | solution.py:400
  74.1 0.0 collective-permute-start.16
  74.1 3.6 %collective-permute-done.19.refs_2_ = bf16[6,48,384]{2,1,0:T(8,128)(2,1)S(1)} collective-permute-done((bf16[6,48,384]{2,1,0:T(8,128)(2,1)S(1)}, bf16[6,48,384]{2,1,0:T(8,128)(2,1)S(1)}, u32[]{:S(2)}, u32[]{:S(2)}) %collective-permute-start.19) | collective-permute-done | bytes 221216 | tf_op jit(solution)/shard_map/ppermute | solution.py:378
  77.7 1.5 %collective-permute-done.20.refs_3_ = bf16[6,48,384]{2,1,0:T(8,128)(2,1)S(1)} collective-permute-done((bf16[6,48,384]{2,1,0:T(8,128)(2,1)S(1)}, bf16[6,48,384]{2,1,0:T(8,128)(2,1)S(1)}, u32[]{:S(2)}, u32[]{:S(2)}) %collective-permute-start.20) | collective-permute-done | bytes 221216 | tf_op jit(solution)/shard_map/ppermute | solution.py:378
  79.1 0.3 split_z.1
  79.4 3.1 %collective-permute-start.21 = (bf16[6,48,96]{2,1,0:T(8,128)(2,1)S(1)}, bf16[6,48,96]{2,1,0:T(8,128)(2,1)S(1)}, u32[]{:S(2)}, u32[]{:S(2)}) collective-permute-start(bf16[6,48,96]{2,1,0:T(8,128)(2,1)S(1)} %get-tuple-element.67), channel_id=1, source_target_pairs={{0,1},{1,0},{2,3},{3,2},{4,5},{5,4},{6,7},{7,6},{8,9},{9,8},{10,11... | collective-permute-start | bytes 165896 | tf_op jit(solution)/shard_map/ppermute | solution.py:378
  82.5 0.5 collective-permute-start.22
  83.0 1.1 collective-permute-start.23
  84.1 2.7 %collective-permute-done.21.refs_1_ = bf16[6,48,96]{2,1,0:T(8,128)(2,1)S(1)} collective-permute-done((bf16[6,48,96]{2,1,0:T(8,128)(2,1)S(1)}, bf16[6,48,96]{2,1,0:T(8,128)(2,1)S(1)}, u32[]{:S(2)}, u32[]{:S(2)}) %collective-permute-start.21) | collective-permute-done | bytes 55328 | tf_op jit(solution)/shard_map/ppermute | solution.py:378
  86.7 1.1 collective-permute-done.22.refs_2_
  87.8 3.4 %collective-permute-done.23.refs_3_ = bf16[6,48,96]{2,1,0:T(8,128)(2,1)S(1)} collective-permute-done((bf16[6,48,96]{2,1,0:T(8,128)(2,1)S(1)}, bf16[6,48,96]{2,1,0:T(8,128)(2,1)S(1)}, u32[]{:S(2)}, u32[]{:S(2)}) %collective-permute-start.23) | collective-permute-done | bytes 55328 | tf_op jit(solution)/shard_map/ppermute | solution.py:378
  91.2 0.2 split_x.1
  91.3 1.8 %collective-permute-start.24 = (bf16[6,48,96]{2,1,0:T(8,128)(2,1)S(1)}, bf16[6,48,96]{2,1,0:T(8,128)(2,1)S(1)}, u32[]{:S(2)}, u32[]{:S(2)}) collective-permute-start(bf16[6,48,96]{2,1,0:T(8,128)(2,1)S(1)} %get-tuple-element.71), channel_id=1, source_target_pairs={{0,64},{64,0},{128,192},{192,128},{1,65},{65,1},{129,193},{193,129... | collective-permute-start | bytes 165896 | tf_op jit(solution)/shard_map/ppermute | solution.py:378
  93.1 2.1 %collective-permute-start.25 = (bf16[6,48,96]{2,1,0:T(8,128)(2,1)S(1)}, bf16[6,48,96]{2,1,0:T(8,128)(2,1)S(1)}, u32[]{:S(2)}, u32[]{:S(2)}) collective-permute-start(bf16[6,48,96]{2,1,0:T(8,128)(2,1)S(1)} %get-tuple-element.72), channel_id=1, source_target_pairs={{0,192},{64,128},{128,64},{192,0},{1,193},{65,129},{129,65},{193,1... | collective-permute-start | bytes 165896 | tf_op jit(solution)/shard_map/ppermute | solution.py:378
  95.2 0.6 collective-permute-start.26
  95.9 0.0 collective-permute-done.14.refs_1_
  95.9 3.1 %d_tokens.1 = (bf16[128,768]{1,0:T(8,128)(2,1)}, bf16[128,1536]{1,0:T(8,128)(2,1)}, f32[8,128]{1,0:T(8,128)S(1)}) custom-call(bf16[128,1536]{1,0:T(8,128)(2,1)S(1)} %bitcast.13, bf16[1536,2304]{1,0:T(8,128)(2,1)S(1)} %bitcast.6, bf16[768,128]{1,0:T(8,128)(2,1)S(1)} %get-tuple-element.53.refs_0_, bf16[768,128]{1,0:T(8,128)(2,1)S(1)} %collective-permute-done.14.refs_1_, ...), custom_call_target="tpu_custom_call" | custom-call | tf_op jit(solution)/shard_map/d_tokens/pallas_call | solution.py:281
  99.0 0.4 collective-permute-done.25.refs_2_
  99.3 1.8 %collective-permute-done.26.refs_3_ = bf16[6,48,96]{2,1,0:T(8,128)(2,1)S(1)} collective-permute-done((bf16[6,48,96]{2,1,0:T(8,128)(2,1)S(1)}, bf16[6,48,96]{2,1,0:T(8,128)(2,1)S(1)}, u32[]{:S(2)}, u32[]{:S(2)}) %collective-permute-start.26) | collective-permute-done | bytes 55328 | tf_op jit(solution)/shard_map/ppermute | solution.py:378
  101.1 0.1 split_zh.1
  101.1 3.9 %collective-permute-start.27 = (bf16[3,48,96]{2,1,0:T(8,128)(2,1)S(1)}, bf16[3,48,96]{2,1,0:T(8,128)(2,1)S(1)}, u32[]{:S(2)}, u32[]{:S(2)}) collective-permute-start(bf16[3,48,96]{2,1,0:T(8,128)(2,1)S(1)} %get-tuple-element.76), channel_id=1, source_target_pairs={{0,35},{1,34},{2,33},{3,32},{32,3},{33,2},{34,1},{35,0},{4,39},{5,... | collective-permute-start | bytes 82952 | tf_op jit(solution)/shard_map/ppermute | solution.py:428
  105.0 3.2 %collective-permute-done.27.got = bf16[3,48,96]{2,1,0:T(8,128)(2,1)S(1)} collective-permute-done((bf16[3,48,96]{2,1,0:T(8,128)(2,1)S(1)}, bf16[3,48,96]{2,1,0:T(8,128)(2,1)S(1)}, u32[]{:S(2)}, u32[]{:S(2)}) %collective-permute-start.27) | collective-permute-done | bytes 27680 | tf_op jit(solution)/shard_map/ppermute | solution.py:428
  108.2 0.6 finish.1
  (13 shorter events, 0.0 us)
Async XLA Ops:
  0.6 31.8 %copy-start = (bf16[1,128,1536]{2,1,0:T(8,128)(2,1)S(1)}, bf16[1,128,1536]{2,1,0:T(8,128)(2,1)}, u32[]{:S(2)}) copy-start(bf16[1,128,1536]{2,1,0:T(8,128)(2,1)} %param.3) | copy-start | bytes 1179652
  0.6 19.1 %collective-permute-start.2 = (bf16[128,1536]{1,0:T(8,128)(2,1)}, bf16[128,1536]{1,0:T(8,128)(2,1)S(1)}, u32[]{:S(2)}, u32[]{:S(2)}) collective-permute-start(bf16[128,1536]{1,0:T(8,128)(2,1)} %bitcast.7), channel_id=1, source_target_pairs={{0,1},{1,0},{2,3},{3,2},{4,5},{5,4},{6,7},{7,6},{8,9},{9,8},{10,11... | collective-permute-start | bytes 1179656 | tf_op jit(solution)/shard_map/ppermute | solution.py:380
  2.6 17.1 %collective-permute-start.1 = (bf16[128,1536]{1,0:T(8,128)(2,1)}, bf16[128,1536]{1,0:T(8,128)(2,1)S(1)}, u32[]{:S(2)}, u32[]{:S(2)}) collective-permute-start(bf16[128,1536]{1,0:T(8,128)(2,1)} %bitcast.8), channel_id=1, source_target_pairs={{1,2},{2,1},{5,6},{6,5},{9,10},{10,9},{13,14},{14,13},{17,18},{18,... | collective-permute-start | bytes 1179656 | tf_op jit(solution)/shard_map/ppermute | solution.py:381
  6.5 89.4 %slice-start = ((s8[7077888]{0:T(1024)(128)(4,1)}), s8[2883584]{0:T(1024)(128)(4,1)S(1)}, s32[]{:S(2)}) async-start(s8[7077888]{0:T(1024)(128)(4,1)} %bitcast.5), calls=%async_computation | async-start | bytes 5767168
  11.6 8.1 %collective-permute-start = (bf16[768,128]{1,0:T(8,128)(2,1)}, bf16[768,128]{1,0:T(8,128)(2,1)S(1)}, u32[]{:S(2)}, u32[]{:S(2)}) collective-permute-start(bf16[768,128]{1,0:T(8,128)(2,1)} %get-tuple-element.41), channel_id=1, source_target_pairs={{0,1},{1,0},{2,3},{3,2},{4,5},{5,4},{6,7},{7,6},{8,9},{9,8},{10,11... | collective-permute-start | bytes 589832 | tf_op jit(solution)/shard_map/ppermute | solution.py:378
  11.7 17.3 %collective-permute-start.3 = (bf16[768,128]{1,0:T(8,128)(2,1)}, bf16[768,128]{1,0:T(8,128)(2,1)S(1)}, u32[]{:S(2)}, u32[]{:S(2)}) collective-permute-start(bf16[768,128]{1,0:T(8,128)(2,1)} %get-tuple-element.43), channel_id=1, source_target_pairs={{0,2},{1,3},{2,0},{3,1},{4,6},{5,7},{6,4},{7,5},{8,10},{9,11},{10,... | collective-permute-start | bytes 589832 | tf_op jit(solution)/shard_map/ppermute | solution.py:378
  13.2 19.2 %collective-permute-start.4 = (bf16[768,128]{1,0:T(8,128)(2,1)}, bf16[768,128]{1,0:T(8,128)(2,1)S(1)}, u32[]{:S(2)}, u32[]{:S(2)}) collective-permute-start(bf16[768,128]{1,0:T(8,128)(2,1)} %get-tuple-element.44), channel_id=1, source_target_pairs={{0,3},{1,2},{2,1},{3,0},{4,7},{5,6},{6,5},{7,4},{8,11},{9,10},{10,... | collective-permute-start | bytes 589832 | tf_op jit(solution)/shard_map/ppermute | solution.py:378
  19.7 0.9 copy-start.1
  20.7 11.6 %collective-permute-start.5 = (bf16[384,256]{1,0:T(8,128)(2,1)S(1)}, bf16[384,256]{1,0:T(8,128)(2,1)S(1)}, u32[]{:S(2)}, u32[]{:S(2)}) collective-permute-start(bf16[384,256]{1,0:T(8,128)(2,1)S(1)} %get-tuple-element.42.refs_0_), channel_id=1, source_target_pairs={{0,12},{4,8},{8,4},{12,0},{1,13},{5,9},{9,5},{13,1},{2,14},{6,10},... | collective-permute-start | bytes 589832 | tf_op jit(solution)/shard_map/ppermute | solution.py:384
  23.8 8.5 %collective-permute-start.6 = (bf16[384,256]{1,0:T(8,128)(2,1)S(1)}, bf16[384,256]{1,0:T(8,128)(2,1)S(1)}, u32[]{:S(2)}, u32[]{:S(2)}) collective-permute-start(bf16[384,256]{1,0:T(8,128)(2,1)S(1)} %get-tuple-element.45.refs_4_), channel_id=1, source_target_pairs={{0,4},{4,0},{8,12},{12,8},{1,5},{5,1},{9,13},{13,9},{2,6},{6,2},{1... | collective-permute-start | bytes 589832 | tf_op jit(solution)/shard_map/ppermute | solution.py:384
  32.4 15.1 %collective-permute-start.10 = (bf16[128,1536]{1,0:T(8,128)(2,1)S(1)}, bf16[128,1536]{1,0:T(8,128)(2,1)S(1)}, u32[]{:S(2)}, u32[]{:S(2)}) collective-permute-start(bf16[128,1536]{1,0:T(8,128)(2,1)S(1)} %bitcast.10), channel_id=1, source_target_pairs={{0,3},{3,0},{4,7},{7,4},{8,11},{11,8},{12,15},{15,12},{16,19},{19,... | collective-permute-start | bytes 1179656 | tf_op jit(solution)/shard_map/ppermute | solution.py:388
  33.1 62.7 %slice-start.1 = ((s8[7077888]{0:T(1024)(128)(4,1)}), s8[4194304]{0:T(1024)(128)(4,1)S(1)}, s32[]{:S(2)}) async-start(s8[7077888]{0:T(1024)(128)(4,1)} %bitcast.5), calls=%async_computation.1 | async-start | bytes 8388608
  33.1 5.9 %collective-permute-start.8 = (bf16[384,256]{1,0:T(8,128)(2,1)S(1)}, bf16[384,256]{1,0:T(8,128)(2,1)S(1)}, u32[]{:S(2)}, u32[]{:S(2)}) collective-permute-start(bf16[384,256]{1,0:T(8,128)(2,1)S(1)} %get-tuple-element.47.refs_5_), channel_id=1, source_target_pairs={{0,4},{4,0},{8,12},{12,8},{1,5},{5,1},{9,13},{13,9},{2,6},{6,2},{1... | collective-permute-start | bytes 589832 | tf_op jit(solution)/shard_map/ppermute | solution.py:390
  34.8 6.9 %collective-permute-start.7 = (bf16[384,256]{1,0:T(8,128)(2,1)S(1)}, bf16[384,256]{1,0:T(8,128)(2,1)S(1)}, u32[]{:S(2)}, u32[]{:S(2)}) collective-permute-start(bf16[384,256]{1,0:T(8,128)(2,1)S(1)} %get-tuple-element.46.refs_1_), channel_id=1, source_target_pairs={{0,12},{4,8},{8,4},{12,0},{1,13},{5,9},{9,5},{13,1},{2,14},{6,10},... | collective-permute-start | bytes 589832 | tf_op jit(solution)/shard_map/ppermute | solution.py:389
  43.6 4.0 %collective-permute-start.9 = (f32[8,1024]{1,0:T(8,128)S(1)}, f32[8,1024]{1,0:T(8,128)S(1)}, u32[]{:S(2)}, u32[]{:S(2)}) collective-permute-start(f32[8,1024]{1,0:T(8,128)S(1)} %stats.1.refs_8_), channel_id=1, source_target_pairs={{0,4},{4,0},{8,12},{12,8},{1,5},{5,1},{9,13},{13,9},{2,6},{6,2},{1... | collective-permute-start | bytes 98312 | tf_op jit(solution)/shard_map/ppermute | solution.py:393
  43.7 15.6 %collective-permute-start.13 = (bf16[128,1536]{1,0:T(8,128)(2,1)S(1)}, bf16[128,1536]{1,0:T(8,128)(2,1)S(1)}, u32[]{:S(2)}, u32[]{:S(2)}) collective-permute-start(bf16[128,1536]{1,0:T(8,128)(2,1)S(1)} %bitcast.11), channel_id=1, source_target_pairs={{0,2},{1,3},{2,0},{3,1},{4,6},{5,7},{6,4},{7,5},{8,10},{9,11},{10,... | collective-permute-start | bytes 1179656 | tf_op jit(solution)/shard_map/ppermute | solution.py:387
  51.2 8.1 %collective-permute-start.11 = (bf16[384,512]{1,0:T(8,128)(2,1)S(1)}, bf16[384,512]{1,0:T(8,128)(2,1)S(1)}, u32[]{:S(2)}, u32[]{:S(2)}) collective-permute-start(bf16[384,512]{1,0:T(8,128)(2,1)S(1)} %get-tuple-element.50), channel_id=1, source_target_pairs={{0,4},{4,0},{8,12},{12,8},{1,5},{5,1},{9,13},{13,9},{2,6},{6,2},{1... | collective-permute-start | bytes 1179656 | tf_op jit(solution)/shard_map/ppermute | solution.py:395
  51.4 9.0 %collective-permute-start.12 = (bf16[384,512]{1,0:T(8,128)(2,1)S(1)}, bf16[384,512]{1,0:T(8,128)(2,1)S(1)}, u32[]{:S(2)}, u32[]{:S(2)}) collective-permute-start(bf16[384,512]{1,0:T(8,128)(2,1)S(1)} %get-tuple-element.52), channel_id=1, source_target_pairs={{0,12},{4,8},{8,4},{12,0},{1,13},{5,9},{9,5},{13,1},{2,14},{6,10},... | collective-permute-start | bytes 1179656 | tf_op jit(solution)/shard_map/ppermute | solution.py:396
  62.1 2.5 %collective-permute-start.17 = (bf16[6,48,1536]{2,1,0:T(8,128)(2,1)S(1)}, bf16[6,48,1536]{2,1,0:T(8,128)(2,1)S(1)}, u32[]{:S(2)}, u32[]{:S(2)}) collective-permute-start(bf16[6,48,1536]{2,1,0:T(8,128)(2,1)S(1)} %get-tuple-element.61), channel_id=1, source_target_pairs={{0,16},{16,0},{1,17},{17,1},{2,18},{18,2},{3,19},{19,3},{4,20},{20... | collective-permute-start | bytes 2654216 | tf_op jit(solution)/shard_map/ppermute | solution.py:405
  62.2 11.8 %collective-permute-start.15 = (bf16[768,128]{1,0:T(8,128)(2,1)S(1)}, bf16[768,128]{1,0:T(8,128)(2,1)S(1)}, u32[]{:S(2)}, u32[]{:S(2)}) collective-permute-start(bf16[768,128]{1,0:T(8,128)(2,1)S(1)} %get-tuple-element.56), channel_id=1, source_target_pairs={{0,3},{1,2},{2,1},{3,0},{4,7},{5,6},{6,5},{7,4},{8,11},{9,10},{10,... | collective-permute-start | bytes 589832 | tf_op jit(solution)/shard_map/ppermute | solution.py:400
  65.2 8.9 %collective-permute-start.18 = (bf16[6,48,384]{2,1,0:T(8,128)(2,1)S(1)}, bf16[6,48,384]{2,1,0:T(8,128)(2,1)S(1)}, u32[]{:S(2)}, u32[]{:S(2)}) collective-permute-start(bf16[6,48,384]{2,1,0:T(8,128)(2,1)S(1)} %get-tuple-element.63), channel_id=1, source_target_pairs={{0,4},{4,0},{8,12},{12,8},{1,5},{5,1},{9,13},{13,9},{2,6},{6,2},{1... | collective-permute-start | bytes 663560 | tf_op jit(solution)/shard_map/ppermute | solution.py:378
  66.0 11.7 %collective-permute-start.19 = (bf16[6,48,384]{2,1,0:T(8,128)(2,1)S(1)}, bf16[6,48,384]{2,1,0:T(8,128)(2,1)S(1)}, u32[]{:S(2)}, u32[]{:S(2)}) collective-permute-start(bf16[6,48,384]{2,1,0:T(8,128)(2,1)S(1)} %get-tuple-element.64), channel_id=1, source_target_pairs={{0,12},{4,8},{8,4},{12,0},{1,13},{5,9},{9,5},{13,1},{2,14},{6,10},... | collective-permute-start | bytes 663560 | tf_op jit(solution)/shard_map/ppermute | solution.py:378
  68.2 11.0 %collective-permute-start.20 = (bf16[6,48,384]{2,1,0:T(8,128)(2,1)S(1)}, bf16[6,48,384]{2,1,0:T(8,128)(2,1)S(1)}, u32[]{:S(2)}, u32[]{:S(2)}) collective-permute-start(bf16[6,48,384]{2,1,0:T(8,128)(2,1)S(1)} %get-tuple-element.65), channel_id=1, source_target_pairs={{0,8},{4,12},{8,0},{12,4},{1,9},{5,13},{9,1},{13,5},{2,10},{6,14},... | collective-permute-start | bytes 663560 | tf_op jit(solution)/shard_map/ppermute | solution.py:378
  69.4 26.5 %collective-permute-start.14 = (bf16[768,128]{1,0:T(8,128)(2,1)S(1)}, bf16[768,128]{1,0:T(8,128)(2,1)S(1)}, u32[]{:S(2)}, u32[]{:S(2)}) collective-permute-start(bf16[768,128]{1,0:T(8,128)(2,1)S(1)} %get-tuple-element.54), channel_id=1, source_target_pairs={{0,1},{1,0},{2,3},{3,2},{4,5},{5,4},{6,7},{7,6},{8,9},{9,8},{10,11... | collective-permute-start | bytes 589832 | tf_op jit(solution)/shard_map/ppermute | solution.py:402
  74.1 21.8 %collective-permute-start.16 = (bf16[768,128]{1,0:T(8,128)(2,1)S(1)}, bf16[768,128]{1,0:T(8,128)(2,1)S(1)}, u32[]{:S(2)}, u32[]{:S(2)}) collective-permute-start(bf16[768,128]{1,0:T(8,128)(2,1)S(1)} %get-tuple-element.57), channel_id=1, source_target_pairs={{0,2},{1,3},{2,0},{3,1},{4,6},{5,7},{6,4},{7,5},{8,10},{9,11},{10,... | collective-permute-start | bytes 589832 | tf_op jit(solution)/shard_map/ppermute | solution.py:402
  79.4 7.3 %collective-permute-start.21 = (bf16[6,48,96]{2,1,0:T(8,128)(2,1)S(1)}, bf16[6,48,96]{2,1,0:T(8,128)(2,1)S(1)}, u32[]{:S(2)}, u32[]{:S(2)}) collective-permute-start(bf16[6,48,96]{2,1,0:T(8,128)(2,1)S(1)} %get-tuple-element.67), channel_id=1, source_target_pairs={{0,1},{1,0},{2,3},{3,2},{4,5},{5,4},{6,7},{7,6},{8,9},{9,8},{10,11... | collective-permute-start | bytes 165896 | tf_op jit(solution)/shard_map/ppermute | solution.py:378
  82.5 5.3 %collective-permute-start.22 = (bf16[6,48,96]{2,1,0:T(8,128)(2,1)S(1)}, bf16[6,48,96]{2,1,0:T(8,128)(2,1)S(1)}, u32[]{:S(2)}, u32[]{:S(2)}) collective-permute-start(bf16[6,48,96]{2,1,0:T(8,128)(2,1)S(1)} %get-tuple-element.68), channel_id=1, source_target_pairs={{0,2},{1,3},{2,0},{3,1},{4,6},{5,7},{6,4},{7,5},{8,10},{9,11},{10,... | collective-permute-start | bytes 165896 | tf_op jit(solution)/shard_map/ppermute | solution.py:378
  83.0 8.1 %collective-permute-start.23 = (bf16[6,48,96]{2,1,0:T(8,128)(2,1)S(1)}, bf16[6,48,96]{2,1,0:T(8,128)(2,1)S(1)}, u32[]{:S(2)}, u32[]{:S(2)}) collective-permute-start(bf16[6,48,96]{2,1,0:T(8,128)(2,1)S(1)} %get-tuple-element.69), channel_id=1, source_target_pairs={{0,3},{1,2},{2,1},{3,0},{4,7},{5,6},{6,5},{7,4},{8,11},{9,10},{10,... | collective-permute-start | bytes 165896 | tf_op jit(solution)/shard_map/ppermute | solution.py:378
  91.3 7.6 %collective-permute-start.24 = (bf16[6,48,96]{2,1,0:T(8,128)(2,1)S(1)}, bf16[6,48,96]{2,1,0:T(8,128)(2,1)S(1)}, u32[]{:S(2)}, u32[]{:S(2)}) collective-permute-start(bf16[6,48,96]{2,1,0:T(8,128)(2,1)S(1)} %get-tuple-element.71), channel_id=1, source_target_pairs={{0,64},{64,0},{128,192},{192,128},{1,65},{65,1},{129,193},{193,129... | collective-permute-start | bytes 165896 | tf_op jit(solution)/shard_map/ppermute | solution.py:378
  93.1 6.2 %collective-permute-start.25 = (bf16[6,48,96]{2,1,0:T(8,128)(2,1)S(1)}, bf16[6,48,96]{2,1,0:T(8,128)(2,1)S(1)}, u32[]{:S(2)}, u32[]{:S(2)}) collective-permute-start(bf16[6,48,96]{2,1,0:T(8,128)(2,1)S(1)} %get-tuple-element.72), channel_id=1, source_target_pairs={{0,192},{64,128},{128,64},{192,0},{1,193},{65,129},{129,65},{193,1... | collective-permute-start | bytes 165896 | tf_op jit(solution)/shard_map/ppermute | solution.py:378
  95.2 5.9 %collective-permute-start.26 = (bf16[6,48,96]{2,1,0:T(8,128)(2,1)S(1)}, bf16[6,48,96]{2,1,0:T(8,128)(2,1)S(1)}, u32[]{:S(2)}, u32[]{:S(2)}) collective-permute-start(bf16[6,48,96]{2,1,0:T(8,128)(2,1)S(1)} %get-tuple-element.73), channel_id=1, source_target_pairs={{0,128},{64,192},{128,0},{192,64},{1,129},{65,193},{129,1},{193,65... | collective-permute-start | bytes 165896 | tf_op jit(solution)/shard_map/ppermute | solution.py:378
  101.1 7.1 %collective-permute-start.27 = (bf16[3,48,96]{2,1,0:T(8,128)(2,1)S(1)}, bf16[3,48,96]{2,1,0:T(8,128)(2,1)S(1)}, u32[]{:S(2)}, u32[]{:S(2)}) collective-permute-start(bf16[3,48,96]{2,1,0:T(8,128)(2,1)S(1)} %get-tuple-element.76), channel_id=1, source_target_pairs={{0,35},{1,34},{2,33},{3,32},{32,3},{33,2},{34,1},{35,0},{4,39},{5,... | collective-permute-start | bytes 82952 | tf_op jit(solution)/shard_map/ppermute | solution.py:428

commit v5 on v4

--- a/solution.py
+++ b/solution.py
@@ -377,13 +377,13 @@
     def spread(blocks, axis):
         return [blocks[0]] + [lax.ppermute(blocks[k], axis, exchange(k)) for k in (1, 2, 3)]
 
-    pair = lax.ppermute(tokens, "zl", near)
     middle = lax.ppermute(tokens, "zl", [(1, 2), (2, 1)])
     heads = spread(project(tokens, w_proj, d_attended[0]), "zl")
-    kv_a, qd_a = stack(heads[:2], [middle, pair])
+    kv_a, qd_a = stack(heads[:2], [middle])
     far_a, near_a = lax.ppermute(kv_a, "y", far), lax.ppermute(qd_a, "y", near)
     kv_b, qd_b = stack(heads[2:], [far_a, near_a])
     late = lax.optimization_barrier((tokens, kv_b))[0]
+    pair = lax.ppermute(late, "zl", near)
     second = lax.ppermute(late, "zl", exchange(2))
     ends = lax.ppermute(late, "zl", [(0, 3), (3, 0)])
     kv = [kv_a, kv_b, far_a, lax.ppermute(kv_b, "y", far)]

time: 109 us -> 108 us (level)
  starting transfers between devices: 43.9 us -> 42 us
    ppermute x1, waiting for transfers between devices: 0.01 us -> 2.78 us  [per_device(): pair = lax.ppermute(late, 'zl', near)]
    ppermute x1, starting transfers between devices: 3.85 us -> 5.74 us  [per_device(): got = lax.ppermute(send, ('zh', 'zl'), [(z, 7 - z) for z in range(8)])]
    ppermute x1, starting transfers between devices: 2.14 us -> 0.44 us  [per_device(): last = lax.ppermute(back[3], 'zl', exchange(3))]
    ppermute x1, waiting for transfers between devices: 0.27 us -> 1.97 us  [per_device(): got = lax.ppermute(send, 'c', swap)]
    ppermute x2, starting transfers between devices: 2.58 us -> 1.21 us  [per_device(): lax.ppermute(b, 'zl', exchange(k))]
    ppermute x1, waiting for transfers between devices: 5.72 us -> 4.37 us  [per_device(): second = lax.ppermute(late, 'zl', exchange(2))]
    ppermute x1, waiting for transfers between devices: 3.2 us -> 1.94 us  [per_device(): got = lax.ppermute(send, ('zh', 'zl'), [(z, 7 - z) for z in range(8)])]
    ppermute x1, starting transfers between devices: 0.17 us -> 1.4 us  [per_device(): qo_got = lax.ppermute(qo_send, 'y', near)]
  transfers between devices with their start and end apart: 28 -> 28, of which waited for: 18 -> 16; matrix products, arithmetic and copies ran while one was open for 0% -> 0% of each run, Pallas kernels for 14% -> 14%
where the time goes in v5:
time: 108 us
  waiting for transfers between devices  46.7 us (43%)
  starting transfers between devices  42 us (39%)
  Pallas kernels  17.2 us (16%)
    ppermute x12, waiting for transfers between devices, spread(): lax.ppermute(blocks[k], axis, exchange(k))  27.2 us
    ppermute x12, starting transfers between devices, spread(): lax.ppermute(blocks[k], axis, exchange(k))  15.9 us
    ppermute x1, starting transfers between devices, per_device(): got = lax.ppermute(send, ('zh', 'zl'), [(z, 7 - z) for z in range(8)])  5.74 us
    pallas_call x1, Pallas kernels, project(): pl.pallas_call(project_kernel, in_specs=[HBM, HBM, HBM], out_specs=[VMEM]...  5.09 us
    ppermute x1, waiting for transfers between devices, per_device(): second = lax.ppermute(late, 'zl', exchange(2))  4.37 us
    ppermute x1, starting transfers between devices, per_device(): middle = lax.ppermute(tokens, 'zl', [(1, 2), (2, 1)])  3.96 us
    pallas_call x1, Pallas kernels, attend(): pl.pallas_call(attend_kernel, in_specs=[VMEM] * (10 + len(after)), out_sh...  3.64 us
    ppermute x1, waiting for transfers between devices, per_device(): last = lax.ppermute(back[3], 'zl', exchange(3))  3.18 us
  transfers between devices with their start and end apart: 28, of which 16 were waited for; matrix products, arithmetic and copies ran while one was open for 0% of the time, Pallas kernels for 14%

profile of v5, /device:TPU:32, one launch (start us, length us, event | category | flops | bytes accessed | tf_op | source)
XLA Modules:
  0.0 107.7 jit_solution(5425415931717449110)
XLA Ops:
  0.6 4.0 %collective-permute-start.1 = (bf16[128,1536]{1,0:T(8,128)(2,1)}, bf16[128,1536]{1,0:T(8,128)(2,1)S(1)}, u32[]{:S(2)}, u32[]{:S(2)}) collective-permute-start(bf16[128,1536]{1,0:T(8,128)(2,1)} %bitcast.7), channel_id=1, source_target_pairs={{1,2},{2,1},{5,6},{6,5},{9,10},{10,9},{13,14},{14,13},{17,18},{18,... | collective-permute-start | bytes 1179656 | tf_op jit(solution)/shard_map/ppermute | solution.py:380
  4.6 0.0 slice-start
  4.6 5.1 %project.1 = (bf16[768,128]{1,0:T(8,128)(2,1)}, bf16[768,128]{1,0:T(8,128)(2,1)}, bf16[768,128]{1,0:T(8,128)(2,1)}, bf16[768,128]{1,0:T(8,128)(2,1)}) custom-call(bf16[128,1536]{1,0:T(8,128)(2,1)} %bitcast.8, bf16[1536,2304]{1,0:T(8,128)(2,1)} %weights.1, bf16[128,768]{1,0:T(8,128)(2,1)} %bitcast.14), custom_call_target="tpu_custom_call" | custom-call | tf_op jit(solution)/shard_map/project/pallas_call | solution.py:83
  9.7 0.1 collective-permute-start
  9.8 1.6 %collective-permute-start.2 = (bf16[768,128]{1,0:T(8,128)(2,1)}, bf16[768,128]{1,0:T(8,128)(2,1)S(1)}, u32[]{:S(2)}, u32[]{:S(2)}) collective-permute-start(bf16[768,128]{1,0:T(8,128)(2,1)} %get-tuple-element.43), channel_id=1, source_target_pairs={{0,2},{1,3},{2,0},{3,1},{4,6},{5,7},{6,4},{7,5},{8,10},{9,11},{10,... | collective-permute-start | bytes 589832 | tf_op jit(solution)/shard_map/ppermute | solution.py:378
  11.4 1.9 %collective-permute-start.3 = (bf16[768,128]{1,0:T(8,128)(2,1)}, bf16[768,128]{1,0:T(8,128)(2,1)S(1)}, u32[]{:S(2)}, u32[]{:S(2)}) collective-permute-start(bf16[768,128]{1,0:T(8,128)(2,1)} %get-tuple-element.44), channel_id=1, source_target_pairs={{0,3},{1,2},{2,1},{3,0},{4,7},{5,6},{6,5},{7,4},{8,11},{9,10},{10,... | collective-permute-start | bytes 589832 | tf_op jit(solution)/shard_map/ppermute | solution.py:378
  13.3 4.5 %collective-permute-done.refs_1_ = bf16[768,128]{1,0:T(8,128)(2,1)S(1)} collective-permute-done((bf16[768,128]{1,0:T(8,128)(2,1)}, bf16[768,128]{1,0:T(8,128)(2,1)S(1)}, u32[]{:S(2)}, u32[]{:S(2)}) %collective-permute-start) | collective-permute-done | bytes 196640 | tf_op jit(solution)/shard_map/ppermute | solution.py:378
  17.8 0.0 collective-permute-done.1.refs_2_.refs_3_
  17.8 0.9 copy-done.1
  18.8 0.1 stack.2
  18.8 3.1 %collective-permute-start.4 = (bf16[384,256]{1,0:T(8,128)(2,1)S(1)}, bf16[384,256]{1,0:T(8,128)(2,1)S(1)}, u32[]{:S(2)}, u32[]{:S(2)}) collective-permute-start(bf16[384,256]{1,0:T(8,128)(2,1)S(1)} %get-tuple-element.42.refs_0_), channel_id=1, source_target_pairs={{0,12},{4,8},{8,4},{12,0},{1,13},{5,9},{9,5},{13,1},{2,14},{6,10},... | collective-permute-start | bytes 589832 | tf_op jit(solution)/shard_map/ppermute | solution.py:383
  21.9 0.1 collective-permute-start.5
  22.1 5.0 %collective-permute-done.2.refs_0_ = bf16[768,128]{1,0:T(8,128)(2,1)S(1)} collective-permute-done((bf16[768,128]{1,0:T(8,128)(2,1)}, bf16[768,128]{1,0:T(8,128)(2,1)S(1)}, u32[]{:S(2)}, u32[]{:S(2)}) %collective-permute-start.2) | collective-permute-done | bytes 196640 | tf_op jit(solution)/shard_map/ppermute | solution.py:378
  27.1 3.7 %collective-permute-done.3.refs_1_ = bf16[768,128]{1,0:T(8,128)(2,1)S(1)} collective-permute-done((bf16[768,128]{1,0:T(8,128)(2,1)}, bf16[768,128]{1,0:T(8,128)(2,1)S(1)}, u32[]{:S(2)}, u32[]{:S(2)}) %collective-permute-start.3) | collective-permute-done | bytes 196640 | tf_op jit(solution)/shard_map/ppermute | solution.py:378
  30.8 0.0 collective-permute-done.4.refs_2_
  30.8 0.0 collective-permute-done.5.refs_3_.refs_6_
  30.8 0.1 stack.3
  30.9 0.7 collective-permute-start.9
  31.6 0.0 slice-start.1
  31.6 1.7 %collective-permute-start.7 = (bf16[384,256]{1,0:T(8,128)(2,1)S(1)}, bf16[384,256]{1,0:T(8,128)(2,1)S(1)}, u32[]{:S(2)}, u32[]{:S(2)}) collective-permute-start(bf16[384,256]{1,0:T(8,128)(2,1)S(1)} %get-tuple-element.47.refs_5_), channel_id=1, source_target_pairs={{0,4},{4,0},{8,12},{12,8},{1,5},{5,1},{9,13},{13,9},{2,6},{6,2},{1... | collective-permute-start | bytes 589832 | tf_op jit(solution)/shard_map/ppermute | solution.py:390
  33.2 2.2 %collective-permute-start.6 = (bf16[384,256]{1,0:T(8,128)(2,1)S(1)}, bf16[384,256]{1,0:T(8,128)(2,1)S(1)}, u32[]{:S(2)}, u32[]{:S(2)}) collective-permute-start(bf16[384,256]{1,0:T(8,128)(2,1)S(1)} %get-tuple-element.46.refs_1_), channel_id=1, source_target_pairs={{0,12},{4,8},{8,4},{12,0},{1,13},{5,9},{9,5},{13,1},{2,14},{6,10},... | collective-permute-start | bytes 589832 | tf_op jit(solution)/shard_map/ppermute | solution.py:389
  35.4 2.1 %collective-permute-done.7.refs_7_ = bf16[384,256]{1,0:T(8,128)(2,1)S(1)} collective-permute-done((bf16[384,256]{1,0:T(8,128)(2,1)S(1)}, bf16[384,256]{1,0:T(8,128)(2,1)S(1)}, u32[]{:S(2)}, u32[]{:S(2)}) %collective-permute-start.7) | collective-permute-done | bytes 196640 | tf_op jit(solution)/shard_map/ppermute | solution.py:390
  37.5 2.6 %collective-permute-done.6.refs_3_ = bf16[384,256]{1,0:T(8,128)(2,1)S(1)} collective-permute-done((bf16[384,256]{1,0:T(8,128)(2,1)S(1)}, bf16[384,256]{1,0:T(8,128)(2,1)S(1)}, u32[]{:S(2)}, u32[]{:S(2)}) %collective-permute-start.6) | collective-permute-done | bytes 196640 | tf_op jit(solution)/shard_map/ppermute | solution.py:389
  40.1 1.9 %stats.1.refs_8_ = f32[8,1024]{1,0:T(8,128)S(1)} custom-call(bf16[384,256]{1,0:T(8,128)(2,1)S(1)} %get-tuple-element.42.refs_0_, bf16[384,256]{1,0:T(8,128)(2,1)S(1)} %get-tuple-element.46.refs_1_, bf16[384,256]{1,0:T(8,128)(2,1)S(1)} %collective-permute-done.4.refs_2_, bf16[384,256]{1,0:T(8,128)(2,1)S(1)} %collective-permute-done.6.refs_3_, ...), custom_call_target="tpu_custom_call" | custom-call | tf_op jit(solution)/shard_map/stats/pallas_call | solution.py:146
  42.0 0.1 collective-permute-start.8
  42.1 2.0 %collective-permute-start.13 = (bf16[128,1536]{1,0:T(8,128)(2,1)S(1)}, bf16[128,1536]{1,0:T(8,128)(2,1)S(1)}, u32[]{:S(2)}, u32[]{:S(2)}) collective-permute-start(bf16[128,1536]{1,0:T(8,128)(2,1)S(1)} %bitcast.10), channel_id=1, source_target_pairs={{0,2},{1,3},{2,0},{3,1},{4,6},{5,7},{6,4},{7,5},{8,10},{9,11},{10,... | collective-permute-start | bytes 1179656 | tf_op jit(solution)/shard_map/ppermute | solution.py:387
  44.1 1.3 %collective-permute-start.12 = (bf16[128,1536]{1,0:T(8,128)(2,1)S(1)}, bf16[128,1536]{1,0:T(8,128)(2,1)S(1)}, u32[]{:S(2)}, u32[]{:S(2)}) collective-permute-start(bf16[128,1536]{1,0:T(8,128)(2,1)S(1)} %bitcast.11), channel_id=1, source_target_pairs={{0,1},{1,0},{2,3},{3,2},{4,5},{5,4},{6,7},{7,6},{8,9},{9,8},{10,11... | collective-permute-start | bytes 1179656 | tf_op jit(solution)/shard_map/ppermute | solution.py:386
  45.4 0.6 collective-permute-done.8.refs_9_
  46.0 0.0 collective-permute-done.9.refs_10_.refs_4_
  46.0 3.6 %attend.1 = (f32[384,512]{1,0:T(8,128)S(1)}, bf16[384,512]{1,0:T(8,128)(2,1)S(1)}, f32[384,512]{1,0:T(8,128)S(1)}, bf16[384,512]{1,0:T(8,128)(2,1)S(1)}) custom-call(bf16[384,256]{1,0:T(8,128)(2,1)S(1)} %get-tuple-element.42.refs_0_, bf16[384,256]{1,0:T(8,128)(2,1)S(1)} %get-tuple-element.46.refs_1_, bf16[384,256]{1,0:T(8,128)(2,1)S(1)} %collective-permute-done.4.refs_2_, ...), custom_call_target="tpu_custom_call" | custom-call | tf_op jit(solution)/shard_map/attend/pallas_call | solution.py:201
  49.6 1.4 %collective-permute-start.10 = (bf16[384,512]{1,0:T(8,128)(2,1)S(1)}, bf16[384,512]{1,0:T(8,128)(2,1)S(1)}, u32[]{:S(2)}, u32[]{:S(2)}) collective-permute-start(bf16[384,512]{1,0:T(8,128)(2,1)S(1)} %get-tuple-element.50), channel_id=1, source_target_pairs={{0,4},{4,0},{8,12},{12,8},{1,5},{5,1},{9,13},{13,9},{2,6},{6,2},{1... | collective-permute-start | bytes 1179656 | tf_op jit(solution)/shard_map/ppermute | solution.py:395
  51.0 2.2 %collective-permute-start.11 = (bf16[384,512]{1,0:T(8,128)(2,1)S(1)}, bf16[384,512]{1,0:T(8,128)(2,1)S(1)}, u32[]{:S(2)}, u32[]{:S(2)}) collective-permute-start(bf16[384,512]{1,0:T(8,128)(2,1)S(1)} %get-tuple-element.52), channel_id=1, source_target_pairs={{0,12},{4,8},{8,4},{12,0},{1,13},{5,9},{9,5},{13,1},{2,14},{6,10},... | collective-permute-start | bytes 1179656 | tf_op jit(solution)/shard_map/ppermute | solution.py:396
  53.2 4.4 %collective-permute-done.13.refs_2_ = bf16[128,1536]{1,0:T(8,128)(2,1)S(1)} collective-permute-done((bf16[128,1536]{1,0:T(8,128)(2,1)S(1)}, bf16[128,1536]{1,0:T(8,128)(2,1)S(1)}, u32[]{:S(2)}, u32[]{:S(2)}) %collective-permute-start.13) | collective-permute-done | bytes 393248 | tf_op jit(solution)/shard_map/ppermute | solution.py:387
  57.6 2.8 %collective-permute-done.12.refs_1_ = bf16[128,1536]{1,0:T(8,128)(2,1)S(1)} collective-permute-done((bf16[128,1536]{1,0:T(8,128)(2,1)S(1)}, bf16[128,1536]{1,0:T(8,128)(2,1)S(1)}, u32[]{:S(2)}, u32[]{:S(2)}) %collective-permute-start.12) | collective-permute-done | bytes 393248 | tf_op jit(solution)/shard_map/ppermute | solution.py:386
  60.4 1.7 %gradient.1 = (bf16[768,128]{1,0:T(8,128)(2,1)S(1)}, bf16[768,128]{1,0:T(8,128)(2,1)S(1)}, bf16[768,128]{1,0:T(8,128)(2,1)S(1)}, bf16[768,128]{1,0:T(8,128)(2,1)...) custom-call(f32[384,512]{1,0:T(8,128)S(1)} %get-tuple-element.49.qo_own, ...), custom_call_target="tpu_custom_call" | custom-call | tf_op jit(solution)/shard_map/gradient/pallas_call | solution.py:243
  62.1 0.1 collective-permute-start.17
  62.2 0.4 collective-permute-start.15
  62.7 2.0 %collective-permute-done.17.got = bf16[6,48,1536]{2,1,0:T(8,128)(2,1)S(1)} collective-permute-done((bf16[6,48,1536]{2,1,0:T(8,128)(2,1)S(1)}, bf16[6,48,1536]{2,1,0:T(8,128)(2,1)S(1)}, u32[]{:S(2)}, u32[]{:S(2)}) %collective-permute-start.17) | collective-permute-done | bytes 884768 | tf_op jit(solution)/shard_map/ppermute | solution.py:405
  64.6 0.5 split_y.1
  65.2 1.7 %collective-permute-start.18 = (bf16[6,48,384]{2,1,0:T(8,128)(2,1)S(1)}, bf16[6,48,384]{2,1,0:T(8,128)(2,1)S(1)}, u32[]{:S(2)}, u32[]{:S(2)}) collective-permute-start(bf16[6,48,384]{2,1,0:T(8,128)(2,1)S(1)} %get-tuple-element.63), channel_id=1, source_target_pairs={{0,4},{4,0},{8,12},{12,8},{1,5},{5,1},{9,13},{13,9},{2,6},{6,2},{1... | collective-permute-start | bytes 663560 | tf_op jit(solution)/shard_map/ppermute | solution.py:378
  66.9 2.2 %collective-permute-start.19 = (bf16[6,48,384]{2,1,0:T(8,128)(2,1)S(1)}, bf16[6,48,384]{2,1,0:T(8,128)(2,1)S(1)}, u32[]{:S(2)}, u32[]{:S(2)}) collective-permute-start(bf16[6,48,384]{2,1,0:T(8,128)(2,1)S(1)} %get-tuple-element.64), channel_id=1, source_target_pairs={{0,12},{4,8},{8,4},{12,0},{1,13},{5,9},{9,5},{13,1},{2,14},{6,10},... | collective-permute-start | bytes 663560 | tf_op jit(solution)/shard_map/ppermute | solution.py:378
  69.1 0.3 collective-permute-start.20
  69.4 1.2 %collective-permute-start.14 = (bf16[768,128]{1,0:T(8,128)(2,1)S(1)}, bf16[768,128]{1,0:T(8,128)(2,1)S(1)}, u32[]{:S(2)}, u32[]{:S(2)}) collective-permute-start(bf16[768,128]{1,0:T(8,128)(2,1)S(1)} %get-tuple-element.54), channel_id=1, source_target_pairs={{0,1},{1,0},{2,3},{3,2},{4,5},{5,4},{6,7},{7,6},{8,9},{9,8},{10,11... | collective-permute-start | bytes 589832 | tf_op jit(solution)/shard_map/ppermute | solution.py:402
  70.6 3.2 %collective-permute-done.15.refs_3_ = bf16[768,128]{1,0:T(8,128)(2,1)S(1)} collective-permute-done((bf16[768,128]{1,0:T(8,128)(2,1)S(1)}, bf16[768,128]{1,0:T(8,128)(2,1)S(1)}, u32[]{:S(2)}, u32[]{:S(2)}) %collective-permute-start.15) | collective-permute-done | bytes 196640 | tf_op jit(solution)/shard_map/ppermute | solution.py:400
  73.8 6.3 %collective-permute-done.19.refs_2_ = bf16[6,48,384]{2,1,0:T(8,128)(2,1)S(1)} collective-permute-done((bf16[6,48,384]{2,1,0:T(8,128)(2,1)S(1)}, bf16[6,48,384]{2,1,0:T(8,128)(2,1)S(1)}, u32[]{:S(2)}, u32[]{:S(2)}) %collective-permute-start.19) | collective-permute-done | bytes 221216 | tf_op jit(solution)/shard_map/ppermute | solution.py:378
  80.1 0.3 split_z.1
  80.3 1.3 %collective-permute-start.21 = (bf16[6,48,96]{2,1,0:T(8,128)(2,1)S(1)}, bf16[6,48,96]{2,1,0:T(8,128)(2,1)S(1)}, u32[]{:S(2)}, u32[]{:S(2)}) collective-permute-start(bf16[6,48,96]{2,1,0:T(8,128)(2,1)S(1)} %get-tuple-element.67), channel_id=1, source_target_pairs={{0,1},{1,0},{2,3},{3,2},{4,5},{5,4},{6,7},{7,6},{8,9},{9,8},{10,11... | collective-permute-start | bytes 165896 | tf_op jit(solution)/shard_map/ppermute | solution.py:378
  81.6 0.6 collective-permute-start.22
  82.2 1.7 %collective-permute-start.23 = (bf16[6,48,96]{2,1,0:T(8,128)(2,1)S(1)}, bf16[6,48,96]{2,1,0:T(8,128)(2,1)S(1)}, u32[]{:S(2)}, u32[]{:S(2)}) collective-permute-start(bf16[6,48,96]{2,1,0:T(8,128)(2,1)S(1)} %get-tuple-element.69), channel_id=1, source_target_pairs={{0,3},{1,2},{2,1},{3,0},{4,7},{5,6},{6,5},{7,4},{8,11},{9,10},{10,... | collective-permute-start | bytes 165896 | tf_op jit(solution)/shard_map/ppermute | solution.py:378
  83.9 1.4 %collective-permute-done.21.refs_1_ = bf16[6,48,96]{2,1,0:T(8,128)(2,1)S(1)} collective-permute-done((bf16[6,48,96]{2,1,0:T(8,128)(2,1)S(1)}, bf16[6,48,96]{2,1,0:T(8,128)(2,1)S(1)}, u32[]{:S(2)}, u32[]{:S(2)}) %collective-permute-start.21) | collective-permute-done | bytes 55328 | tf_op jit(solution)/shard_map/ppermute | solution.py:378
  85.4 2.5 %collective-permute-done.22.refs_2_ = bf16[6,48,96]{2,1,0:T(8,128)(2,1)S(1)} collective-permute-done((bf16[6,48,96]{2,1,0:T(8,128)(2,1)S(1)}, bf16[6,48,96]{2,1,0:T(8,128)(2,1)S(1)}, u32[]{:S(2)}, u32[]{:S(2)}) %collective-permute-start.22) | collective-permute-done | bytes 55328 | tf_op jit(solution)/shard_map/ppermute | solution.py:378
  87.9 1.6 %collective-permute-done.23.refs_3_ = bf16[6,48,96]{2,1,0:T(8,128)(2,1)S(1)} collective-permute-done((bf16[6,48,96]{2,1,0:T(8,128)(2,1)S(1)}, bf16[6,48,96]{2,1,0:T(8,128)(2,1)S(1)}, u32[]{:S(2)}, u32[]{:S(2)}) %collective-permute-start.23) | collective-permute-done | bytes 55328 | tf_op jit(solution)/shard_map/ppermute | solution.py:378
  89.4 0.2 split_x.1
  89.6 1.8 %collective-permute-start.24 = (bf16[6,48,96]{2,1,0:T(8,128)(2,1)S(1)}, bf16[6,48,96]{2,1,0:T(8,128)(2,1)S(1)}, u32[]{:S(2)}, u32[]{:S(2)}) collective-permute-start(bf16[6,48,96]{2,1,0:T(8,128)(2,1)S(1)} %get-tuple-element.71), channel_id=1, source_target_pairs={{0,64},{64,0},{128,192},{192,128},{1,65},{65,1},{129,193},{193,129... | collective-permute-start | bytes 165896 | tf_op jit(solution)/shard_map/ppermute | solution.py:378
  91.4 2.1 %collective-permute-start.25 = (bf16[6,48,96]{2,1,0:T(8,128)(2,1)S(1)}, bf16[6,48,96]{2,1,0:T(8,128)(2,1)S(1)}, u32[]{:S(2)}, u32[]{:S(2)}) collective-permute-start(bf16[6,48,96]{2,1,0:T(8,128)(2,1)S(1)} %get-tuple-element.72), channel_id=1, source_target_pairs={{0,192},{64,128},{128,64},{192,0},{1,193},{65,129},{129,65},{193,1... | collective-permute-start | bytes 165896 | tf_op jit(solution)/shard_map/ppermute | solution.py:378
  93.5 0.6 collective-permute-start.26
  94.1 0.0 collective-permute-done.14.refs_1_
  94.1 0.0 collective-permute-done.16.refs_2_
  94.2 3.1 %d_tokens.1 = (bf16[128,768]{1,0:T(8,128)(2,1)}, bf16[128,1536]{1,0:T(8,128)(2,1)}, f32[8,128]{1,0:T(8,128)S(1)}) custom-call(bf16[128,1536]{1,0:T(8,128)(2,1)S(1)} %bitcast.13, bf16[1536,2304]{1,0:T(8,128)(2,1)S(1)} %bitcast.6, bf16[768,128]{1,0:T(8,128)(2,1)S(1)} %get-tuple-element.53.refs_0_, bf16[768,128]{1,0:T(8,128)(2,1)S(1)} %collective-permute-done.14.refs_1_, ...), custom_call_target="tpu_custom_call" | custom-call | tf_op jit(solution)/shard_map/d_tokens/pallas_call | solution.py:281
  97.2 2.1 %collective-permute-done.26.refs_3_ = bf16[6,48,96]{2,1,0:T(8,128)(2,1)S(1)} collective-permute-done((bf16[6,48,96]{2,1,0:T(8,128)(2,1)S(1)}, bf16[6,48,96]{2,1,0:T(8,128)(2,1)S(1)}, u32[]{:S(2)}, u32[]{:S(2)}) %collective-permute-start.26) | collective-permute-done | bytes 55328 | tf_op jit(solution)/shard_map/ppermute | solution.py:378
  99.4 0.1 split_zh.1
  99.4 5.7 %collective-permute-start.27 = (bf16[3,48,96]{2,1,0:T(8,128)(2,1)S(1)}, bf16[3,48,96]{2,1,0:T(8,128)(2,1)S(1)}, u32[]{:S(2)}, u32[]{:S(2)}) collective-permute-start(bf16[3,48,96]{2,1,0:T(8,128)(2,1)S(1)} %get-tuple-element.76), channel_id=1, source_target_pairs={{0,35},{1,34},{2,33},{3,32},{32,3},{33,2},{34,1},{35,0},{4,39},{5,... | collective-permute-start | bytes 82952 | tf_op jit(solution)/shard_map/ppermute | solution.py:428
  105.2 1.9 %collective-permute-done.27.got = bf16[3,48,96]{2,1,0:T(8,128)(2,1)S(1)} collective-permute-done((bf16[3,48,96]{2,1,0:T(8,128)(2,1)S(1)}, bf16[3,48,96]{2,1,0:T(8,128)(2,1)S(1)}, u32[]{:S(2)}, u32[]{:S(2)}) %collective-permute-start.27) | collective-permute-done | bytes 27680 | tf_op jit(solution)/shard_map/ppermute | solution.py:428
  107.1 0.6 finish.1
  (13 shorter events, 0.0 us)
Async XLA Ops:
  0.6 30.2 %copy-start = (bf16[1,128,1536]{2,1,0:T(8,128)(2,1)S(1)}, bf16[1,128,1536]{2,1,0:T(8,128)(2,1)}, u32[]{:S(2)}) copy-start(bf16[1,128,1536]{2,1,0:T(8,128)(2,1)} %param.3) | copy-start | bytes 1179652
  0.6 17.2 %collective-permute-start.1 = (bf16[128,1536]{1,0:T(8,128)(2,1)}, bf16[128,1536]{1,0:T(8,128)(2,1)S(1)}, u32[]{:S(2)}, u32[]{:S(2)}) collective-permute-start(bf16[128,1536]{1,0:T(8,128)(2,1)} %bitcast.7), channel_id=1, source_target_pairs={{1,2},{2,1},{5,6},{6,5},{9,10},{10,9},{13,14},{14,13},{17,18},{18,... | collective-permute-start | bytes 1179656 | tf_op jit(solution)/shard_map/ppermute | solution.py:380
  4.6 89.5 %slice-start = ((s8[7077888]{0:T(1024)(128)(4,1)}), s8[2883584]{0:T(1024)(128)(4,1)S(1)}, s32[]{:S(2)}) async-start(s8[7077888]{0:T(1024)(128)(4,1)} %bitcast.5), calls=%async_computation | async-start | bytes 5767168
  9.7 8.1 %collective-permute-start = (bf16[768,128]{1,0:T(8,128)(2,1)}, bf16[768,128]{1,0:T(8,128)(2,1)S(1)}, u32[]{:S(2)}, u32[]{:S(2)}) collective-permute-start(bf16[768,128]{1,0:T(8,128)(2,1)} %get-tuple-element.41), channel_id=1, source_target_pairs={{0,1},{1,0},{2,3},{3,2},{4,5},{5,4},{6,7},{7,6},{8,9},{9,8},{10,11... | collective-permute-start | bytes 589832 | tf_op jit(solution)/shard_map/ppermute | solution.py:378
  9.8 17.2 %collective-permute-start.2 = (bf16[768,128]{1,0:T(8,128)(2,1)}, bf16[768,128]{1,0:T(8,128)(2,1)S(1)}, u32[]{:S(2)}, u32[]{:S(2)}) collective-permute-start(bf16[768,128]{1,0:T(8,128)(2,1)} %get-tuple-element.43), channel_id=1, source_target_pairs={{0,2},{1,3},{2,0},{3,1},{4,6},{5,7},{6,4},{7,5},{8,10},{9,11},{10,... | collective-permute-start | bytes 589832 | tf_op jit(solution)/shard_map/ppermute | solution.py:378
  11.4 19.4 %collective-permute-start.3 = (bf16[768,128]{1,0:T(8,128)(2,1)}, bf16[768,128]{1,0:T(8,128)(2,1)S(1)}, u32[]{:S(2)}, u32[]{:S(2)}) collective-permute-start(bf16[768,128]{1,0:T(8,128)(2,1)} %get-tuple-element.44), channel_id=1, source_target_pairs={{0,3},{1,2},{2,1},{3,0},{4,7},{5,6},{6,5},{7,4},{8,11},{9,10},{10,... | collective-permute-start | bytes 589832 | tf_op jit(solution)/shard_map/ppermute | solution.py:378
  17.8 0.9 copy-start.1
  18.8 11.9 %collective-permute-start.4 = (bf16[384,256]{1,0:T(8,128)(2,1)S(1)}, bf16[384,256]{1,0:T(8,128)(2,1)S(1)}, u32[]{:S(2)}, u32[]{:S(2)}) collective-permute-start(bf16[384,256]{1,0:T(8,128)(2,1)S(1)} %get-tuple-element.42.refs_0_), channel_id=1, source_target_pairs={{0,12},{4,8},{8,4},{12,0},{1,13},{5,9},{9,5},{13,1},{2,14},{6,10},... | collective-permute-start | bytes 589832 | tf_op jit(solution)/shard_map/ppermute | solution.py:383
  21.9 8.8 %collective-permute-start.5 = (bf16[384,256]{1,0:T(8,128)(2,1)S(1)}, bf16[384,256]{1,0:T(8,128)(2,1)S(1)}, u32[]{:S(2)}, u32[]{:S(2)}) collective-permute-start(bf16[384,256]{1,0:T(8,128)(2,1)S(1)} %get-tuple-element.45.refs_4_), channel_id=1, source_target_pairs={{0,4},{4,0},{8,12},{12,8},{1,5},{5,1},{9,13},{13,9},{2,6},{6,2},{1... | collective-permute-start | bytes 589832 | tf_op jit(solution)/shard_map/ppermute | solution.py:383
  30.9 15.1 %collective-permute-start.9 = (bf16[128,1536]{1,0:T(8,128)(2,1)S(1)}, bf16[128,1536]{1,0:T(8,128)(2,1)S(1)}, u32[]{:S(2)}, u32[]{:S(2)}) collective-permute-start(bf16[128,1536]{1,0:T(8,128)(2,1)S(1)} %bitcast.9), channel_id=1, source_target_pairs={{0,3},{3,0},{4,7},{7,4},{8,11},{11,8},{12,15},{15,12},{16,19},{19,... | collective-permute-start | bytes 1179656 | tf_op jit(solution)/shard_map/ppermute | solution.py:388
  31.6 62.6 %slice-start.1 = ((s8[7077888]{0:T(1024)(128)(4,1)}), s8[4194304]{0:T(1024)(128)(4,1)S(1)}, s32[]{:S(2)}) async-start(s8[7077888]{0:T(1024)(128)(4,1)} %bitcast.5), calls=%async_computation.1 | async-start | bytes 8388608
  31.6 5.9 %collective-permute-start.7 = (bf16[384,256]{1,0:T(8,128)(2,1)S(1)}, bf16[384,256]{1,0:T(8,128)(2,1)S(1)}, u32[]{:S(2)}, u32[]{:S(2)}) collective-permute-start(bf16[384,256]{1,0:T(8,128)(2,1)S(1)} %get-tuple-element.47.refs_5_), channel_id=1, source_target_pairs={{0,4},{4,0},{8,12},{12,8},{1,5},{5,1},{9,13},{13,9},{2,6},{6,2},{1... | collective-permute-start | bytes 589832 | tf_op jit(solution)/shard_map/ppermute | solution.py:390
  33.2 6.9 %collective-permute-start.6 = (bf16[384,256]{1,0:T(8,128)(2,1)S(1)}, bf16[384,256]{1,0:T(8,128)(2,1)S(1)}, u32[]{:S(2)}, u32[]{:S(2)}) collective-permute-start(bf16[384,256]{1,0:T(8,128)(2,1)S(1)} %get-tuple-element.46.refs_1_), channel_id=1, source_target_pairs={{0,12},{4,8},{8,4},{12,0},{1,13},{5,9},{9,5},{13,1},{2,14},{6,10},... | collective-permute-start | bytes 589832 | tf_op jit(solution)/shard_map/ppermute | solution.py:389
  42.0 4.0 %collective-permute-start.8 = (f32[8,1024]{1,0:T(8,128)S(1)}, f32[8,1024]{1,0:T(8,128)S(1)}, u32[]{:S(2)}, u32[]{:S(2)}) collective-permute-start(f32[8,1024]{1,0:T(8,128)S(1)} %stats.1.refs_8_), channel_id=1, source_target_pairs={{0,4},{4,0},{8,12},{12,8},{1,5},{5,1},{9,13},{13,9},{2,6},{6,2},{1... | collective-permute-start | bytes 98312 | tf_op jit(solution)/shard_map/ppermute | solution.py:393
  42.1 15.5 %collective-permute-start.13 = (bf16[128,1536]{1,0:T(8,128)(2,1)S(1)}, bf16[128,1536]{1,0:T(8,128)(2,1)S(1)}, u32[]{:S(2)}, u32[]{:S(2)}) collective-permute-start(bf16[128,1536]{1,0:T(8,128)(2,1)S(1)} %bitcast.10), channel_id=1, source_target_pairs={{0,2},{1,3},{2,0},{3,1},{4,6},{5,7},{6,4},{7,5},{8,10},{9,11},{10,... | collective-permute-start | bytes 1179656 | tf_op jit(solution)/shard_map/ppermute | solution.py:387
  44.1 16.3 %collective-permute-start.12 = (bf16[128,1536]{1,0:T(8,128)(2,1)S(1)}, bf16[128,1536]{1,0:T(8,128)(2,1)S(1)}, u32[]{:S(2)}, u32[]{:S(2)}) collective-permute-start(bf16[128,1536]{1,0:T(8,128)(2,1)S(1)} %bitcast.11), channel_id=1, source_target_pairs={{0,1},{1,0},{2,3},{3,2},{4,5},{5,4},{6,7},{7,6},{8,9},{9,8},{10,11... | collective-permute-start | bytes 1179656 | tf_op jit(solution)/shard_map/ppermute | solution.py:386
  49.6 10.7 %collective-permute-start.10 = (bf16[384,512]{1,0:T(8,128)(2,1)S(1)}, bf16[384,512]{1,0:T(8,128)(2,1)S(1)}, u32[]{:S(2)}, u32[]{:S(2)}) collective-permute-start(bf16[384,512]{1,0:T(8,128)(2,1)S(1)} %get-tuple-element.50), channel_id=1, source_target_pairs={{0,4},{4,0},{8,12},{12,8},{1,5},{5,1},{9,13},{13,9},{2,6},{6,2},{1... | collective-permute-start | bytes 1179656 | tf_op jit(solution)/shard_map/ppermute | solution.py:395
  51.0 9.3 %collective-permute-start.11 = (bf16[384,512]{1,0:T(8,128)(2,1)S(1)}, bf16[384,512]{1,0:T(8,128)(2,1)S(1)}, u32[]{:S(2)}, u32[]{:S(2)}) collective-permute-start(bf16[384,512]{1,0:T(8,128)(2,1)S(1)} %get-tuple-element.52), channel_id=1, source_target_pairs={{0,12},{4,8},{8,4},{12,0},{1,13},{5,9},{9,5},{13,1},{2,14},{6,10},... | collective-permute-start | bytes 1179656 | tf_op jit(solution)/shard_map/ppermute | solution.py:396
  62.1 2.5 %collective-permute-start.17 = (bf16[6,48,1536]{2,1,0:T(8,128)(2,1)S(1)}, bf16[6,48,1536]{2,1,0:T(8,128)(2,1)S(1)}, u32[]{:S(2)}, u32[]{:S(2)}) collective-permute-start(bf16[6,48,1536]{2,1,0:T(8,128)(2,1)S(1)} %get-tuple-element.61), channel_id=1, source_target_pairs={{0,16},{16,0},{1,17},{17,1},{2,18},{18,2},{3,19},{19,3},{4,20},{20... | collective-permute-start | bytes 2654216 | tf_op jit(solution)/shard_map/ppermute | solution.py:405
  62.2 11.5 %collective-permute-start.15 = (bf16[768,128]{1,0:T(8,128)(2,1)S(1)}, bf16[768,128]{1,0:T(8,128)(2,1)S(1)}, u32[]{:S(2)}, u32[]{:S(2)}) collective-permute-start(bf16[768,128]{1,0:T(8,128)(2,1)S(1)} %get-tuple-element.56), channel_id=1, source_target_pairs={{0,3},{1,2},{2,1},{3,0},{4,7},{5,6},{6,5},{7,4},{8,11},{9,10},{10,... | collective-permute-start | bytes 589832 | tf_op jit(solution)/shard_map/ppermute | solution.py:400
  65.2 8.6 %collective-permute-start.18 = (bf16[6,48,384]{2,1,0:T(8,128)(2,1)S(1)}, bf16[6,48,384]{2,1,0:T(8,128)(2,1)S(1)}, u32[]{:S(2)}, u32[]{:S(2)}) collective-permute-start(bf16[6,48,384]{2,1,0:T(8,128)(2,1)S(1)} %get-tuple-element.63), channel_id=1, source_target_pairs={{0,4},{4,0},{8,12},{12,8},{1,5},{5,1},{9,13},{13,9},{2,6},{6,2},{1... | collective-permute-start | bytes 663560 | tf_op jit(solution)/shard_map/ppermute | solution.py:378
  66.9 13.1 %collective-permute-start.19 = (bf16[6,48,384]{2,1,0:T(8,128)(2,1)S(1)}, bf16[6,48,384]{2,1,0:T(8,128)(2,1)S(1)}, u32[]{:S(2)}, u32[]{:S(2)}) collective-permute-start(bf16[6,48,384]{2,1,0:T(8,128)(2,1)S(1)} %get-tuple-element.64), channel_id=1, source_target_pairs={{0,12},{4,8},{8,4},{12,0},{1,13},{5,9},{9,5},{13,1},{2,14},{6,10},... | collective-permute-start | bytes 663560 | tf_op jit(solution)/shard_map/ppermute | solution.py:378
  69.1 11.0 %collective-permute-start.20 = (bf16[6,48,384]{2,1,0:T(8,128)(2,1)S(1)}, bf16[6,48,384]{2,1,0:T(8,128)(2,1)S(1)}, u32[]{:S(2)}, u32[]{:S(2)}) collective-permute-start(bf16[6,48,384]{2,1,0:T(8,128)(2,1)S(1)} %get-tuple-element.65), channel_id=1, source_target_pairs={{0,8},{4,12},{8,0},{12,4},{1,9},{5,13},{9,1},{13,5},{2,10},{6,14},... | collective-permute-start | bytes 663560 | tf_op jit(solution)/shard_map/ppermute | solution.py:378
  69.4 24.8 %collective-permute-start.14 = (bf16[768,128]{1,0:T(8,128)(2,1)S(1)}, bf16[768,128]{1,0:T(8,128)(2,1)S(1)}, u32[]{:S(2)}, u32[]{:S(2)}) collective-permute-start(bf16[768,128]{1,0:T(8,128)(2,1)S(1)} %get-tuple-element.54), channel_id=1, source_target_pairs={{0,1},{1,0},{2,3},{3,2},{4,5},{5,4},{6,7},{7,6},{8,9},{9,8},{10,11... | collective-permute-start | bytes 589832 | tf_op jit(solution)/shard_map/ppermute | solution.py:402
  73.8 20.4 %collective-permute-start.16 = (bf16[768,128]{1,0:T(8,128)(2,1)S(1)}, bf16[768,128]{1,0:T(8,128)(2,1)S(1)}, u32[]{:S(2)}, u32[]{:S(2)}) collective-permute-start(bf16[768,128]{1,0:T(8,128)(2,1)S(1)} %get-tuple-element.57), channel_id=1, source_target_pairs={{0,2},{1,3},{2,0},{3,1},{4,6},{5,7},{6,4},{7,5},{8,10},{9,11},{10,... | collective-permute-start | bytes 589832 | tf_op jit(solution)/shard_map/ppermute | solution.py:402
  80.3 5.0 %collective-permute-start.21 = (bf16[6,48,96]{2,1,0:T(8,128)(2,1)S(1)}, bf16[6,48,96]{2,1,0:T(8,128)(2,1)S(1)}, u32[]{:S(2)}, u32[]{:S(2)}) collective-permute-start(bf16[6,48,96]{2,1,0:T(8,128)(2,1)S(1)} %get-tuple-element.67), channel_id=1, source_target_pairs={{0,1},{1,0},{2,3},{3,2},{4,5},{5,4},{6,7},{7,6},{8,9},{9,8},{10,11... | collective-permute-start | bytes 165896 | tf_op jit(solution)/shard_map/ppermute | solution.py:378
  81.6 6.2 %collective-permute-start.22 = (bf16[6,48,96]{2,1,0:T(8,128)(2,1)S(1)}, bf16[6,48,96]{2,1,0:T(8,128)(2,1)S(1)}, u32[]{:S(2)}, u32[]{:S(2)}) collective-permute-start(bf16[6,48,96]{2,1,0:T(8,128)(2,1)S(1)} %get-tuple-element.68), channel_id=1, source_target_pairs={{0,2},{1,3},{2,0},{3,1},{4,6},{5,7},{6,4},{7,5},{8,10},{9,11},{10,... | collective-permute-start | bytes 165896 | tf_op jit(solution)/shard_map/ppermute | solution.py:378
  82.2 7.2 %collective-permute-start.23 = (bf16[6,48,96]{2,1,0:T(8,128)(2,1)S(1)}, bf16[6,48,96]{2,1,0:T(8,128)(2,1)S(1)}, u32[]{:S(2)}, u32[]{:S(2)}) collective-permute-start(bf16[6,48,96]{2,1,0:T(8,128)(2,1)S(1)} %get-tuple-element.69), channel_id=1, source_target_pairs={{0,3},{1,2},{2,1},{3,0},{4,7},{5,6},{6,5},{7,4},{8,11},{9,10},{10,... | collective-permute-start | bytes 165896 | tf_op jit(solution)/shard_map/ppermute | solution.py:378
  89.6 7.6 %collective-permute-start.24 = (bf16[6,48,96]{2,1,0:T(8,128)(2,1)S(1)}, bf16[6,48,96]{2,1,0:T(8,128)(2,1)S(1)}, u32[]{:S(2)}, u32[]{:S(2)}) collective-permute-start(bf16[6,48,96]{2,1,0:T(8,128)(2,1)S(1)} %get-tuple-element.71), channel_id=1, source_target_pairs={{0,64},{64,0},{128,192},{192,128},{1,65},{65,1},{129,193},{193,129... | collective-permute-start | bytes 165896 | tf_op jit(solution)/shard_map/ppermute | solution.py:378
  91.4 5.8 %collective-permute-start.25 = (bf16[6,48,96]{2,1,0:T(8,128)(2,1)S(1)}, bf16[6,48,96]{2,1,0:T(8,128)(2,1)S(1)}, u32[]{:S(2)}, u32[]{:S(2)}) collective-permute-start(bf16[6,48,96]{2,1,0:T(8,128)(2,1)S(1)} %get-tuple-element.72), channel_id=1, source_target_pairs={{0,192},{64,128},{128,64},{192,0},{1,193},{65,129},{129,65},{193,1... | collective-permute-start | bytes 165896 | tf_op jit(solution)/shard_map/ppermute | solution.py:378
  93.5 5.9 %collective-permute-start.26 = (bf16[6,48,96]{2,1,0:T(8,128)(2,1)S(1)}, bf16[6,48,96]{2,1,0:T(8,128)(2,1)S(1)}, u32[]{:S(2)}, u32[]{:S(2)}) collective-permute-start(bf16[6,48,96]{2,1,0:T(8,128)(2,1)S(1)} %get-tuple-element.73), channel_id=1, source_target_pairs={{0,128},{64,192},{128,0},{192,64},{1,129},{65,193},{129,1},{193,65... | collective-permute-start | bytes 165896 | tf_op jit(solution)/shard_map/ppermute | solution.py:378
  99.4 7.7 %collective-permute-start.27 = (bf16[3,48,96]{2,1,0:T(8,128)(2,1)S(1)}, bf16[3,48,96]{2,1,0:T(8,128)(2,1)S(1)}, u32[]{:S(2)}, u32[]{:S(2)}) collective-permute-start(bf16[3,48,96]{2,1,0:T(8,128)(2,1)S(1)} %get-tuple-element.76), channel_id=1, source_target_pairs={{0,35},{1,34},{2,33},{3,32},{32,3},{33,2},{34,1},{35,0},{4,39},{5,... | collective-permute-start | bytes 82952 | tf_op jit(solution)/shard_map/ppermute | solution.py:428

commit v6 on v5

--- a/solution.py
+++ b/solution.py
@@ -344,10 +344,13 @@
     return list(zip(*tables))
 
 
+FAR_FIRST = (0, 3, 2, 1)
+
+
 def split_x_kernel(*refs):
     blocks, outs, by_head, cut = refs[:4], refs[4:8], refs[8], refs[9]
     for k in range(4):
-        by_head[place[0] ^ k] = blocks[k][...]
+        by_head[place[0] ^ FAR_FIRST[k]] = blocks[k][...]
     for slot, (first, second) in enumerate(lists()):
         head, at = (jnp.where(place[2] == 0, a, b) for a, b in zip(first, second))
         cut[slot] = by_head[head, at]
@@ -408,19 +411,20 @@
         [shape((6, 48, 384))] * 4, [pltpu.VMEM((6, 48, D), BF)],
     )
     blocks = spread(blocks, "y")
-    blocks = [blocks[k] for k in (0, 1, 3, 2)]
+    blocks = [blocks[k] for k in (0, 2, 1, 3)]
     blocks = small(
         split_z_kernel, "split_z", blocks,
         [shape((6, 48, 96))] * 4, [pltpu.VMEM((4, 6, 48, 96), BF)],
     )
     blocks = spread(blocks, "zl")
+    blocks = [blocks[k] for k in FAR_FIRST]
     blocks = small(
         split_x_kernel, "split_x", blocks,
         [shape((6, 48, 96))] * 4,
         [pltpu.VMEM((4, 6, 48, 96), BF), pltpu.VMEM((24, 48, 96), BF)],
     )
     blocks = spread(blocks, "x")
-    blocks = [blocks[k] for k in (0, 1, 3, 2)]
+    blocks = [blocks[k] for k in (0, 2, 1, 3)]
     keep, send = small(
         split_zh_kernel, "split_zh", blocks,
         [shape((3, 48, 96), F32), shape((3, 48, 96))], [pltpu.VMEM((6, 48, 96), F32)], [done],

time: 108 us -> 108 us (level); the launches traced: 108 us -> 107 us
  waiting for transfers between devices: 46.7 us -> 45.4 us
    ppermute x12, waiting for transfers between devices: 27.2 us -> 26.1 us  [spread(): lax.ppermute(blocks[k], axis, exchange(k))]
  transfers between devices with their start and end apart: 28 -> 28, of which waited for: 16 -> 17; matrix products, arithmetic and copies ran while one was open for 0% -> 0% of each run, Pallas kernels for 14% -> 14%
where the time goes in v6:
time: 108 us; the launch traced here: 107 us
  waiting for transfers between devices  45.4 us (42%)
  starting transfers between devices  42.2 us (39%)
  Pallas kernels  17.2 us (16%)
    ppermute x12, waiting for transfers between devices, spread(): lax.ppermute(blocks[k], axis, exchange(k))  26.1 us
    ppermute x12, starting transfers between devices, spread(): lax.ppermute(blocks[k], axis, exchange(k))  16.1 us
    ppermute x1, starting transfers between devices, per_device(): got = lax.ppermute(send, ('zh', 'zl'), [(z, 7 - z) for z in range(8)])  5.69 us
    pallas_call x1, Pallas kernels, project(): pl.pallas_call(project_kernel, in_specs=[HBM, HBM, HBM], out_specs=[VMEM]...  5.09 us
    ppermute x1, waiting for transfers between devices, per_device(): second = lax.ppermute(late, 'zl', exchange(2))  4.37 us
    ppermute x1, starting transfers between devices, per_device(): middle = lax.ppermute(tokens, 'zl', [(1, 2), (2, 1)])  3.96 us
    pallas_call x1, Pallas kernels, attend(): pl.pallas_call(attend_kernel, in_specs=[VMEM] * (10 + len(after)), out_sh...  3.64 us
    ppermute x1, starting transfers between devices, per_device(): lax.ppermute(kv_a, 'y', far)  3.1 us
  transfers between devices with their start and end apart: 28, of which 17 were waited for; matrix products, arithmetic and copies ran while one was open for 0% of the time, Pallas kernels for 14%

profile of v6, /device:TPU:32, one launch (start us, length us, event | category | flops | bytes accessed | tf_op | source)
XLA Modules:
  0.0 106.6 jit_solution(4265966628020874095)
XLA Ops:
  0.6 4.0 %collective-permute-start.1 = (bf16[128,1536]{1,0:T(8,128)(2,1)}, bf16[128,1536]{1,0:T(8,128)(2,1)S(1)}, u32[]{:S(2)}, u32[]{:S(2)}) collective-permute-start(bf16[128,1536]{1,0:T(8,128)(2,1)} %bitcast.7), channel_id=1, source_target_pairs={{1,2},{2,1},{5,6},{6,5},{9,10},{10,9},{13,14},{14,13},{17,18},{18,... | collective-permute-start | bytes 1179656 | tf_op jit(solution)/shard_map/ppermute | solution.py:383
  4.6 0.0 slice-start
  4.6 5.1 %project.1 = (bf16[768,128]{1,0:T(8,128)(2,1)}, bf16[768,128]{1,0:T(8,128)(2,1)}, bf16[768,128]{1,0:T(8,128)(2,1)}, bf16[768,128]{1,0:T(8,128)(2,1)}) custom-call(bf16[128,1536]{1,0:T(8,128)(2,1)} %bitcast.8, bf16[1536,2304]{1,0:T(8,128)(2,1)} %weights.1, bf16[128,768]{1,0:T(8,128)(2,1)} %bitcast.14), custom_call_target="tpu_custom_call" | custom-call | tf_op jit(solution)/shard_map/project/pallas_call | solution.py:83
  9.7 0.1 collective-permute-start
  9.8 1.6 %collective-permute-start.2 = (bf16[768,128]{1,0:T(8,128)(2,1)}, bf16[768,128]{1,0:T(8,128)(2,1)S(1)}, u32[]{:S(2)}, u32[]{:S(2)}) collective-permute-start(bf16[768,128]{1,0:T(8,128)(2,1)} %get-tuple-element.43), channel_id=1, source_target_pairs={{0,2},{1,3},{2,0},{3,1},{4,6},{5,7},{6,4},{7,5},{8,10},{9,11},{10,... | collective-permute-start | bytes 589832 | tf_op jit(solution)/shard_map/ppermute | solution.py:381
  11.4 1.9 %collective-permute-start.3 = (bf16[768,128]{1,0:T(8,128)(2,1)}, bf16[768,128]{1,0:T(8,128)(2,1)S(1)}, u32[]{:S(2)}, u32[]{:S(2)}) collective-permute-start(bf16[768,128]{1,0:T(8,128)(2,1)} %get-tuple-element.44), channel_id=1, source_target_pairs={{0,3},{1,2},{2,1},{3,0},{4,7},{5,6},{6,5},{7,4},{8,11},{9,10},{10,... | collective-permute-start | bytes 589832 | tf_op jit(solution)/shard_map/ppermute | solution.py:381
  13.3 4.5 %collective-permute-done.refs_1_ = bf16[768,128]{1,0:T(8,128)(2,1)S(1)} collective-permute-done((bf16[768,128]{1,0:T(8,128)(2,1)}, bf16[768,128]{1,0:T(8,128)(2,1)S(1)}, u32[]{:S(2)}, u32[]{:S(2)}) %collective-permute-start) | collective-permute-done | bytes 196640 | tf_op jit(solution)/shard_map/ppermute | solution.py:381
  17.8 0.0 collective-permute-done.1.refs_2_.refs_3_
  17.8 0.9 copy-done.1
  18.8 0.1 stack.2
  18.8 3.1 %collective-permute-start.4 = (bf16[384,256]{1,0:T(8,128)(2,1)S(1)}, bf16[384,256]{1,0:T(8,128)(2,1)S(1)}, u32[]{:S(2)}, u32[]{:S(2)}) collective-permute-start(bf16[384,256]{1,0:T(8,128)(2,1)S(1)} %get-tuple-element.42.refs_0_), channel_id=1, source_target_pairs={{0,12},{4,8},{8,4},{12,0},{1,13},{5,9},{9,5},{13,1},{2,14},{6,10},... | collective-permute-start | bytes 589832 | tf_op jit(solution)/shard_map/ppermute | solution.py:386
  21.9 0.1 collective-permute-start.5
  22.1 5.0 %collective-permute-done.2.refs_0_ = bf16[768,128]{1,0:T(8,128)(2,1)S(1)} collective-permute-done((bf16[768,128]{1,0:T(8,128)(2,1)}, bf16[768,128]{1,0:T(8,128)(2,1)S(1)}, u32[]{:S(2)}, u32[]{:S(2)}) %collective-permute-start.2) | collective-permute-done | bytes 196640 | tf_op jit(solution)/shard_map/ppermute | solution.py:381
  27.1 3.7 %collective-permute-done.3.refs_1_ = bf16[768,128]{1,0:T(8,128)(2,1)S(1)} collective-permute-done((bf16[768,128]{1,0:T(8,128)(2,1)}, bf16[768,128]{1,0:T(8,128)(2,1)S(1)}, u32[]{:S(2)}, u32[]{:S(2)}) %collective-permute-start.3) | collective-permute-done | bytes 196640 | tf_op jit(solution)/shard_map/ppermute | solution.py:381
  30.8 0.0 collective-permute-done.4.refs_2_
  30.8 0.0 collective-permute-done.5.refs_3_.refs_6_
  30.8 0.1 stack.3
  30.9 0.7 collective-permute-start.9
  31.6 0.0 slice-start.1
  31.6 1.7 %collective-permute-start.7 = (bf16[384,256]{1,0:T(8,128)(2,1)S(1)}, bf16[384,256]{1,0:T(8,128)(2,1)S(1)}, u32[]{:S(2)}, u32[]{:S(2)}) collective-permute-start(bf16[384,256]{1,0:T(8,128)(2,1)S(1)} %get-tuple-element.47.refs_5_), channel_id=1, source_target_pairs={{0,4},{4,0},{8,12},{12,8},{1,5},{5,1},{9,13},{13,9},{2,6},{6,2},{1... | collective-permute-start | bytes 589832 | tf_op jit(solution)/shard_map/ppermute | solution.py:393
  33.2 2.2 %collective-permute-start.6 = (bf16[384,256]{1,0:T(8,128)(2,1)S(1)}, bf16[384,256]{1,0:T(8,128)(2,1)S(1)}, u32[]{:S(2)}, u32[]{:S(2)}) collective-permute-start(bf16[384,256]{1,0:T(8,128)(2,1)S(1)} %get-tuple-element.46.refs_1_), channel_id=1, source_target_pairs={{0,12},{4,8},{8,4},{12,0},{1,13},{5,9},{9,5},{13,1},{2,14},{6,10},... | collective-permute-start | bytes 589832 | tf_op jit(solution)/shard_map/ppermute | solution.py:392
  35.4 2.1 %collective-permute-done.7.refs_7_ = bf16[384,256]{1,0:T(8,128)(2,1)S(1)} collective-permute-done((bf16[384,256]{1,0:T(8,128)(2,1)S(1)}, bf16[384,256]{1,0:T(8,128)(2,1)S(1)}, u32[]{:S(2)}, u32[]{:S(2)}) %collective-permute-start.7) | collective-permute-done | bytes 196640 | tf_op jit(solution)/shard_map/ppermute | solution.py:393
  37.5 2.6 %collective-permute-done.6.refs_3_ = bf16[384,256]{1,0:T(8,128)(2,1)S(1)} collective-permute-done((bf16[384,256]{1,0:T(8,128)(2,1)S(1)}, bf16[384,256]{1,0:T(8,128)(2,1)S(1)}, u32[]{:S(2)}, u32[]{:S(2)}) %collective-permute-start.6) | collective-permute-done | bytes 196640 | tf_op jit(solution)/shard_map/ppermute | solution.py:392
  40.1 1.9 %stats.1.refs_8_ = f32[8,1024]{1,0:T(8,128)S(1)} custom-call(bf16[384,256]{1,0:T(8,128)(2,1)S(1)} %get-tuple-element.42.refs_0_, bf16[384,256]{1,0:T(8,128)(2,1)S(1)} %get-tuple-element.46.refs_1_, bf16[384,256]{1,0:T(8,128)(2,1)S(1)} %collective-permute-done.4.refs_2_, bf16[384,256]{1,0:T(8,128)(2,1)S(1)} %collective-permute-done.6.refs_3_, ...), custom_call_target="tpu_custom_call" | custom-call | tf_op jit(solution)/shard_map/stats/pallas_call | solution.py:146
  42.0 0.1 collective-permute-start.8
  42.1 2.0 %collective-permute-start.13 = (bf16[128,1536]{1,0:T(8,128)(2,1)S(1)}, bf16[128,1536]{1,0:T(8,128)(2,1)S(1)}, u32[]{:S(2)}, u32[]{:S(2)}) collective-permute-start(bf16[128,1536]{1,0:T(8,128)(2,1)S(1)} %bitcast.10), channel_id=1, source_target_pairs={{0,2},{1,3},{2,0},{3,1},{4,6},{5,7},{6,4},{7,5},{8,10},{9,11},{10,... | collective-permute-start | bytes 1179656 | tf_op jit(solution)/shard_map/ppermute | solution.py:390
  44.1 1.3 %collective-permute-start.12 = (bf16[128,1536]{1,0:T(8,128)(2,1)S(1)}, bf16[128,1536]{1,0:T(8,128)(2,1)S(1)}, u32[]{:S(2)}, u32[]{:S(2)}) collective-permute-start(bf16[128,1536]{1,0:T(8,128)(2,1)S(1)} %bitcast.11), channel_id=1, source_target_pairs={{0,1},{1,0},{2,3},{3,2},{4,5},{5,4},{6,7},{7,6},{8,9},{9,8},{10,11... | collective-permute-start | bytes 1179656 | tf_op jit(solution)/shard_map/ppermute | solution.py:389
  45.4 0.6 collective-permute-done.8.refs_9_
  46.0 0.0 collective-permute-done.9.refs_10_.refs_4_
  46.0 3.6 %attend.1 = (f32[384,512]{1,0:T(8,128)S(1)}, bf16[384,512]{1,0:T(8,128)(2,1)S(1)}, f32[384,512]{1,0:T(8,128)S(1)}, bf16[384,512]{1,0:T(8,128)(2,1)S(1)}) custom-call(bf16[384,256]{1,0:T(8,128)(2,1)S(1)} %get-tuple-element.42.refs_0_, bf16[384,256]{1,0:T(8,128)(2,1)S(1)} %get-tuple-element.46.refs_1_, bf16[384,256]{1,0:T(8,128)(2,1)S(1)} %collective-permute-done.4.refs_2_, ...), custom_call_target="tpu_custom_call" | custom-call | tf_op jit(solution)/shard_map/attend/pallas_call | solution.py:201
  49.6 1.4 %collective-permute-start.10 = (bf16[384,512]{1,0:T(8,128)(2,1)S(1)}, bf16[384,512]{1,0:T(8,128)(2,1)S(1)}, u32[]{:S(2)}, u32[]{:S(2)}) collective-permute-start(bf16[384,512]{1,0:T(8,128)(2,1)S(1)} %get-tuple-element.50), channel_id=1, source_target_pairs={{0,4},{4,0},{8,12},{12,8},{1,5},{5,1},{9,13},{13,9},{2,6},{6,2},{1... | collective-permute-start | bytes 1179656 | tf_op jit(solution)/shard_map/ppermute | solution.py:398
  51.0 2.2 %collective-permute-start.11 = (bf16[384,512]{1,0:T(8,128)(2,1)S(1)}, bf16[384,512]{1,0:T(8,128)(2,1)S(1)}, u32[]{:S(2)}, u32[]{:S(2)}) collective-permute-start(bf16[384,512]{1,0:T(8,128)(2,1)S(1)} %get-tuple-element.52), channel_id=1, source_target_pairs={{0,12},{4,8},{8,4},{12,0},{1,13},{5,9},{9,5},{13,1},{2,14},{6,10},... | collective-permute-start | bytes 1179656 | tf_op jit(solution)/shard_map/ppermute | solution.py:399
  53.2 4.4 %collective-permute-done.13.refs_2_ = bf16[128,1536]{1,0:T(8,128)(2,1)S(1)} collective-permute-done((bf16[128,1536]{1,0:T(8,128)(2,1)S(1)}, bf16[128,1536]{1,0:T(8,128)(2,1)S(1)}, u32[]{:S(2)}, u32[]{:S(2)}) %collective-permute-start.13) | collective-permute-done | bytes 393248 | tf_op jit(solution)/shard_map/ppermute | solution.py:390
  57.6 2.8 %collective-permute-done.12.refs_1_ = bf16[128,1536]{1,0:T(8,128)(2,1)S(1)} collective-permute-done((bf16[128,1536]{1,0:T(8,128)(2,1)S(1)}, bf16[128,1536]{1,0:T(8,128)(2,1)S(1)}, u32[]{:S(2)}, u32[]{:S(2)}) %collective-permute-start.12) | collective-permute-done | bytes 393248 | tf_op jit(solution)/shard_map/ppermute | solution.py:389
  60.4 1.7 %gradient.1 = (bf16[768,128]{1,0:T(8,128)(2,1)S(1)}, bf16[768,128]{1,0:T(8,128)(2,1)S(1)}, bf16[768,128]{1,0:T(8,128)(2,1)S(1)}, bf16[768,128]{1,0:T(8,128)(2,1)...) custom-call(f32[384,512]{1,0:T(8,128)S(1)} %get-tuple-element.49.qo_own, ...), custom_call_target="tpu_custom_call" | custom-call | tf_op jit(solution)/shard_map/gradient/pallas_call | solution.py:243
  62.1 0.1 collective-permute-start.17
  62.2 0.4 collective-permute-start.15
  62.7 2.0 %collective-permute-done.17.got = bf16[6,48,1536]{2,1,0:T(8,128)(2,1)S(1)} collective-permute-done((bf16[6,48,1536]{2,1,0:T(8,128)(2,1)S(1)}, bf16[6,48,1536]{2,1,0:T(8,128)(2,1)S(1)}, u32[]{:S(2)}, u32[]{:S(2)}) %collective-permute-start.17) | collective-permute-done | bytes 884768 | tf_op jit(solution)/shard_map/ppermute | solution.py:408
  64.6 0.5 split_y.1
  65.2 3.4 %collective-permute-start.18 = (bf16[6,48,384]{2,1,0:T(8,128)(2,1)S(1)}, bf16[6,48,384]{2,1,0:T(8,128)(2,1)S(1)}, u32[]{:S(2)}, u32[]{:S(2)}) collective-permute-start(bf16[6,48,384]{2,1,0:T(8,128)(2,1)S(1)} %get-tuple-element.63), channel_id=1, source_target_pairs={{0,8},{4,12},{8,0},{12,4},{1,9},{5,13},{9,1},{13,5},{2,10},{6,14},... | collective-permute-start | bytes 663560 | tf_op jit(solution)/shard_map/ppermute | solution.py:381
  68.5 1.1 collective-permute-start.20
  69.6 1.2 %collective-permute-start.14 = (bf16[768,128]{1,0:T(8,128)(2,1)S(1)}, bf16[768,128]{1,0:T(8,128)(2,1)S(1)}, u32[]{:S(2)}, u32[]{:S(2)}) collective-permute-start(bf16[768,128]{1,0:T(8,128)(2,1)S(1)} %get-tuple-element.54), channel_id=1, source_target_pairs={{0,1},{1,0},{2,3},{3,2},{4,5},{5,4},{6,7},{7,6},{8,9},{9,8},{10,11... | collective-permute-start | bytes 589832 | tf_op jit(solution)/shard_map/ppermute | solution.py:405
  70.8 2.9 %collective-permute-done.15.refs_3_ = bf16[768,128]{1,0:T(8,128)(2,1)S(1)} collective-permute-done((bf16[768,128]{1,0:T(8,128)(2,1)S(1)}, bf16[768,128]{1,0:T(8,128)(2,1)S(1)}, u32[]{:S(2)}, u32[]{:S(2)}) %collective-permute-start.15) | collective-permute-done | bytes 196640 | tf_op jit(solution)/shard_map/ppermute | solution.py:403
  73.8 1.3 %collective-permute-done.18.refs_1_ = bf16[6,48,384]{2,1,0:T(8,128)(2,1)S(1)} collective-permute-done((bf16[6,48,384]{2,1,0:T(8,128)(2,1)S(1)}, bf16[6,48,384]{2,1,0:T(8,128)(2,1)S(1)}, u32[]{:S(2)}, u32[]{:S(2)}) %collective-permute-start.18) | collective-permute-done | bytes 221216 | tf_op jit(solution)/shard_map/ppermute | solution.py:381
  75.0 3.5 %collective-permute-done.19.refs_2_ = bf16[6,48,384]{2,1,0:T(8,128)(2,1)S(1)} collective-permute-done((bf16[6,48,384]{2,1,0:T(8,128)(2,1)S(1)}, bf16[6,48,384]{2,1,0:T(8,128)(2,1)S(1)}, u32[]{:S(2)}, u32[]{:S(2)}) %collective-permute-start.19) | collective-permute-done | bytes 221216 | tf_op jit(solution)/shard_map/ppermute | solution.py:381
  78.5 0.5 collective-permute-done.20.refs_3_
  79.0 0.3 split_z.1
  79.3 0.4 collective-permute-start.21
  79.7 3.2 %collective-permute-start.22 = (bf16[6,48,96]{2,1,0:T(8,128)(2,1)S(1)}, bf16[6,48,96]{2,1,0:T(8,128)(2,1)S(1)}, u32[]{:S(2)}, u32[]{:S(2)}) collective-permute-start(bf16[6,48,96]{2,1,0:T(8,128)(2,1)S(1)} %get-tuple-element.68), channel_id=1, source_target_pairs={{0,2},{1,3},{2,0},{3,1},{4,6},{5,7},{6,4},{7,5},{8,10},{9,11},{10,... | collective-permute-start | bytes 165896 | tf_op jit(solution)/shard_map/ppermute | solution.py:381
  82.9 0.0 collective-permute-start.23
  82.9 5.7 %collective-permute-done.21.refs_1_ = bf16[6,48,96]{2,1,0:T(8,128)(2,1)S(1)} collective-permute-done((bf16[6,48,96]{2,1,0:T(8,128)(2,1)S(1)}, bf16[6,48,96]{2,1,0:T(8,128)(2,1)S(1)}, u32[]{:S(2)}, u32[]{:S(2)}) %collective-permute-start.21) | collective-permute-done | bytes 55328 | tf_op jit(solution)/shard_map/ppermute | solution.py:381
  88.6 0.0 collective-permute-done.22.refs_2_
  88.6 0.0 collective-permute-done.23.refs_3_
  88.6 0.2 split_x.1
  88.8 3.3 %collective-permute-start.24 = (bf16[6,48,96]{2,1,0:T(8,128)(2,1)S(1)}, bf16[6,48,96]{2,1,0:T(8,128)(2,1)S(1)}, u32[]{:S(2)}, u32[]{:S(2)}) collective-permute-start(bf16[6,48,96]{2,1,0:T(8,128)(2,1)S(1)} %get-tuple-element.71), channel_id=1, source_target_pairs={{0,128},{64,192},{128,0},{192,64},{1,129},{65,193},{129,1},{193,65... | collective-permute-start | bytes 165896 | tf_op jit(solution)/shard_map/ppermute | solution.py:381
  92.1 0.6 collective-permute-start.25
  92.7 0.6 collective-permute-start.26
  93.3 3.1 %d_tokens.1 = (bf16[128,768]{1,0:T(8,128)(2,1)}, bf16[128,1536]{1,0:T(8,128)(2,1)}, f32[8,128]{1,0:T(8,128)S(1)}) custom-call(bf16[128,1536]{1,0:T(8,128)(2,1)S(1)} %bitcast.13, bf16[1536,2304]{1,0:T(8,128)(2,1)S(1)} %bitcast.6, bf16[768,128]{1,0:T(8,128)(2,1)S(1)} %get-tuple-element.53.refs_0_, bf16[768,128]{1,0:T(8,128)(2,1)S(1)} %collective-permute-done.14.refs_1_, ...), custom_call_target="tpu_custom_call" | custom-call | tf_op jit(solution)/shard_map/d_tokens/pallas_call | solution.py:281
  96.4 0.1 collective-permute-done.25.refs_2_
  96.5 1.8 %collective-permute-done.26.refs_3_ = bf16[6,48,96]{2,1,0:T(8,128)(2,1)S(1)} collective-permute-done((bf16[6,48,96]{2,1,0:T(8,128)(2,1)S(1)}, bf16[6,48,96]{2,1,0:T(8,128)(2,1)S(1)}, u32[]{:S(2)}, u32[]{:S(2)}) %collective-permute-start.26) | collective-permute-done | bytes 55328 | tf_op jit(solution)/shard_map/ppermute | solution.py:381
  98.3 0.1 split_zh.1
  98.3 5.7 %collective-permute-start.27 = (bf16[3,48,96]{2,1,0:T(8,128)(2,1)S(1)}, bf16[3,48,96]{2,1,0:T(8,128)(2,1)S(1)}, u32[]{:S(2)}, u32[]{:S(2)}) collective-permute-start(bf16[3,48,96]{2,1,0:T(8,128)(2,1)S(1)} %get-tuple-element.76), channel_id=1, source_target_pairs={{0,35},{1,34},{2,33},{3,32},{32,3},{33,2},{34,1},{35,0},{4,39},{5,... | collective-permute-start | bytes 82952 | tf_op jit(solution)/shard_map/ppermute | solution.py:432
  104.0 1.9 %collective-permute-done.27.got = bf16[3,48,96]{2,1,0:T(8,128)(2,1)S(1)} collective-permute-done((bf16[3,48,96]{2,1,0:T(8,128)(2,1)S(1)}, bf16[3,48,96]{2,1,0:T(8,128)(2,1)S(1)}, u32[]{:S(2)}, u32[]{:S(2)}) %collective-permute-start.27) | collective-permute-done | bytes 27680 | tf_op jit(solution)/shard_map/ppermute | solution.py:432
  106.0 0.6 finish.1
  (13 shorter events, 0.0 us)
Async XLA Ops:
  0.6 30.2 %copy-start = (bf16[1,128,1536]{2,1,0:T(8,128)(2,1)S(1)}, bf16[1,128,1536]{2,1,0:T(8,128)(2,1)}, u32[]{:S(2)}) copy-start(bf16[1,128,1536]{2,1,0:T(8,128)(2,1)} %param.3) | copy-start | bytes 1179652
  0.6 17.2 %collective-permute-start.1 = (bf16[128,1536]{1,0:T(8,128)(2,1)}, bf16[128,1536]{1,0:T(8,128)(2,1)S(1)}, u32[]{:S(2)}, u32[]{:S(2)}) collective-permute-start(bf16[128,1536]{1,0:T(8,128)(2,1)} %bitcast.7), channel_id=1, source_target_pairs={{1,2},{2,1},{5,6},{6,5},{9,10},{10,9},{13,14},{14,13},{17,18},{18,... | collective-permute-start | bytes 1179656 | tf_op jit(solution)/shard_map/ppermute | solution.py:383
  4.6 88.7 %slice-start = ((s8[7077888]{0:T(1024)(128)(4,1)}), s8[2883584]{0:T(1024)(128)(4,1)S(1)}, s32[]{:S(2)}) async-start(s8[7077888]{0:T(1024)(128)(4,1)} %bitcast.5), calls=%async_computation | async-start | bytes 5767168
  9.7 8.1 %collective-permute-start = (bf16[768,128]{1,0:T(8,128)(2,1)}, bf16[768,128]{1,0:T(8,128)(2,1)S(1)}, u32[]{:S(2)}, u32[]{:S(2)}) collective-permute-start(bf16[768,128]{1,0:T(8,128)(2,1)} %get-tuple-element.41), channel_id=1, source_target_pairs={{0,1},{1,0},{2,3},{3,2},{4,5},{5,4},{6,7},{7,6},{8,9},{9,8},{10,11... | collective-permute-start | bytes 589832 | tf_op jit(solution)/shard_map/ppermute | solution.py:381
  9.8 17.2 %collective-permute-start.2 = (bf16[768,128]{1,0:T(8,128)(2,1)}, bf16[768,128]{1,0:T(8,128)(2,1)S(1)}, u32[]{:S(2)}, u32[]{:S(2)}) collective-permute-start(bf16[768,128]{1,0:T(8,128)(2,1)} %get-tuple-element.43), channel_id=1, source_target_pairs={{0,2},{1,3},{2,0},{3,1},{4,6},{5,7},{6,4},{7,5},{8,10},{9,11},{10,... | collective-permute-start | bytes 589832 | tf_op jit(solution)/shard_map/ppermute | solution.py:381
  11.4 19.4 %collective-permute-start.3 = (bf16[768,128]{1,0:T(8,128)(2,1)}, bf16[768,128]{1,0:T(8,128)(2,1)S(1)}, u32[]{:S(2)}, u32[]{:S(2)}) collective-permute-start(bf16[768,128]{1,0:T(8,128)(2,1)} %get-tuple-element.44), channel_id=1, source_target_pairs={{0,3},{1,2},{2,1},{3,0},{4,7},{5,6},{6,5},{7,4},{8,11},{9,10},{10,... | collective-permute-start | bytes 589832 | tf_op jit(solution)/shard_map/ppermute | solution.py:381
  17.8 0.9 copy-start.1
  18.8 11.9 %collective-permute-start.4 = (bf16[384,256]{1,0:T(8,128)(2,1)S(1)}, bf16[384,256]{1,0:T(8,128)(2,1)S(1)}, u32[]{:S(2)}, u32[]{:S(2)}) collective-permute-start(bf16[384,256]{1,0:T(8,128)(2,1)S(1)} %get-tuple-element.42.refs_0_), channel_id=1, source_target_pairs={{0,12},{4,8},{8,4},{12,0},{1,13},{5,9},{9,5},{13,1},{2,14},{6,10},... | collective-permute-start | bytes 589832 | tf_op jit(solution)/shard_map/ppermute | solution.py:386
  21.9 8.8 %collective-permute-start.5 = (bf16[384,256]{1,0:T(8,128)(2,1)S(1)}, bf16[384,256]{1,0:T(8,128)(2,1)S(1)}, u32[]{:S(2)}, u32[]{:S(2)}) collective-permute-start(bf16[384,256]{1,0:T(8,128)(2,1)S(1)} %get-tuple-element.45.refs_4_), channel_id=1, source_target_pairs={{0,4},{4,0},{8,12},{12,8},{1,5},{5,1},{9,13},{13,9},{2,6},{6,2},{1... | collective-permute-start | bytes 589832 | tf_op jit(solution)/shard_map/ppermute | solution.py:386
  30.9 15.1 %collective-permute-start.9 = (bf16[128,1536]{1,0:T(8,128)(2,1)S(1)}, bf16[128,1536]{1,0:T(8,128)(2,1)S(1)}, u32[]{:S(2)}, u32[]{:S(2)}) collective-permute-start(bf16[128,1536]{1,0:T(8,128)(2,1)S(1)} %bitcast.9), channel_id=1, source_target_pairs={{0,3},{3,0},{4,7},{7,4},{8,11},{11,8},{12,15},{15,12},{16,19},{19,... | collective-permute-start | bytes 1179656 | tf_op jit(solution)/shard_map/ppermute | solution.py:391
  31.6 61.7 %slice-start.1 = ((s8[7077888]{0:T(1024)(128)(4,1)}), s8[4194304]{0:T(1024)(128)(4,1)S(1)}, s32[]{:S(2)}) async-start(s8[7077888]{0:T(1024)(128)(4,1)} %bitcast.5), calls=%async_computation.1 | async-start | bytes 8388608
  31.6 5.9 %collective-permute-start.7 = (bf16[384,256]{1,0:T(8,128)(2,1)S(1)}, bf16[384,256]{1,0:T(8,128)(2,1)S(1)}, u32[]{:S(2)}, u32[]{:S(2)}) collective-permute-start(bf16[384,256]{1,0:T(8,128)(2,1)S(1)} %get-tuple-element.47.refs_5_), channel_id=1, source_target_pairs={{0,4},{4,0},{8,12},{12,8},{1,5},{5,1},{9,13},{13,9},{2,6},{6,2},{1... | collective-permute-start | bytes 589832 | tf_op jit(solution)/shard_map/ppermute | solution.py:393
  33.2 6.9 %collective-permute-start.6 = (bf16[384,256]{1,0:T(8,128)(2,1)S(1)}, bf16[384,256]{1,0:T(8,128)(2,1)S(1)}, u32[]{:S(2)}, u32[]{:S(2)}) collective-permute-start(bf16[384,256]{1,0:T(8,128)(2,1)S(1)} %get-tuple-element.46.refs_1_), channel_id=1, source_target_pairs={{0,12},{4,8},{8,4},{12,0},{1,13},{5,9},{9,5},{13,1},{2,14},{6,10},... | collective-permute-start | bytes 589832 | tf_op jit(solution)/shard_map/ppermute | solution.py:392
  42.0 4.0 %collective-permute-start.8 = (f32[8,1024]{1,0:T(8,128)S(1)}, f32[8,1024]{1,0:T(8,128)S(1)}, u32[]{:S(2)}, u32[]{:S(2)}) collective-permute-start(f32[8,1024]{1,0:T(8,128)S(1)} %stats.1.refs_8_), channel_id=1, source_target_pairs={{0,4},{4,0},{8,12},{12,8},{1,5},{5,1},{9,13},{13,9},{2,6},{6,2},{1... | collective-permute-start | bytes 98312 | tf_op jit(solution)/shard_map/ppermute | solution.py:396
  42.1 15.5 %collective-permute-start.13 = (bf16[128,1536]{1,0:T(8,128)(2,1)S(1)}, bf16[128,1536]{1,0:T(8,128)(2,1)S(1)}, u32[]{:S(2)}, u32[]{:S(2)}) collective-permute-start(bf16[128,1536]{1,0:T(8,128)(2,1)S(1)} %bitcast.10), channel_id=1, source_target_pairs={{0,2},{1,3},{2,0},{3,1},{4,6},{5,7},{6,4},{7,5},{8,10},{9,11},{10,... | collective-permute-start | bytes 1179656 | tf_op jit(solution)/shard_map/ppermute | solution.py:390
  44.1 16.3 %collective-permute-start.12 = (bf16[128,1536]{1,0:T(8,128)(2,1)S(1)}, bf16[128,1536]{1,0:T(8,128)(2,1)S(1)}, u32[]{:S(2)}, u32[]{:S(2)}) collective-permute-start(bf16[128,1536]{1,0:T(8,128)(2,1)S(1)} %bitcast.11), channel_id=1, source_target_pairs={{0,1},{1,0},{2,3},{3,2},{4,5},{5,4},{6,7},{7,6},{8,9},{9,8},{10,11... | collective-permute-start | bytes 1179656 | tf_op jit(solution)/shard_map/ppermute | solution.py:389
  49.6 10.7 %collective-permute-start.10 = (bf16[384,512]{1,0:T(8,128)(2,1)S(1)}, bf16[384,512]{1,0:T(8,128)(2,1)S(1)}, u32[]{:S(2)}, u32[]{:S(2)}) collective-permute-start(bf16[384,512]{1,0:T(8,128)(2,1)S(1)} %get-tuple-element.50), channel_id=1, source_target_pairs={{0,4},{4,0},{8,12},{12,8},{1,5},{5,1},{9,13},{13,9},{2,6},{6,2},{1... | collective-permute-start | bytes 1179656 | tf_op jit(solution)/shard_map/ppermute | solution.py:398
  51.0 9.3 %collective-permute-start.11 = (bf16[384,512]{1,0:T(8,128)(2,1)S(1)}, bf16[384,512]{1,0:T(8,128)(2,1)S(1)}, u32[]{:S(2)}, u32[]{:S(2)}) collective-permute-start(bf16[384,512]{1,0:T(8,128)(2,1)S(1)} %get-tuple-element.52), channel_id=1, source_target_pairs={{0,12},{4,8},{8,4},{12,0},{1,13},{5,9},{9,5},{13,1},{2,14},{6,10},... | collective-permute-start | bytes 1179656 | tf_op jit(solution)/shard_map/ppermute | solution.py:399
  62.1 2.5 %collective-permute-start.17 = (bf16[6,48,1536]{2,1,0:T(8,128)(2,1)S(1)}, bf16[6,48,1536]{2,1,0:T(8,128)(2,1)S(1)}, u32[]{:S(2)}, u32[]{:S(2)}) collective-permute-start(bf16[6,48,1536]{2,1,0:T(8,128)(2,1)S(1)} %get-tuple-element.61), channel_id=1, source_target_pairs={{0,16},{16,0},{1,17},{17,1},{2,18},{18,2},{3,19},{19,3},{4,20},{20... | collective-permute-start | bytes 2654216 | tf_op jit(solution)/shard_map/ppermute | solution.py:408
  62.2 11.5 %collective-permute-start.15 = (bf16[768,128]{1,0:T(8,128)(2,1)S(1)}, bf16[768,128]{1,0:T(8,128)(2,1)S(1)}, u32[]{:S(2)}, u32[]{:S(2)}) collective-permute-start(bf16[768,128]{1,0:T(8,128)(2,1)S(1)} %get-tuple-element.56), channel_id=1, source_target_pairs={{0,3},{1,2},{2,1},{3,0},{4,7},{5,6},{6,5},{7,4},{8,11},{9,10},{10,... | collective-permute-start | bytes 589832 | tf_op jit(solution)/shard_map/ppermute | solution.py:403
  65.2 9.9 %collective-permute-start.18 = (bf16[6,48,384]{2,1,0:T(8,128)(2,1)S(1)}, bf16[6,48,384]{2,1,0:T(8,128)(2,1)S(1)}, u32[]{:S(2)}, u32[]{:S(2)}) collective-permute-start(bf16[6,48,384]{2,1,0:T(8,128)(2,1)S(1)} %get-tuple-element.63), channel_id=1, source_target_pairs={{0,8},{4,12},{8,0},{12,4},{1,9},{5,13},{9,1},{13,5},{2,10},{6,14},... | collective-permute-start | bytes 663560 | tf_op jit(solution)/shard_map/ppermute | solution.py:381
  68.5 10.0 %collective-permute-start.19 = (bf16[6,48,384]{2,1,0:T(8,128)(2,1)S(1)}, bf16[6,48,384]{2,1,0:T(8,128)(2,1)S(1)}, u32[]{:S(2)}, u32[]{:S(2)}) collective-permute-start(bf16[6,48,384]{2,1,0:T(8,128)(2,1)S(1)} %get-tuple-element.64), channel_id=1, source_target_pairs={{0,4},{4,0},{8,12},{12,8},{1,5},{5,1},{9,13},{13,9},{2,6},{6,2},{1... | collective-permute-start | bytes 663560 | tf_op jit(solution)/shard_map/ppermute | solution.py:381
  68.5 10.5 %collective-permute-start.20 = (bf16[6,48,384]{2,1,0:T(8,128)(2,1)S(1)}, bf16[6,48,384]{2,1,0:T(8,128)(2,1)S(1)}, u32[]{:S(2)}, u32[]{:S(2)}) collective-permute-start(bf16[6,48,384]{2,1,0:T(8,128)(2,1)S(1)} %get-tuple-element.65), channel_id=1, source_target_pairs={{0,12},{4,8},{8,4},{12,0},{1,13},{5,9},{9,5},{13,1},{2,14},{6,10},... | collective-permute-start | bytes 663560 | tf_op jit(solution)/shard_map/ppermute | solution.py:381
  69.6 23.7 %collective-permute-start.14 = (bf16[768,128]{1,0:T(8,128)(2,1)S(1)}, bf16[768,128]{1,0:T(8,128)(2,1)S(1)}, u32[]{:S(2)}, u32[]{:S(2)}) collective-permute-start(bf16[768,128]{1,0:T(8,128)(2,1)S(1)} %get-tuple-element.54), channel_id=1, source_target_pairs={{0,1},{1,0},{2,3},{3,2},{4,5},{5,4},{6,7},{7,6},{8,9},{9,8},{10,11... | collective-permute-start | bytes 589832 | tf_op jit(solution)/shard_map/ppermute | solution.py:405
  73.8 19.5 %collective-permute-start.16 = (bf16[768,128]{1,0:T(8,128)(2,1)S(1)}, bf16[768,128]{1,0:T(8,128)(2,1)S(1)}, u32[]{:S(2)}, u32[]{:S(2)}) collective-permute-start(bf16[768,128]{1,0:T(8,128)(2,1)S(1)} %get-tuple-element.57), channel_id=1, source_target_pairs={{0,2},{1,3},{2,0},{3,1},{4,6},{5,7},{6,4},{7,5},{8,10},{9,11},{10,... | collective-permute-start | bytes 589832 | tf_op jit(solution)/shard_map/ppermute | solution.py:405
  79.3 9.3 %collective-permute-start.21 = (bf16[6,48,96]{2,1,0:T(8,128)(2,1)S(1)}, bf16[6,48,96]{2,1,0:T(8,128)(2,1)S(1)}, u32[]{:S(2)}, u32[]{:S(2)}) collective-permute-start(bf16[6,48,96]{2,1,0:T(8,128)(2,1)S(1)} %get-tuple-element.67), channel_id=1, source_target_pairs={{0,3},{1,2},{2,1},{3,0},{4,7},{5,6},{6,5},{7,4},{8,11},{9,10},{10,... | collective-permute-start | bytes 165896 | tf_op jit(solution)/shard_map/ppermute | solution.py:381
  79.7 8.9 %collective-permute-start.22 = (bf16[6,48,96]{2,1,0:T(8,128)(2,1)S(1)}, bf16[6,48,96]{2,1,0:T(8,128)(2,1)S(1)}, u32[]{:S(2)}, u32[]{:S(2)}) collective-permute-start(bf16[6,48,96]{2,1,0:T(8,128)(2,1)S(1)} %get-tuple-element.68), channel_id=1, source_target_pairs={{0,2},{1,3},{2,0},{3,1},{4,6},{5,7},{6,4},{7,5},{8,10},{9,11},{10,... | collective-permute-start | bytes 165896 | tf_op jit(solution)/shard_map/ppermute | solution.py:381
  82.9 5.7 %collective-permute-start.23 = (bf16[6,48,96]{2,1,0:T(8,128)(2,1)S(1)}, bf16[6,48,96]{2,1,0:T(8,128)(2,1)S(1)}, u32[]{:S(2)}, u32[]{:S(2)}) collective-permute-start(bf16[6,48,96]{2,1,0:T(8,128)(2,1)S(1)} %get-tuple-element.69), channel_id=1, source_target_pairs={{0,1},{1,0},{2,3},{3,2},{4,5},{5,4},{6,7},{7,6},{8,9},{9,8},{10,11... | collective-permute-start | bytes 165896 | tf_op jit(solution)/shard_map/ppermute | solution.py:381
  88.8 7.6 %collective-permute-start.24 = (bf16[6,48,96]{2,1,0:T(8,128)(2,1)S(1)}, bf16[6,48,96]{2,1,0:T(8,128)(2,1)S(1)}, u32[]{:S(2)}, u32[]{:S(2)}) collective-permute-start(bf16[6,48,96]{2,1,0:T(8,128)(2,1)S(1)} %get-tuple-element.71), channel_id=1, source_target_pairs={{0,128},{64,192},{128,0},{192,64},{1,129},{65,193},{129,1},{193,65... | collective-permute-start | bytes 165896 | tf_op jit(solution)/shard_map/ppermute | solution.py:381
  92.1 4.4 %collective-permute-start.25 = (bf16[6,48,96]{2,1,0:T(8,128)(2,1)S(1)}, bf16[6,48,96]{2,1,0:T(8,128)(2,1)S(1)}, u32[]{:S(2)}, u32[]{:S(2)}) collective-permute-start(bf16[6,48,96]{2,1,0:T(8,128)(2,1)S(1)} %get-tuple-element.72), channel_id=1, source_target_pairs={{0,64},{64,0},{128,192},{192,128},{1,65},{65,1},{129,193},{193,129... | collective-permute-start | bytes 165896 | tf_op jit(solution)/shard_map/ppermute | solution.py:381
  92.7 5.6 %collective-permute-start.26 = (bf16[6,48,96]{2,1,0:T(8,128)(2,1)S(1)}, bf16[6,48,96]{2,1,0:T(8,128)(2,1)S(1)}, u32[]{:S(2)}, u32[]{:S(2)}) collective-permute-start(bf16[6,48,96]{2,1,0:T(8,128)(2,1)S(1)} %get-tuple-element.73), channel_id=1, source_target_pairs={{0,192},{64,128},{128,64},{192,0},{1,193},{65,129},{129,65},{193,1... | collective-permute-start | bytes 165896 | tf_op jit(solution)/shard_map/ppermute | solution.py:381
  98.3 7.6 %collective-permute-start.27 = (bf16[3,48,96]{2,1,0:T(8,128)(2,1)S(1)}, bf16[3,48,96]{2,1,0:T(8,128)(2,1)S(1)}, u32[]{:S(2)}, u32[]{:S(2)}) collective-permute-start(bf16[3,48,96]{2,1,0:T(8,128)(2,1)S(1)} %get-tuple-element.76), channel_id=1, source_target_pairs={{0,35},{1,34},{2,33},{3,32},{32,3},{33,2},{34,1},{35,0},{4,39},{5,... | collective-permute-start | bytes 82952 | tf_op jit(solution)/shard_map/ppermute | solution.py:432
